TPU v7x, 256 devices: a whole 4x4x8 slice. The times are simulated.
256 devices in a mesh: ctx: 64 (over z, x, core), dp: 4 (over y).
Axes of the slice: x: 4, y: 4, z: 8, core: 2. Of those that a mesh axis runs over, the one named last changes fastest.
Arguments:
- layer_input: bfloat16 [4, 16384, 4096], P('dp', 'ctx'), may hold values from -6 to 6
- queries: bfloat16 [4, 16384, 512], P('dp', 'ctx'), may hold values from -6 to 6
- keys: bfloat16 [4, 16384, 512], P('dp', 'ctx'), may hold values from -6 to 6
- values: bfloat16 [4, 16384, 1024], P('dp', 'ctx'), may hold values from -6 to 6
- grad_out: bfloat16 [4, 16384, 1024], P('dp', 'ctx'), may hold values from -6 to 6
- doc_pos: int32 [4, 16384], P('dp', 'ctx'), may hold values from 0 to 8319, as said below
- w_input: bfloat16 [4096, 4], replicated, may hold values from -0.09375 to 0.09375
- b_input: float32 [4], replicated, may hold values from -8 to -1
- w_forget: bfloat16 [4096, 4], replicated, may hold values from -0.046875 to 0.046875
- b_forget: float32 [4], replicated, may hold values from 3 to 16
Outputs:
- grad_queries: bfloat16 [4, 16384, 512], P('dp', 'ctx')
- grad_keys: bfloat16 [4, 16384, 512], P('dp', 'ctx')
- grad_values: bfloat16 [4, 16384, 1024], P('dp', 'ctx')
- grad_w_input: float32 [4096, 4], replicated
- grad_w_forget: float32 [4096, 4], replicated
Inputs may be any that keep to these rules, and one draw needn't show every extreme that they name: doc_pos[b, 0] = 0 and doc_pos[b, t] is either 0 (a new document starts at t) or doc_pos[b, t-1] + 1; each sequence holds 4 documents, and a document always starts at token 8320.
All inputs are finite; a program needn't handle non-finite values.
Results may differ from a plain program's by a relative error of at most 0.004.
Values sent between devices are 32-bit elements; how exact they have to be, the bound alone decides.
No kernel may reach another device: no remote copies, remote signals or barrier semaphores. Data moves between devices by JAX's collectives and lax.ppermute only.
A program may use at most 128 MiB of HBM per device.

v0:
```python
import jax
import jax.numpy as jnp
from jax import lax
from jax.sharding import PartitionSpec as P

very_negative = -1e30


def prefix(part, axis, combine, identity, reverse):
    count = lax.axis_size(axis)
    place = lax.axis_index(axis)
    ahead = count - 1 - place if reverse else place
    gathered = jax.tree.map(lambda a: lax.all_gather(a, axis), part)
    state = jax.tree.map(lambda a, e: jnp.zeros_like(a) + jnp.asarray(e, a.dtype), part, identity)

    def one(hop, state):
        source = count - 1 - hop if reverse else hop
        return combine(
            state, jax.tree.map(lambda a: lax.dynamic_index_in_dim(a, source, 0, False), gathered)
        )

    return lax.fori_loop(0, ahead, one, state)


def inner_product(form, *operands):
    return jnp.einsum(form, *operands, precision=lax.Precision.HIGHEST)


def combine_states(former, latter):
    reset_former, total_former, max_former, matrix_former, vector_former = former
    reset_latter, total_latter, max_latter, matrix_latter, vector_latter = latter
    cut = reset_latter > 0.5
    shifted = max_former + total_latter
    new_max = jnp.where(cut, max_latter, jnp.maximum(shifted, max_latter))
    keep_former = jnp.where(cut, 0.0, jnp.exp(shifted - new_max))
    keep_latter = jnp.exp(max_latter - new_max)
    matrix_new = (
        keep_former[:, None, None] * matrix_former + keep_latter[:, None, None] * matrix_latter
    )
    vector_new = keep_former[:, None] * vector_former + keep_latter[:, None] * vector_latter
    return (
        jnp.maximum(reset_former, reset_latter),
        total_former + total_latter,
        new_max,
        matrix_new,
        vector_new,
    )


def add_sums(former, latter):
    return former + latter


def local(
    layer_input, queries, keys, values, grad_out, doc_pos, w_input, b_input, w_forget, b_forget
):
    head_count = w_input.shape[1]
    block_rows = queries.shape[1]
    key_width = queries.shape[2] // head_count
    value_width = values.shape[2] // head_count
    score_scale = key_width ** (-0.5)
    layer_rows = layer_input[0]
    in_gate = jnp.dot(layer_rows, w_input, preferred_element_type=jnp.float32) + b_input
    forget_pre = jnp.dot(layer_rows, w_forget, preferred_element_type=jnp.float32) + b_forget
    log_cum = jnp.cumsum(jax.nn.log_sigmoid(forget_pre), axis=0)
    block_total = log_cum[-1]
    doc_count = jnp.cumsum((doc_pos[0] == 0).astype(jnp.int32))
    reset_flag = (doc_count[-1:] > 0).astype(jnp.float32)
    query_low = queries[0].reshape(block_rows, head_count, key_width)
    key_low = keys[0].reshape(block_rows, head_count, key_width)
    value_low = values[0].reshape(block_rows, head_count, value_width)
    grad_low = grad_out[0].reshape(block_rows, head_count, value_width)
    scaled_query = query_low.astype(jnp.float32) * score_scale
    key_row_slab = key_low.astype(jnp.float32)
    value_row_slab = value_low.astype(jnp.float32)
    grad_rows = grad_low.astype(jnp.float32)
    zero_flag = jnp.zeros((1,), jnp.float32)
    zero_total = jnp.zeros((head_count,), jnp.float32)
    lowest_max = jnp.full((head_count,), very_negative, jnp.float32)
    zero_matrix = jnp.zeros((head_count, key_width, value_width), jnp.float32)
    zero_vector = jnp.zeros((head_count, key_width), jnp.float32)
    identity = (zero_flag, zero_total, lowest_max, zero_matrix, zero_vector)
    key_valid = doc_count == doc_count[-1]
    key_log = jnp.where(key_valid[:, None], block_total[None] - log_cum + in_gate, very_negative)
    state_max = jnp.max(key_log, axis=0)
    key_matrix_weight = jnp.exp(key_log - state_max[None])
    own_memory_matrix = inner_product(
        "nx,nxq,nxd->xqd", key_matrix_weight, key_row_slab, value_row_slab
    )
    vector_own = inner_product("sh,shk->hk", key_matrix_weight, key_row_slab)
    forward_parts = (reset_flag, block_total, state_max, own_memory_matrix, vector_own)
    earlier = prefix(forward_parts, "ctx", combine_states, identity, False)
    in_max, incoming_matrix, incoming_vector = (earlier[2], earlier[3], earlier[4])
    positions = jnp.arange(block_rows)
    pair_mask = (positions[:, None] >= positions[None, :]) & (
        doc_count[:, None] == doc_count[None, :]
    )
    pair_log = jnp.where(
        pair_mask[None],
        log_cum.T[:, :, None] - log_cum.T[:, None, :] + in_gate.T[:, None, :],
        very_negative,
    )
    query_valid = doc_count == 0
    cross_log = jnp.where(query_valid[:, None], log_cum + in_max[None], very_negative)
    row_max = jnp.maximum(jnp.max(pair_log, axis=2).T, cross_log)
    weights = jnp.exp(pair_log - row_max.T[:, :, None])
    scores = (
        jnp.einsum("thk,shk->hts", query_low, key_low, preferred_element_type=jnp.float32)
        * score_scale
    )
    coupled_scores = scores * weights
    crossing_scale = jnp.exp(cross_log - row_max)
    sums = jnp.sum(coupled_scores, axis=2).T + crossing_scale * inner_product(
        "thk,hk->th", scaled_query, incoming_vector
    )
    numerator = inner_product("cxu,ucp->xcp", coupled_scores, value_row_slab) + crossing_scale[
        :, :, None
    ] * inner_product("scj,cju->scu", scaled_query, incoming_matrix)
    floor_value = jnp.exp(-row_max)
    denom = jnp.maximum(jnp.abs(sums), floor_value)
    layer_out = numerator / denom[:, :, None]
    numerator_gradient = grad_rows / denom[:, :, None]
    grad_denom = -jnp.sum(grad_rows * layer_out, axis=2) / denom
    gradient_totals = (
        grad_denom * jnp.sign(sums) * (jnp.abs(sums) > floor_value).astype(jnp.float32)
    )
    grad_coupled = (
        jnp.einsum("thv,shv->hts", grad_low, value_low, preferred_element_type=jnp.float32)
        / denom.T[:, :, None]
        + gradient_totals.T[:, :, None]
    )
    grad_scores = grad_coupled * weights
    grad_query = inner_product("hts,shk->thk", grad_scores, key_row_slab) + crossing_scale[
        :, :, None
    ] * (
        inner_product("jwb,ajb->ajw", incoming_matrix, numerator_gradient)
        + gradient_totals[:, :, None] * incoming_vector[None]
    )
    grad_key = inner_product("hts,thk->shk", grad_scores, scaled_query)
    grad_value = inner_product("hts,thv->shv", coupled_scores, numerator_gradient)
    dual_log = jnp.where(query_valid[:, None], log_cum - row_max, very_negative)
    dual_max = jnp.max(dual_log, axis=0)
    query_matrix_weight = jnp.exp(dual_log - dual_max[None]) * query_valid[:, None].astype(
        jnp.float32
    )
    adjoint_matrix = inner_product(
        "qf,qfu,qfx->fux", query_matrix_weight, scaled_query, numerator_gradient
    )
    dual_vector = inner_product("th,thk->hk", query_matrix_weight * gradient_totals, scaled_query)
    dual_parts = (reset_flag, block_total, dual_max, adjoint_matrix, dual_vector)
    later = prefix(dual_parts, "ctx", combine_states, identity, True)
    later_max, following_matrix, following_vector = (later[2], later[3], later[4])
    key_scale = jnp.exp(key_log + later_max[None])
    grad_key = grad_key + key_scale[:, :, None] * (
        inner_product("qig,wqg->wqi", following_matrix, value_row_slab) + following_vector[None]
    )
    grad_value = grad_value + key_scale[:, :, None] * inner_product(
        "npd,znp->znd", following_matrix, key_row_slab
    )
    row_part = jnp.sum(scaled_query * grad_query, axis=2)
    column_part = jnp.sum(key_row_slab * grad_key, axis=2)
    layer_wide = layer_rows.astype(jnp.float32)
    local_suffix = jnp.cumsum((row_part - column_part)[::-1], axis=0)[::-1]
    block_sum = local_suffix[0]
    after = prefix(block_sum, "ctx", add_sums, jnp.zeros_like(block_sum), True)
    grad_forget_pre = (local_suffix + after[None]) * jax.nn.sigmoid(-forget_pre)
    grad_forget_local = inner_product("sd,sh->dh", layer_wide, grad_forget_pre)
    grad_w_input, grad_w_forget = lax.psum(
        (inner_product("sd,sh->dh", layer_wide, column_part), grad_forget_local), ("ctx", "dp")
    )
    grad_queries = (
        (grad_query * score_scale)
        .reshape(1, block_rows, head_count * key_width)
        .astype(jnp.bfloat16)
    )
    grad_keys = grad_key.reshape(1, block_rows, head_count * key_width).astype(jnp.bfloat16)
    grad_values = grad_value.reshape(1, block_rows, head_count * value_width).astype(jnp.bfloat16)
    return (grad_queries, grad_keys, grad_values, grad_w_input, grad_w_forget)


def solution(mesh):
    placed = (
        P("dp", "ctx", None),
        P("dp", "ctx", None),
        P("dp", "ctx", None),
        P("dp", "ctx", None),
        P("dp", "ctx", None),
        P("dp", "ctx"),
        P(),
        P(),
        P(),
        P(),
    )
    return jax.shard_map(
        local,
        mesh=mesh,
        in_specs=placed,
        out_specs=(P("dp", "ctx", None), P("dp", "ctx", None), P("dp", "ctx", None), P(), P()),
        check_vma=False,
    )
```

profile of v0, /device:TPU:1, one launch (start us, length us, event | category | flops | bytes accessed | tf_op | source)
XLA Modules:
  0.0 1328.4 jit_solution(1033627645053359588)
XLA Ops:
  10.6 1.4 fusion.58
  18.9 130.0 %all-reduce.4 = (f32[64]{0:T(128)S(1)}, f32[256]{0:T(256)S(1)}) all-reduce(f32[64]{0:T(128)S(1)} %fusion.77, f32[256]{0:T(256)S(1)} %dynamic-update-slice.1), channel_id=2, replica_groups=mesh['ctx'=64,'dp'=4] {'ctx'}, use_global_device_ids=true, to_apply=%add | all-reduce | flops 320 | bytes 2560
  149.7 1.8 copy.66
  152.5 40.3 %all-gather.7 = f32[64,1,4]{2,1,0:T(1,128)S(1)} all-gather(f32[1,1,4]{2,1,0:T(1,128)S(1)} %bitcast.364), channel_id=1, replica_groups=mesh['ctx'=64,'dp'=4] {'ctx'}, dimensions={0}, use_global_device_ids=true | all-gather | bytes 1040 | tf_op jit(solution)/shard_map/all_gather | solution.py:13
  193.2 53.8 %all-gather.8 = f32[64,4,128]{2,1,0:T(4,128)} all-gather(f32[1,4,128]{2,1,0:T(4,128)S(1)} %bitcast.362), channel_id=5, replica_groups=mesh['ctx'=64,'dp'=4] {'ctx'}, dimensions={0}, use_global_device_ids=true | all-gather | bytes 133120 | tf_op jit(solution)/shard_map/all_gather | solution.py:13
  247.5 4.7 while.48
  254.2 1.7 fusion.89
  258.2 2.1 fusion.46
  260.6 414.6 %all-reduce.2 = f32[256]{0:T(256)S(1)} all-reduce(f32[256]{0:T(256)S(1)} %dynamic-update-slice.2), channel_id=6, replica_groups=mesh['ctx'=64,'dp'=4] {'ctx'}, use_global_device_ids=true, to_apply=%add.2 | all-reduce | flops 256 | bytes 2048
  676.1 2.0 fusion.31
  679.9 1.4 fusion.45
  682.6 52.0 %all-gather.9 = f32[64,4,128]{2,1,0:T(4,128)S(1)} all-gather(f32[1,4,128]{2,1,0:T(4,128)S(1)} %bitcast.363), channel_id=8, replica_groups=mesh['ctx'=64,'dp'=4] {'ctx'}, dimensions={0}, use_global_device_ids=true | all-gather | bytes 133120 | tf_op jit(solution)/shard_map/all_gather | solution.py:13
  734.6 2.8 convolution_bitcast_fusion.6
  737.4 2.2 convolution_bitcast_fusion.3
  739.7 290.9 %while.49 = (s32[]{:T(128)}, f32[4]{0:T(128)S(1)}, f32[4,128,256]{2,1,0:T(8,128)S(1)}, f32[4,128]{1,0:T(4,128)S(1)}, s32[]{:T(128)}, /*index=5*/f32[64,1]{0,1:T(...) while((s32[]{:T(128)}, f32[4]{0:T(128)S(1)}, ...), condition=%wide.region_12.13_spmd, body=%wide.region_11.12_spmd.sunk | while | flops 394783 | bytes 1579413 | solution.py:22
  853.4 1.4 broadcast_select_fusion.9
  858.1 1.4 broadcast_select_fusion.9
  862.8 1.4 broadcast_select_fusion.9
  872.2 1.4 broadcast_select_fusion.9
  876.9 1.4 broadcast_select_fusion.9
  881.6 1.4 broadcast_select_fusion.9
  886.3 1.4 broadcast_select_fusion.9
  1030.7 2.5 fusion.44
  1035.4 1.6 convolution_bitcast_fusion.1
  1036.9 40.0 %all-gather.10 = f32[64,1,4]{2,1,0:T(1,128)S(1)} all-gather(f32[1,1,4]{2,1,0:T(1,128)S(1)} %bitcast.368), channel_id=1, replica_groups=mesh['ctx'=64,'dp'=4] {'ctx'}, dimensions={0}, use_global_device_ids=true | all-gather | bytes 1040 | tf_op jit(solution)/shard_map/all_gather | solution.py:13
  1076.9 2.4 while.50
  1079.3 1.6 convolution_bitcast_fusion
  1080.9 1.9 fusion.25
  1083.8 1.8 copy.85
  1085.6 233.4 %all-reduce.7.cloned.1.call-done = (f32[4096,4]{0,1:T(4,128)}, f32[4096,4]{0,1:T(4,128)}) async-done(((f32[4096,4]{0,1:T(4,128)}, f32[4096,4]{0,1:T(4,128)}), (f32[4096,4]{0,1:T(4,128)}, f32[4096,4]{0,1:T(4,128)})) %all-reduce.7.cloned.1.call-update) | async-done | bytes 131088 | tf_op jit(solution)/shard_map/psum | solution.py:168
  1318.9 1.5 copy.210
  1320.4 1.5 copy.211
  (497 shorter events, 309.5 us)
Async XLA Ops:
  7.2 3.4 copy-start
  7.2 6.6 copy-start.11
  7.2 6.8 copy-start.6
  7.2 7.2 copy-start.22
  7.2 7.2 copy-start.13
  7.2 240.2 %all-gather.14.cloned.1.call-start = ((), (), s32[]{:S(2)}) async-start(), calls=%async_computation | async-start | bytes 34078720 | tf_op jit(solution)/shard_map/all_gather | solution.py:13
  14.4 2.2 copy-start.23
  14.4 137.1 %copy-start.7 = (bf16[1,256,1024]{2,1,0:T(8,128)(2,1)S(1)}, bf16[1,256,1024]{2,1,0:T(8,128)(2,1)}, u32[]{:S(2)}) copy-start(bf16[1,256,1024]{2,1,0:T(8,128)(2,1)} %param.20) | copy-start | bytes 1572868
  16.5 723.1 %all-gather.16.cloned.1.call-start = ((), (), s32[]{:S(2)}) async-start(), calls=%async_computation.1 | async-start | bytes 34078720 | tf_op jit(solution)/shard_map/all_gather | solution.py:13
  247.5 6.6 copy-start.15
  252.2 0.5 copy-start.24
  252.3 4.4 copy-start.12
  254.2 2.5 copy-start.17
  254.2 2.7 copy-start.1
  254.2 2.7 copy-start.8
  255.9 2.2 copy-start.4
  256.9 419.2 %copy-start.20 = (f32[256,4]{0,1:T(4,128)}, f32[256,4]{0,1:T(4,128)S(1)}, u32[]{:S(2)}) copy-start(f32[256,4]{0,1:T(4,128)S(1)} %get-tuple-element.400) | copy-start | bytes 12292
  256.9 1.2 copy-start.16
  256.9 1.2 copy-start.19
  260.3 1058.6 %all-reduce.7.cloned.1.call-start = ((), (), s32[]{:S(2)}) async-start(), calls=%async_computation.2 | async-start | bytes 262144 | tf_op jit(solution)/shard_map/psum | solution.py:168
  676.0 2.0 copy-start.9
  676.0 2.0 copy-start.18
  678.1 1.8 copy-start.2
  678.8 1.0 copy-start.3
  679.9 57.6 %copy-start.21 = (f32[256,4]{0,1:T(4,128)S(1)}, f32[256,4]{0,1:T(4,128)}, u32[]{:S(2)}) copy-start(f32[256,4]{0,1:T(4,128)} %copy-done.20) | copy-start | bytes 12292
  682.1 55.4 %copy-start.5 = (f32[4,256,256]{2,1,0:T(8,128)S(1)}, f32[4,256,256]{2,1,0:T(8,128)}, u32[]{:S(2)}) copy-start(f32[4,256,256]{2,1,0:T(8,128)} %copy-done.4) | copy-start | bytes 3145732
  682.1 55.4 %copy-start.10 = (bf16[1,256,1024]{1,2,0:T(8,128)(2,1)S(1)}, bf16[1,256,1024]{1,2,0:T(8,128)(2,1)}, u32[]{:S(2)}) copy-start(bf16[1,256,1024]{1,2,0:T(8,128)(2,1)} %copy.63) | copy-start | bytes 1572868
  1030.6 2.5 copy-start.14
Sparse Core Ops, SparseCore 0:
  16.6 147.4 all-gather.13
  260.4 430.0 all-gather.15
  1081.0 237.8 all-reduce.6
where the time goes:
time: 1340 us; the launch traced here: 1330 us
  blocking collectives  731 us (55%)
  other arithmetic  302 us (23%)
  waiting for transfers between devices  233 us (17%)
  matrix products  27.9 us (2%)
  local copies, waits for them, and re-layouts  16.3 us (1%)
  between operations  14.9 us (1%)
    unnamed x2, blocking collectives  545 us
    psum x1, waiting for transfers between devices, local(): lax.psum((inner_product('sd,sh->dh', layer_wide, column_part), grad_forge...  233 us
    all_gather x4, blocking collectives, prefix(): gathered = jax.tree.map(lambda a: lax.all_gather(a, axis), part)  186 us
    select_n x63, other arithmetic, combine_states(): keep_former = jnp.where(cut, 0.0, jnp.exp(shifted - new_max))  85.6 us
    add x63, other arithmetic, combine_states(): keep_former[:, None, None] * matrix_former  82.5 us
    gt x63, other arithmetic, combine_states(): cut = reset_latter > 0.5  76.3 us
    exp x63, other arithmetic, combine_states(): keep_latter = jnp.exp(max_latter - new_max)  44 us
  transfers between devices with their start and end apart: 3, of which 1 were waited for; matrix products, arithmetic and copies ran while one was open for 2% of the time, Pallas kernels for 0%

commit v1 on v0

v1 whole, which is shorter than its diff:
```python
import functools

import jax
import jax.numpy as jnp
from jax import lax
from jax.experimental import pallas as pl
from jax.experimental.pallas import tpu as pltpu
from jax.sharding import PartitionSpec as P

NEG = -1e30
BIG = 1e30
F32 = jnp.float32
BF16 = jnp.bfloat16
VMEM = pl.BlockSpec(memory_space=pltpu.VMEM)
SMEM = pl.BlockSpec(memory_space=pltpu.SMEM)


def dot(a, b, ca, cb):
    return lax.dot_general(a, b, (((ca,), (cb,)), ((), ())), preferred_element_type=F32)


def split(x):
    high = x.astype(BF16)
    return high, (x - high.astype(F32)).astype(BF16)


def dot_left(x, b, ca, cb):
    high, low = split(x)
    return dot(high, b, ca, cb) + dot(low, b, ca, cb)


def dot_right(a, x, ca, cb):
    high, low = split(x)
    return dot(a, high, ca, cb) + dot(a, low, ca, cb)


def dot_exact(a, b):
    return lax.dot_general(
        a, b, (((1,), (0,)), ((), ())), precision=lax.Precision.HIGHEST, preferred_element_type=F32
    )


def iota(shape, dim):
    return lax.broadcasted_iota(jnp.int32, shape, dim)


def column_of(rows):
    r, n = rows.shape
    padded = jnp.concatenate([rows, jnp.zeros((128 - r, n), F32)], axis=0)
    return padded.T


def put(acc, col, h):
    return jnp.where(iota(acc.shape, 1) == h, col, acc)


def gates_kernel(
    heads, x_ref, wi_ref, wf_ref, bi_ref, bf_ref, pos_ref, k_ref, v_ref,
    pay_ref, mem_ref, rows_ref, lc_ref, dc_ref, kl_ref,
):
    n = x_ref.shape[0]
    dk = k_ref.shape[1] // heads
    dv = v_ref.shape[1] // heads
    w8 = jnp.concatenate([wi_ref[...].astype(F32), wf_ref[...].astype(F32)], axis=0).astype(BF16)
    gates = dot(w8, x_ref[...], 1, 1)
    row8 = iota(gates.shape, 0)
    for h in range(heads):
        gates = gates + jnp.where(row8 == h, bi_ref[h], 0.0)
        gates = gates + jnp.where(row8 == h + heads, bf_ref[h], 0.0)
    in_gate, forget_pre = gates[:heads], gates[heads:]
    log_forget = jnp.minimum(forget_pre, 0.0) - jnp.log1p(jnp.exp(-jnp.abs(forget_pre)))
    start = (pos_ref[...] == 0).astype(F32)
    stacked = jnp.concatenate([log_forget, start, jnp.zeros((7 - heads, n), F32)], axis=0)
    upto = (iota((n, n), 0) <= iota((n, n), 1)).astype(F32)
    cum = dot_exact(stacked, upto)
    lc_row, dc_row = cum[:heads], cum[heads : heads + 1]
    rows_ref[...] = jnp.concatenate(
        [in_gate, forget_pre, lc_row, dc_row, jnp.zeros((3, n), F32)], axis=0
    )
    ig = column_of(in_gate)
    lc = column_of(lc_row)
    dc = jnp.broadcast_to(dc_row, (128, n)).T
    lc_ref[...] = lc
    dc_ref[...] = dc
    total, last = lc[n - 1 :], dc[n - 1 :]
    key_log = jnp.where(dc == last, total - lc + ig, NEG)
    kl_ref[...] = key_log
    own_max = jnp.max(key_log, axis=0, keepdims=True)
    weight = jnp.exp(key_log - own_max)
    vectors = []
    for h in range(heads):
        weighted = k_ref[:, dk * h : dk * (h + 1)].astype(F32) * weight[:, h : h + 1]
        vectors.append(jnp.sum(weighted, axis=0, keepdims=True))
        memory = dot_left(weighted, v_ref[:, dv * h : dv * (h + 1)], 0, 0)
        mem_ref[dk // 8 * h : dk // 8 * (h + 1)] = memory.reshape(dk // 8, 8, dv)
    cut = jnp.where(last > 0.5, BIG, 0.0)
    tile = jnp.concatenate(
        vectors
        + [own_max, total - cut, ig[:1] - lc[:1], jnp.where(dc[:1] < 0.5, 1.0, 0.0)],
        axis=0,
    )
    pay_ref[...] = jnp.broadcast_to(tile[None], pay_ref.shape)


def pairs_kernel(
    heads, rows_ref, lc_ref, dc_ref, q_ref, k_ref, v_ref, g_ref,
    wl_ref, pc_ref, gv_ref, rm_ref, ls_ref, lg_ref,
):
    n = q_ref.shape[0]
    dk = k_ref.shape[1] // heads
    dv = v_ref.shape[1] // heads
    lc, dc = lc_ref[...], dc_ref[...]
    mask = (iota((n, n), 0) >= iota((n, n), 1)) & (dc[:, :1] == rows_ref[3 * heads : 3 * heads + 1])
    rm = jnp.zeros((n, 128), F32)
    ls, lg = rm, rm
    for h in range(heads):
        offset = rows_ref[h : h + 1] - rows_ref[2 * heads + h : 2 * heads + h + 1]
        pair_log = jnp.where(mask, lc[:, h : h + 1] + offset, NEG)
        row_max = jnp.max(pair_log, axis=1, keepdims=True)
        weight = jnp.exp(pair_log - row_max)
        ks, vs = slice(dk * h, dk * (h + 1)), slice(dv * h, dv * (h + 1))
        coupled = dot(q_ref[:, ks], k_ref[:, ks], 1, 1) * weight
        grad_pair = dot(g_ref[:, vs], v_ref[:, vs], 1, 1)
        wl_ref[h] = weight
        pc_ref[h] = coupled
        gv_ref[h] = grad_pair
        rm = put(rm, row_max, h)
        ls = put(ls, jnp.sum(coupled, axis=1, keepdims=True), h)
        lg = put(lg, jnp.sum(coupled * grad_pair, axis=1, keepdims=True), h)
    rm_ref[...] = rm
    ls_ref[...] = ls
    lg_ref[...] = lg


def shift_down(x, d, fill):
    return jnp.where(iota(x.shape, 0) < d, fill, pltpu.roll(x, d, 0))


def shift_up(x, d, fill):
    size = x.shape[0]
    return jnp.where(iota(x.shape, 0) >= size - d, fill, pltpu.roll(x, size - d, 0))


def dual_kernel(
    heads, scale, me_ref, ag_ref, mem_ref, lc_ref, dc_ref, rm_ref, ls_ref, q_ref, g_ref,
    pay_ref, coef_ref, later_ref, small_ref, cols_ref,
):
    count = ag_ref.shape[0]
    n = q_ref.shape[0]
    dk = q_ref.shape[1] // heads
    dv = g_ref.shape[1] // heads
    me = me_ref[0]
    own_max, total = ag_ref[:, heads, :], ag_ref[:, heads + 1, :]
    first, valid = ag_ref[:, heads + 2, :], ag_ref[:, heads + 3, :]
    row = iota(own_max.shape, 0)
    lane = iota(own_max.shape, 1)
    steps = [1 << i for i in range((count - 1).bit_length())]
    t, m = total, own_max
    for d in steps:
        m = jnp.maximum(shift_down(m, d, NEG) + t, m)
        t = shift_down(t, d, 0.0) + t
    in_max = shift_down(m, 1, NEG)
    dual_max = jnp.where(valid > 0.5, -jnp.maximum(in_max, first), NEG)
    t, r = total, dual_max
    for d in steps:
        r = jnp.maximum(r, t + shift_up(r, d, NEG))
        t = t + shift_up(t, d, 0.0)
    later_max = shift_up(r, 1, NEG)
    my_head = me // (count // heads)
    coefs = (
        jnp.exp(in_max + total - m),
        jnp.exp(own_max - m),
        jnp.exp(total + later_max - r),
        jnp.exp(dual_max - r),
    )
    for i, c in enumerate(coefs):
        mine = jnp.sum(jnp.where(lane == my_head, c, 0.0), axis=1, keepdims=True)
        coef_ref[i] = jnp.broadcast_to(mine, c.shape)

    def at_me(x):
        return jnp.sum(jnp.where(row == me, x, 0.0), axis=0, keepdims=True)

    in_me, later_me, dual_me, total_me = at_me(in_max), at_me(later_max), at_me(dual_max), at_me(total)
    later_row = iota((count, count), 0) < iota((count, count), 1)
    between = dot_exact(later_row.astype(F32), jnp.where(row < me, total, 0.0))
    weight = jnp.where(row < me, jnp.exp(jnp.minimum(own_max + between - in_me, 0.0)), 0.0)
    earlier_row = iota((count, count), 0) > iota((count, count), 1)
    between = dot_exact(earlier_row.astype(F32), jnp.where(row > me, total, 0.0))
    later_ref[...] = jnp.where(
        row > me, jnp.exp(jnp.minimum(dual_max + between - later_me, 0.0)), 0.0
    )
    vectors = [
        jnp.sum(weight[:, h : h + 1] * ag_ref[:, h, :], axis=0, keepdims=True) for h in range(heads)
    ]
    through = jnp.exp(in_me + total_me + later_me)
    small_ref[...] = jnp.concatenate(
        vectors + [later_me, through, jnp.zeros((6 - heads, 128), F32)], axis=0
    )

    lc, open_query = lc_ref[...], dc_ref[...] < 0.5
    cross_log = jnp.where(open_query, lc + in_me, NEG)
    row_max = jnp.maximum(rm_ref[...], cross_log)
    inside = jnp.exp(rm_ref[...] - row_max)
    cross = jnp.exp(cross_log - row_max)
    qn = jnp.zeros((n, 128), F32)
    for h in range(heads):
        along = q_ref[:, dk * h : dk * (h + 1)].astype(F32) * vectors[h]
        qn = put(qn, jnp.sum(along, axis=1, keepdims=True), h)
    sums = scale * (ls_ref[...] * inside + cross * qn)
    floor = jnp.exp(-row_max)
    size = jnp.abs(sums)
    inverse = 1.0 / jnp.maximum(size, floor)
    active = jnp.where(size > floor, jnp.where(sums > 0.0, 1.0, -1.0), 0.0)
    query_weight = jnp.where(open_query, jnp.exp(jnp.minimum(lc - row_max - dual_me, 0.0)), 0.0)
    cols_ref[0] = inside
    cols_ref[1] = cross
    cols_ref[2] = inverse
    cols_ref[3] = active
    cols_ref[4] = query_weight
    cols_ref[5] = qn
    grad_weight = query_weight * inverse * scale
    pay_ref[:, 0:8, :] = mem_ref[...]
    for h in range(heads):
        weighted = g_ref[:, dv * h : dv * (h + 1)].astype(F32) * grad_weight[:, h : h + 1]
        memory = dot_right(q_ref[:, dk * h : dk * (h + 1)], weighted, 0, 0)
        pay_ref[dk // 8 * h : dk // 8 * (h + 1), 8:16, :] = memory.reshape(dk // 8, 8, dv)


def scan_kernel(got_ref, coef_ref, out_ref):
    count = got_ref.shape[0]
    dv = got_ref.shape[2]
    reps = dv // 128

    def wide(i, j):
        return jnp.concatenate([coef_ref[i, pl.ds(j, 1), :]] * reps, axis=1)

    def forward(j, state):
        out_ref[j, 0:8, :] = state
        return wide(0, j) * state + wide(1, j) * got_ref[j, 0:8, :]

    def backward(i, state):
        j = count - 1 - i
        out_ref[j, 8:16, :] = state
        return wide(2, j) * state + wide(3, j) * got_ref[j, 8:16, :]

    def both(i, states):
        return forward(i, states[0]), backward(i, states[1])

    zero = jnp.zeros((8, dv), F32)
    lax.fori_loop(0, count, both, (zero, zero), unroll=8)


def vector_kernel(
    heads, scale, mem_ref, cols_ref, lg_ref, q_ref, g_ref, pay_ref, gt_ref, gc_ref
):
    n = q_ref.shape[0]
    dk = q_ref.shape[1] // heads
    dv = g_ref.shape[1] // heads
    gc = jnp.zeros((n, 128), F32)
    for h in range(heads):
        memory = mem_ref[dk // 8 * h : dk // 8 * (h + 1), 0:8, :].reshape(dk, dv)
        crossing = dot_right(q_ref[:, dk * h : dk * (h + 1)], memory, 1, 0)
        along = g_ref[:, dv * h : dv * (h + 1)].astype(F32) * crossing
        gc = put(gc, jnp.sum(along, axis=1, keepdims=True), h)
    inverse = cols_ref[2]
    gt = -scale * (lg_ref[...] * cols_ref[0] + cols_ref[1] * gc) * inverse * inverse * cols_ref[3]
    gt_ref[...] = gt
    gc_ref[...] = gc
    weight = cols_ref[4] * gt * scale
    vectors = [
        jnp.sum(
            q_ref[:, dk * h : dk * (h + 1)].astype(F32) * weight[:, h : h + 1], axis=0, keepdims=True
        )
        for h in range(heads)
    ]
    pay_ref[...] = jnp.broadcast_to(jnp.concatenate(vectors, axis=0)[None], pay_ref.shape)


def grads_kernel(
    heads, scale, mem_ref, cols_ref, small_ref, kl_ref, gt_ref, gc_ref, wl_ref, pc_ref, gv_ref,
    q_ref, k_ref, v_ref, g_ref,
    gq_ref, gvalue_ref, gk_ref, row_ref, cc_ref, cold_ref, pass_ref,
):
    n = q_ref.shape[0]
    dk = q_ref.shape[1] // heads
    dv = g_ref.shape[1] // heads
    gt, gc = gt_ref[...], gc_ref[...]
    inside, cross, inverse, qn = cols_ref[0], cols_ref[1], cols_ref[2], cols_ref[5]
    key_scale = jnp.exp(kl_ref[...] + small_ref[heads : heads + 1])
    row_part = scale * cross * (inverse * gc + gt * qn)
    column_cross = jnp.zeros((n, 128), F32)
    through = jnp.zeros((1, 128), F32)
    for h in range(heads):
        ks, vs = slice(dk * h, dk * (h + 1)), slice(dv * h, dv * (h + 1))
        one = slice(h, h + 1)
        q, k, v, g = q_ref[:, ks], k_ref[:, ks], v_ref[:, vs], g_ref[:, vs]
        slab = slice(dk // 8 * h, dk // 8 * (h + 1))
        memory = mem_ref[slab, 0:8, :].reshape(dk, dv)
        following = mem_ref[slab, 8:16, :].reshape(dk, dv)
        follow_high, follow_low = split(following)
        factor = inside[:, one] * (inverse[:, one] * gv_ref[h] + gt[:, one])
        pair_grad = factor * pc_ref[h]
        cold_ref[one, :] = scale * jnp.sum(pair_grad, axis=0, keepdims=True)
        row_part = row_part + put(
            jnp.zeros((n, 128), F32), scale * jnp.sum(pair_grad, axis=1, keepdims=True), h
        )
        score_high, score_low = split(factor * wl_ref[h])
        grad_query = dot(score_high, k, 1, 0) + dot(score_low, k, 1, 0)
        grad_query = grad_query + cross[:, one] * (
            inverse[:, one] * dot_right(g, memory, 1, 1) + gt[:, one] * small_ref[one]
        )
        gq_ref[:, ks] = (scale * grad_query).astype(BF16)
        grad_key = dot(score_high, q, 0, 0) + dot(score_low, q, 0, 0)
        carried = dot(v, follow_high, 1, 1) + dot(v, follow_low, 1, 1)
        gk_ref[:, ks] = scale * grad_key + key_scale[:, one] * carried
        carried = dot(k, follow_high, 1, 0) + dot(k, follow_low, 1, 0)
        along = jnp.sum(v.astype(F32) * carried, axis=1, keepdims=True)
        column_cross = put(column_cross, key_scale[:, one] * along, h)
        coupled = pc_ref[h] * (scale * inside[:, one] * inverse[:, one])
        grad_value = dot_left(coupled, g, 0, 0) + key_scale[:, one] * carried
        gvalue_ref[:, vs] = grad_value.astype(BF16)
        product = jnp.sum(jnp.sum(memory * following, axis=0, keepdims=True), axis=1, keepdims=True)
        through = put(through, product, h)
    row_ref[...] = row_part
    cc_ref[...] = column_cross
    cold_ref[heads:, :] = jnp.zeros((8 - heads, n), F32)
    pass_ref[...] = jnp.broadcast_to(through, pass_ref.shape)


def weights_kernel(
    heads, got_ref, later_ref, small_ref, kl_ref, rows_ref, row_ref, cc_ref, cold_ref, pass_ref,
    gk_ref, k_ref, x_ref, gkey_ref, pay_ref,
):
    n = k_ref.shape[0]
    dk = k_ref.shape[1] // heads
    key_scale = jnp.exp(kl_ref[...] + small_ref[heads : heads + 1])
    later = later_ref[...]
    column_cross = cc_ref[...]
    through = pass_ref[:1]
    for h in range(heads):
        ks, one = slice(dk * h, dk * (h + 1)), slice(h, h + 1)
        vector = jnp.sum(later[:, one] * got_ref[:, h, :], axis=0, keepdims=True)
        k = k_ref[:, ks].astype(F32)
        along = jnp.sum(k * vector, axis=1, keepdims=True)
        column_cross = column_cross + put(jnp.zeros((n, 128), F32), key_scale[:, one] * along, h)
        gkey_ref[:, ks] = (gk_ref[:, ks] + key_scale[:, one] * vector).astype(BF16)
        product = jnp.sum(small_ref[one] * vector, axis=1, keepdims=True)
        through = through + put(jnp.zeros((1, 128), F32), product, h)
    through = through * small_ref[heads + 1 : heads + 2]
    row = row_ref[...].T[:8]
    crossing = column_cross.T[:8]
    passing = jnp.broadcast_to(through, (128, 128)).T[:8, :1]
    inner = cold_ref[...]
    after = iota((n, n), 0) >= iota((n, n), 1)
    suffix = dot_exact(row - inner, after.astype(F32))
    prefix = dot_exact(crossing, 1.0 - after.astype(F32))
    grad_log = suffix + prefix + passing
    grad_forget = grad_log[:heads] / (1.0 + jnp.exp(rows_ref[heads : 2 * heads, :]))
    coefs = jnp.concatenate([(inner + crossing)[:heads], grad_forget], axis=0)
    high = coefs.astype(BF16).astype(F32)
    both = jnp.concatenate([high, coefs - high], axis=0).astype(BF16)
    product = dot(both, x_ref[...], 1, 0)
    result = product[: 2 * heads] + product[2 * heads :]
    tiles = result.shape[1] // 128
    for c in range(tiles):
        pay_ref[c] = result[:heads, 128 * c : 128 * (c + 1)]
        pay_ref[tiles + c] = result[heads:, 128 * c : 128 * (c + 1)]


def sum_kernel(got_ref, out_ref):
    total = jnp.sum(got_ref[...], axis=0, keepdims=True)
    out_ref[...] = jnp.broadcast_to(total, out_ref.shape)


def place_kernel(got_ref, first_ref, second_ref):
    tiles = got_ref.shape[0] // 2
    for c in range(tiles):
        first_ref[:, 128 * c : 128 * (c + 1)] = got_ref[c]
        second_ref[:, 128 * c : 128 * (c + 1)] = got_ref[tiles + c]


def call(body, shapes, *args, scalars=()):
    shapes = [s if isinstance(s, jax.ShapeDtypeStruct) else jax.ShapeDtypeStruct(s, F32) for s in shapes]
    return pl.pallas_call(
        body,
        out_shape=shapes,
        in_specs=[SMEM if i in scalars else VMEM for i in range(len(args))],
        out_specs=[VMEM] * len(shapes),
        compiler_params=pltpu.CompilerParams(vmem_limit_bytes=40 * 1024 * 1024),
    )(*args)


def exchange(x, axis):
    return lax.all_to_all(x, axis, 0, 0)


def local(
    layer_input, queries, keys, values, grad_out, doc_pos, w_input, b_input, w_forget, b_forget
):
    x, q, k, v, g = layer_input[0], queries[0], keys[0], values[0], grad_out[0]
    heads = w_input.shape[1]
    n = q.shape[0]
    dk, dv = q.shape[1] // heads, v.shape[1] // heads
    scale = dk ** (-0.5)
    count = lax.axis_size("ctx")
    me = lax.axis_index("ctx").astype(jnp.int32).reshape(1)
    part = functools.partial
    cols = (n, 128)
    pay, memory, rows, lc, dc, kl = call(
        part(gates_kernel, heads),
        [(count, 8, 128), (count, 8, dv), (16, n), cols, cols, cols],
        x, w_input.T, w_forget.T, b_input, b_forget, doc_pos, k, v,
        scalars=(3, 4),
    )
    got = exchange(pay, "ctx")
    wl, pc, gv, rm, ls, lg = call(
        part(pairs_kernel, heads),
        [(heads, n, n)] * 3 + [cols] * 3,
        rows, lc, dc, q, k, v, g,
    )
    pay, coef, later, small, tokens = call(
        part(dual_kernel, heads, scale),
        [(count, 16, dv), (4, count, 128), (count, 128), (8, 128), (6, n, 128)],
        me, got, memory, lc, dc, rm, ls, q, g,
        scalars=(0,),
    )
    got = exchange(pay, "ctx")
    (pay,) = call(scan_kernel, [(count, 16, dv)], got, coef)
    states = exchange(pay, "ctx")
    pay, gt, gc = call(
        part(vector_kernel, heads, scale), [(count, heads, 128), cols, cols], states, tokens, lg, q, g
    )
    got = exchange(pay, "ctx")
    grad_q, grad_v, gk, row, cc, cold, through = call(
        part(grads_kernel, heads, scale),
        [
            jax.ShapeDtypeStruct(q.shape, BF16), jax.ShapeDtypeStruct(v.shape, BF16),
            k.shape, cols, cols, (8, n), (8, 128),
        ],
        states, tokens, small, kl, gt, gc, wl, pc, gv, q, k, v, g,
    )
    chunks = 2 * x.shape[1] // 128
    grad_k, pay = call(
        part(weights_kernel, heads),
        [jax.ShapeDtypeStruct(k.shape, BF16), (chunks, heads, 128)],
        got, later, small, kl, rows, row, cc, cold, through, gk, k, x,
    )
    got = exchange(pay, "ctx")
    (pay,) = call(sum_kernel, [(lax.axis_size("dp"), heads, 128)], got)
    got = exchange(pay, "dp")
    (pay,) = call(sum_kernel, [(count, heads, 128)], got)
    got = exchange(pay, "ctx")
    first, second = call(place_kernel, [(heads, x.shape[1])] * 2, got)
    return (grad_q[None], grad_k[None], grad_v[None], first.T, second.T)


def solution(mesh):
    split_rows = P("dp", "ctx", None)
    placed = (split_rows,) * 5 + (P("dp", "ctx"),) + (P(),) * 4
    return jax.shard_map(
        local,
        mesh=mesh,
        in_specs=placed,
        out_specs=(split_rows, split_rows, split_rows, P(), P()),
        check_vma=False,
    )
```

time: 1340 us -> 189 us (0.14)
  blocking collectives: 731 us -> 112 us
  other arithmetic: 302 us -> 0 us
  waiting for transfers between devices: 233 us -> 6.88 us
  matrix products: 27.9 us -> 0 us
  starting transfers between devices: 0.12 us -> 19.6 us
  local copies, waits for them, and re-layouts: 16.3 us -> 33.7 us
  Pallas kernels: 0 us -> 14.7 us
  between operations: 14.9 us -> 0.81 us
    unnamed x2 -> x0, blocking collectives: 545 us -> none
    psum x1 -> x0, waiting for transfers between devices: 233 us -> none  [local(): lax.psum((inner_product('sd,sh->dh', layer_wide, column_part), grad_forge...]
    all_gather x4 -> x0, blocking collectives: 186 us -> none  [prefix(): gathered = jax.tree.map(lambda a: lax.all_gather(a, axis), part)]
    all_to_all x0 -> x5, blocking collectives: none -> 112 us  [exchange(): return lax.all_to_all(x, axis, 0, 0)]
    add x188 -> x0, other arithmetic: 89.2 us -> none  [the longest x63 82.5 us: combine_states(): keep_former[:, None, None] * matrix_former]
    select_n x63 -> x0, other arithmetic: 85.6 us -> none  [combine_states(): keep_former = jnp.where(cut, 0.0, jnp.exp(shifted - new_max))]
    gt x63 -> x0, other arithmetic: 76.3 us -> none  [combine_states(): cut = reset_latter > 0.5]
    exp x66 -> x0, other arithmetic: 44.2 us -> none  [the longest x63 44 us: combine_states(): keep_latter = jnp.exp(max_latter - new_max)]
  transfers between devices with their start and end apart: 3 -> 2, of which waited for: 1 -> 1; matrix products, arithmetic and copies ran while one was open for 2% -> 0% of each run, Pallas kernels for 0% -> 3%
where the time goes in v1:
time: 189 us; the launch traced here: 188 us
  blocking collectives  112 us (59%)
  local copies, waits for them, and re-layouts  33.7 us (18%)
  starting transfers between devices  19.6 us (10%)
  Pallas kernels  14.7 us (8%)
  waiting for transfers between devices  6.88 us (4%)
    all_to_all x5, blocking collectives, exchange(): return lax.all_to_all(x, axis, 0, 0)  112 us
    unnamed x90, local copies, waits for them, and re-layouts  33.7 us
    all_to_all x2, starting transfers between devices, exchange(): return lax.all_to_all(x, axis, 0, 0)  19.6 us
    pallas_call x10, Pallas kernels, call(): pl.pallas_call(body, out_shape=shapes, in_specs=[SMEM if i in scalars els...  14.7 us
    all_to_all x2, waiting for transfers between devices, exchange(): return lax.all_to_all(x, axis, 0, 0)  6.88 us
  transfers between devices with their start and end apart: 2, of which 1 were waited for; matrix products, arithmetic and copies ran while one was open for 0% of the time, Pallas kernels for 3%

profile of v1, /device:TPU:1, one launch (start us, length us, event | category | flops | bytes accessed | tf_op | source)
XLA Modules:
  0.0 188.1 jit_solution(1842870414438531625)
XLA Ops:
  0.7 1.6 copy-done.1
  2.3 1.0 copy-done.3
  3.3 0.9 copy-done.6
  5.0 0.8 copy-done.32
  7.8 2.8 %shard_map.137 = (f32[64,8,128]{2,1,0:T(8,128)}, f32[64,8,256]{2,1,0:T(8,128)S(1)}, f32[16,256]{1,0:T(8,128)S(1)}, f32[256,128]{1,0:T(8,128)S(1)}, f32[256,128]{1,0:T(8,128)S(1)}, /*index=5*/f32[256,128]{1,0:T(8,128)S(1)}) custom-call(bf16[256,4096]{1,0:T(8,128)(2,1)S(1)} %bitcast.17, bf16[4,4096]{1,0:T(4,128)(2,1)S(1)} %bitcast.30, ...), custom_call_target="tpu_custom_call" | custom-call | tf_op jit(solution)/shard_map/pallas_call | solution.py:384
  10.6 13.0 %all-to-all-start = ((f32[64,8,128]{2,1,0:T(8,128)}), f32[64,8,128]{2,1,0:T(8,128)S(1)}, u32[]{:S(2)}, u32[]{:S(2)}) async-start(f32[64,8,128]{2,1,0:T(8,128)} %get-tuple-element.36), calls=%async_computation | async-start | bytes 524288 | tf_op jit(solution)/shard_map/all_to_all | solution.py:394
  23.6 1.3 shard_map.138
  24.9 1.0 copy-done.8
  25.9 1.0 copy-done.10
  26.9 1.0 copy-done.12
  29.8 6.9 %all-to-all-done.ag_ref = f32[64,8,128]{2,1,0:T(8,128)S(1)} async-done(((f32[64,8,128]{2,1,0:T(8,128)}), f32[64,8,128]{2,1,0:T(8,128)S(1)}, u32[]{:S(2)}, u32[]{:S(2)}) %all-to-all-start) | async-done | bytes 262176 | tf_op jit(solution)/shard_map/all_to_all | solution.py:394
  36.7 0.9 copy-done.21
  37.6 0.9 copy-done.23
  38.5 1.2 shard_map.139
  41.0 32.5 %all_to_all.35.got_ref = f32[64,16,256]{2,1,0:T(8,128)S(1)} all-to-all(f32[64,16,256]{2,1,0:T(8,128)S(1)} %get-tuple-element.43), channel_id=1, replica_groups=mesh['ctx'=64,'dp'=4] {'ctx'}, dimensions={0} | all-to-all | bytes 2097152 | tf_op jit(solution)/shard_map/all_to_all | solution.py:394
  73.7 34.2 %all_to_all.36.mem_ref = f32[64,16,256]{2,1,0:T(8,128)S(1)} all-to-all(f32[64,16,256]{2,1,0:T(8,128)S(1)} %shard_map.140), channel_id=1, replica_groups=mesh['ctx'=64,'dp'=4] {'ctx'}, dimensions={0} | all-to-all | bytes 2097152 | tf_op jit(solution)/shard_map/all_to_all | solution.py:394
  110.6 6.7 %all-to-all-start.3 = ((f32[64,4,128]{2,1,0:T(4,128)}), f32[64,4,128]{2,1,0:T(4,128)}, u32[]{:S(2)}, u32[]{:S(2)}) async-start(f32[64,4,128]{2,1,0:T(4,128)} %copy-done.24), calls=%async_computation.3 | async-start | bytes 262144 | tf_op jit(solution)/shard_map/all_to_all | solution.py:394
  117.3 1.2 copy-done.9
  118.5 1.2 copy-done.11
  119.7 1.2 copy-done.13
  121.0 0.9 copy-done.17
  121.9 0.9 copy-done.19
  123.5 5.1 %shard_map.142 = (bf16[256,512]{1,0:T(8,128)(2,1)}, bf16[256,1024]{1,0:T(8,128)(2,1)}, f32[256,512]{1,0:T(8,128)S(1)}, f32[256,128]{1,0:T(8,128)S(1)}, f32[256,1...) custom-call(f32[64,16,256]{2,1,0:T(8,128)S(1)} %all_to_all.36.mem_ref, ...), custom_call_target="tpu_custom_call" | custom-call | tf_op jit(solution)/shard_map/pallas_call | solution.py:384
  128.5 0.8 copy-done.14
  131.8 1.6 copy-done.2
  133.4 1.0 copy-done.15
  134.4 0.9 copy-done.28
  135.4 0.9 copy-done.30
  139.1 2.6 %shard_map.143 = (bf16[256,512]{1,0:T(8,128)(2,1)}, f32[64,4,128]{2,1,0:T(4,128)S(1)}) custom-call(f32[64,4,128]{2,1,0:T(4,128)} %all-to-all-done.3.got_ref, f32[64,128]{1,0:T(8,128)S(1)} %copy-done.34, f32[8,128]{1,0:T(8,128)S(1)} %copy-done.37, f32[256,128]{1,0:T(8,128)S(1)} %get-tuple-element.47.kl_ref, f32[16,256]{1,0:T(8,128)S(1)} %get-tuple-element.40.rows_ref, ...), custom_call_target="tpu_custom_call" | custom-call | tf_op jit(solution)/shard_map/pallas_call | solution.py:384
  141.7 21.2 %all_to_all.37.got_ref = f32[64,4,128]{2,1,0:T(4,128)S(1)} all-to-all(f32[64,4,128]{2,1,0:T(4,128)S(1)} %get-tuple-element.64), channel_id=1, replica_groups=mesh['ctx'=64,'dp'=4] {'ctx'}, dimensions={0} | all-to-all | bytes 262144 | tf_op jit(solution)/shard_map/all_to_all | solution.py:394
  162.9 8.2 %all_to_all.38.got_ref = f32[4,4,128]{2,1,0:T(4,128)S(1)} all-to-all(f32[4,4,128]{2,1,0:T(4,128)S(1)} %shard_map.144), channel_id=1, replica_groups=mesh['ctx'=64,'dp'=4] {'dp'}, dimensions={0} | all-to-all | bytes 16384 | tf_op jit(solution)/shard_map/all_to_all | solution.py:394
  171.1 16.4 %all_to_all.39.got_ref = f32[64,4,128]{2,1,0:T(4,128)S(1)} all-to-all(f32[64,4,128]{2,1,0:T(4,128)S(1)} %shard_map.145), channel_id=1, replica_groups=mesh['ctx'=64,'dp'=4] {'ctx'}, dimensions={0} | all-to-all | bytes 262144 | tf_op jit(solution)/shard_map/all_to_all | solution.py:394
  (77 shorter events, 15.6 us)
Async XLA Ops:
  0.6 22.9 %copy-start = (bf16[1,256,1024]{2,1,0:T(8,128)(2,1)S(1)}, bf16[1,256,1024]{2,1,0:T(8,128)(2,1)}, u32[]{:S(2)}) copy-start(bf16[1,256,1024]{2,1,0:T(8,128)(2,1)} %param.14) | copy-start | bytes 1572868
  0.6 1.7 copy-start.1
  2.3 1.0 copy-start.3
  3.3 0.9 copy-start.6
  4.3 0.8 copy-start.31
  5.0 0.8 copy-start.32
  5.8 0.7 copy-start.42
  7.8 15.8 %copy-start.4 = (bf16[1,256,1024]{2,1,0:T(8,128)(2,1)S(1)}, bf16[1,256,1024]{2,1,0:T(8,128)(2,1)}, u32[]{:S(2)}) copy-start(bf16[1,256,1024]{2,1,0:T(8,128)(2,1)} %param.13) | copy-start | bytes 1572868
  7.8 15.8 %copy-start.5 = (bf16[1,256,512]{2,1,0:T(8,128)(2,1)S(1)}, bf16[1,256,512]{2,1,0:T(8,128)(2,1)}, u32[]{:S(2)}) copy-start(bf16[1,256,512]{2,1,0:T(8,128)(2,1)} %param.11) | copy-start | bytes 786436
  7.8 15.8 %copy-start.7 = (bf16[1,256,512]{2,1,0:T(8,128)(2,1)S(1)}, bf16[1,256,512]{2,1,0:T(8,128)(2,1)}, u32[]{:S(2)}) copy-start(bf16[1,256,512]{2,1,0:T(8,128)(2,1)} %param.12) | copy-start | bytes 786436
  10.6 26.2 %all-to-all-start = ((f32[64,8,128]{2,1,0:T(8,128)}), f32[64,8,128]{2,1,0:T(8,128)S(1)}, u32[]{:S(2)}, u32[]{:S(2)}) async-start(f32[64,8,128]{2,1,0:T(8,128)} %get-tuple-element.36), calls=%async_computation | async-start | bytes 524288 | tf_op jit(solution)/shard_map/all_to_all | solution.py:394
  24.9 1.0 copy-start.8
  25.9 1.0 copy-start.10
  26.9 1.0 copy-start.12
  36.7 0.9 copy-start.21
  37.6 0.9 copy-start.23
  73.4 34.5 %copy-start.26 = (f32[256,128]{1,0:T(8,128)S(1)}, f32[256,128]{1,0:T(8,128)}, u32[]{:S(2)}) copy-start(f32[256,128]{1,0:T(8,128)} %copy-done.25) | copy-start | bytes 393220
  110.6 21.2 %all-to-all-start.3 = ((f32[64,4,128]{2,1,0:T(4,128)}), f32[64,4,128]{2,1,0:T(4,128)}, u32[]{:S(2)}, u32[]{:S(2)}) async-start(f32[64,4,128]{2,1,0:T(4,128)} %copy-done.24), calls=%async_computation.3 | async-start | bytes 262144 | tf_op jit(solution)/shard_map/all_to_all | solution.py:394
  117.3 1.2 copy-start.9
  118.5 1.2 copy-start.11
  119.7 1.2 copy-start.13
  121.0 0.9 copy-start.17
  121.9 0.9 copy-start.19
  122.8 0.7 copy-start.36
  128.5 0.8 copy-start.14
  131.8 1.6 copy-start.2
  133.4 1.0 copy-start.15
  134.4 0.9 copy-start.28
  135.4 0.9 copy-start.30
  136.3 0.8 copy-start.34
  137.0 0.7 copy-start.37
  137.7 0.7 copy-start.39
  (15 other events, 9.6 us)

commit v2 on v1

--- a/solution.py
+++ b/solution.py
@@ -54,10 +54,15 @@
     return jnp.where(iota(acc.shape, 1) == h, col, acc)
 
 
+def pick(row, lane):
+    return jnp.sum(jnp.where(iota(row.shape, 1) == lane, row, 0.0), axis=1, keepdims=True)
+
+
 def gates_kernel(
-    heads, x_ref, wi_ref, wf_ref, bi_ref, bf_ref, pos_ref, k_ref, v_ref,
-    pay_ref, mem_ref, rows_ref, lc_ref, dc_ref, kl_ref,
-):
+    heads, me_ref, x_ref, wi_ref, wf_ref, bi_ref, bf_ref, pos_ref, k_ref, v_ref,
+    give_ref, mem_ref, tile_ref, rows_ref, lc_ref, dc_ref, kl_ref,
+):
+    core = me_ref[0] % 2
     n = x_ref.shape[0]
     dk = k_ref.shape[1] // heads
     dv = v_ref.shape[1] // heads
@@ -99,7 +104,36 @@
         + [own_max, total - cut, ig[:1] - lc[:1], jnp.where(dc[:1] < 0.5, 1.0, 0.0)],
         axis=0,
     )
-    pay_ref[...] = jnp.broadcast_to(tile[None], pay_ref.shape)
+    tile_ref[...] = tile
+    half = mem_ref.shape[0] // 2
+    give_ref[:half] = mem_ref[pl.ds((1 - core) * half, half)]
+    give_ref[half] = jnp.concatenate([tile, jnp.zeros((8, dv - 128), F32)], axis=1)
+
+
+def first_kernel(heads, me_ref, mem_ref, tile_ref, got_ref, out_ref):
+    core = me_ref[0] % 2
+    half, dv = out_ref.shape[0], mem_ref.shape[2]
+    mine, other = tile_ref[...], got_ref[half, :, :128]
+    even = jnp.where(core == 0, mine, other)
+    odd = jnp.where(core == 0, other, mine)
+    chip_max = jnp.maximum(even[4:5] + odd[5:6], odd[4:5])
+    keep = jnp.exp(even[4:5] + odd[5:6] - chip_max)
+    add = jnp.exp(odd[4:5] - chip_max)
+    vectors = [
+        keep[:, h : h + 1] * even[h : h + 1] + add[:, h : h + 1] * odd[h : h + 1]
+        for h in range(heads)
+    ]
+    both = jnp.where(iota(even.shape, 1) < heads, even, pltpu.roll(odd, heads, 1))
+    tile = jnp.concatenate(vectors + [both[heads:]], axis=0)
+    out_ref[:, :, dv:] = jnp.broadcast_to(tile[None], (half, 8, 128))
+    weight_mine = jnp.where(core == 0, keep, add)
+    weight_other = jnp.where(core == 0, add, keep)
+    per_head = half // (heads // 2)
+    for i in range(heads // 2):
+        at = core * (heads // 2) + i
+        slab = slice(i * per_head, (i + 1) * per_head)
+        own = mem_ref[pl.ds(core * half + i * per_head, per_head)]
+        out_ref[slab, :, :dv] = pick(weight_mine, at) * own + pick(weight_other, at) * got_ref[slab]
 
 
 def pairs_kernel(
@@ -142,59 +176,93 @@
 
 
 def dual_kernel(
-    heads, scale, me_ref, ag_ref, mem_ref, lc_ref, dc_ref, rm_ref, ls_ref, q_ref, g_ref,
-    pay_ref, coef_ref, later_ref, small_ref, cols_ref,
-):
-    count = ag_ref.shape[0]
+    heads, scale, me_ref, got_ref, tile_ref, pair_ref, lc_ref, dc_ref, rm_ref, ls_ref, q_ref, g_ref,
+    give_ref, dual_ref, coef_ref, later_ref, small_ref, cols_ref,
+):
+    count = got_ref.shape[0]
     n = q_ref.shape[0]
     dk = q_ref.shape[1] // heads
     dv = g_ref.shape[1] // heads
     me = me_ref[0]
-    own_max, total = ag_ref[:, heads, :], ag_ref[:, heads + 1, :]
-    first, valid = ag_ref[:, heads + 2, :], ag_ref[:, heads + 3, :]
-    row = iota(own_max.shape, 0)
-    lane = iota(own_max.shape, 1)
+    core, chip = me % 2, me // 2
+    max_even, total_even = got_ref[:, heads, dv:], got_ref[:, heads + 1, dv:]
+    first_even, valid_even = got_ref[:, heads + 2, dv:], got_ref[:, heads + 3, dv:]
+    max_odd, total_odd, first_odd, valid_odd = (
+        pltpu.roll(x, 128 - heads, 1) for x in (max_even, total_even, first_even, valid_even)
+    )
+    row = iota(max_even.shape, 0)
+    lane = iota(max_even.shape, 1)
     steps = [1 << i for i in range((count - 1).bit_length())]
-    t, m = total, own_max
+    chip_max = jnp.maximum(max_even + total_odd, max_odd)
+    total = total_even + total_odd
+    t, m = total, chip_max
     for d in steps:
         m = jnp.maximum(shift_down(m, d, NEG) + t, m)
         t = shift_down(t, d, 0.0) + t
-    in_max = shift_down(m, 1, NEG)
-    dual_max = jnp.where(valid > 0.5, -jnp.maximum(in_max, first), NEG)
-    t, r = total, dual_max
+    in_even = shift_down(m, 1, NEG)
+    in_odd = jnp.maximum(in_even + total_even, max_even)
+    dual_even = jnp.where(valid_even > 0.5, -jnp.maximum(in_even, first_even), NEG)
+    dual_odd = jnp.where(valid_odd > 0.5, -jnp.maximum(in_odd, first_odd), NEG)
+    chip_dual = jnp.maximum(dual_even, total_even + dual_odd)
+    t, r = total, chip_dual
     for d in steps:
         r = jnp.maximum(r, t + shift_up(r, d, NEG))
         t = t + shift_up(t, d, 0.0)
-    later_max = shift_up(r, 1, NEG)
-    my_head = me // (count // heads)
+    later_odd = shift_up(r, 1, NEG)
+    later_even = jnp.maximum(dual_odd, total_odd + later_odd)
+    my_head = (heads // 2) * core + chip // (2 * count // heads)
     coefs = (
-        jnp.exp(in_max + total - m),
-        jnp.exp(own_max - m),
-        jnp.exp(total + later_max - r),
-        jnp.exp(dual_max - r),
+        jnp.exp(in_even + total - m),
+        jnp.exp(chip_max - m),
+        jnp.exp(total + later_odd - r),
+        jnp.exp(chip_dual - r),
     )
     for i, c in enumerate(coefs):
         mine = jnp.sum(jnp.where(lane == my_head, c, 0.0), axis=1, keepdims=True)
         coef_ref[i] = jnp.broadcast_to(mine, c.shape)
 
-    def at_me(x):
-        return jnp.sum(jnp.where(row == me, x, 0.0), axis=0, keepdims=True)
-
-    in_me, later_me, dual_me, total_me = at_me(in_max), at_me(later_max), at_me(dual_max), at_me(total)
+    def here(x):
+        return jnp.sum(jnp.where(row == chip, x, 0.0), axis=0, keepdims=True)
+
+    def mine_of(even, odd):
+        return here(jnp.where(core == 0, even, odd))
+
+    in_me, later_me = mine_of(in_even, in_odd), mine_of(later_even, later_odd)
+    dual_me, total_me = mine_of(dual_even, dual_odd), mine_of(total_even, total_odd)
+    keep = here(jnp.exp(in_even + total_even - in_odd))
+    add = here(jnp.exp(max_even - in_odd))
     later_row = iota((count, count), 0) < iota((count, count), 1)
-    between = dot_exact(later_row.astype(F32), jnp.where(row < me, total, 0.0))
-    weight = jnp.where(row < me, jnp.exp(jnp.minimum(own_max + between - in_me, 0.0)), 0.0)
+    between = dot_exact(later_row.astype(F32), jnp.where(row < chip, total, 0.0))
+    weight = jnp.where(
+        row < chip, jnp.exp(jnp.minimum(chip_max + between - here(in_even), 0.0)), 0.0
+    )
     earlier_row = iota((count, count), 0) > iota((count, count), 1)
-    between = dot_exact(earlier_row.astype(F32), jnp.where(row > me, total, 0.0))
+    between = dot_exact(earlier_row.astype(F32), jnp.where(row > chip, total, 0.0))
+    source = jnp.where(core == 0, dual_even, total_even + dual_odd)
     later_ref[...] = jnp.where(
-        row > me, jnp.exp(jnp.minimum(dual_max + between - later_me, 0.0)), 0.0
-    )
-    vectors = [
-        jnp.sum(weight[:, h : h + 1] * ag_ref[:, h, :], axis=0, keepdims=True) for h in range(heads)
-    ]
-    through = jnp.exp(in_me + total_me + later_me)
+        row > chip, jnp.exp(jnp.minimum(source + between - here(later_odd), 0.0)), 0.0
+    )
+    even_tile = jnp.where(core == 0, tile_ref[...], pair_ref[0, :, :128])
+    vectors = []
+    for h in range(heads):
+        one = slice(h, h + 1)
+        vector = jnp.sum(weight[:, one] * got_ref[:, h, dv:], axis=0, keepdims=True)
+        second = keep[:, one] * vector + add[:, one] * even_tile[one]
+        vectors.append(jnp.where(core == 0, vector, second))
     small_ref[...] = jnp.concatenate(
-        vectors + [later_me, through, jnp.zeros((6 - heads, 128), F32)], axis=0
+        vectors
+        + [
+            later_me,
+            jnp.exp(in_me + total_me + later_me),
+            keep,
+            add,
+            here(jnp.exp(total_odd + later_odd - later_even)),
+            here(jnp.exp(dual_odd - later_even)),
+            here(jnp.exp(dual_even - chip_dual)),
+            here(jnp.exp(total_even + dual_odd - chip_dual)),
+            jnp.zeros((8 - heads, 128), F32),
+        ],
+        axis=0,
     )
 
     lc, open_query = lc_ref[...], dc_ref[...] < 0.5
@@ -219,46 +287,77 @@
     cols_ref[4] = query_weight
     cols_ref[5] = qn
     grad_weight = query_weight * inverse * scale
-    pay_ref[:, 0:8, :] = mem_ref[...]
     for h in range(heads):
         weighted = g_ref[:, dv * h : dv * (h + 1)].astype(F32) * grad_weight[:, h : h + 1]
         memory = dot_right(q_ref[:, dk * h : dk * (h + 1)], weighted, 0, 0)
-        pay_ref[dk // 8 * h : dk // 8 * (h + 1), 8:16, :] = memory.reshape(dk // 8, 8, dv)
-
-
-def scan_kernel(got_ref, coef_ref, out_ref):
-    count = got_ref.shape[0]
-    dv = got_ref.shape[2]
+        dual_ref[dk // 8 * h : dk // 8 * (h + 1)] = memory.reshape(dk // 8, 8, dv)
+    half = give_ref.shape[0]
+    give_ref[...] = dual_ref[pl.ds((1 - core) * half, half)]
+
+
+def wide(coef_ref, i, j, reps):
+    return jnp.concatenate([coef_ref[i, pl.ds(j, 1), :]] * reps, axis=1)
+
+
+def second_kernel(heads, me_ref, got_ref, coef_ref, small_ref, dual_ref, pair_ref, out_ref):
+    core = me_ref[0] % 2
+    count, dv = got_ref.shape[0], dual_ref.shape[2]
     reps = dv // 128
 
-    def wide(i, j):
-        return jnp.concatenate([coef_ref[i, pl.ds(j, 1), :]] * reps, axis=1)
-
     def forward(j, state):
-        out_ref[j, 0:8, :] = state
-        return wide(0, j) * state + wide(1, j) * got_ref[j, 0:8, :]
-
-    def backward(i, state):
-        j = count - 1 - i
-        out_ref[j, 8:16, :] = state
-        return wide(2, j) * state + wide(3, j) * got_ref[j, 8:16, :]
-
-    def both(i, states):
-        return forward(i, states[0]), backward(i, states[1])
-
-    zero = jnp.zeros((8, dv), F32)
-    lax.fori_loop(0, count, both, (zero, zero), unroll=8)
+        out_ref[j, :, :dv] = state
+        step = wide(coef_ref, 1, j, reps) * got_ref[j, :, :dv]
+        return wide(coef_ref, 0, j, reps) * state + step
+
+    lax.fori_loop(0, count, forward, jnp.zeros((8, dv), F32), unroll=8)
+    even, odd = small_ref[10:11], small_ref[11:12]
+    weight_mine = jnp.where(core == 0, even, odd)
+    weight_other = jnp.where(core == 0, odd, even)
+    per_head = count // (heads // 2)
+    for i in range(heads // 2):
+        at = core * (heads // 2) + i
+        slab = slice(i * per_head, (i + 1) * per_head)
+        own = dual_ref[pl.ds(core * count + i * per_head, per_head)]
+        out_ref[slab, :, dv:] = pick(weight_mine, at) * own + pick(weight_other, at) * pair_ref[slab]
+
+
+def halves_kernel(heads, me_ref, got_ref, mem_ref, pair_ref, small_ref, give_ref, mine_ref):
+    core = me_ref[0] % 2
+    count, dv = give_ref.shape[0], mem_ref.shape[2]
+    per_head = count // (heads // 2)
+
+    def fill(even_ref, odd_ref, even_own):
+        for i in range(heads // 2):
+            at = core * (heads // 2) + i
+            slab = slice(i * per_head, (i + 1) * per_head)
+            before = got_ref[slab, :, :dv]
+            even_ref[slab] = before
+            odd_ref[slab] = pick(small_ref[6:7], at) * before + pick(small_ref[7:8], at) * even_own(slab)
+
+    @pl.when(core == 0)
+    def _():
+        fill(mine_ref, give_ref, lambda slab: mem_ref[slab])
+
+    @pl.when(core == 1)
+    def _():
+        fill(give_ref, mine_ref, lambda slab: pair_ref[slab])
 
 
 def vector_kernel(
-    heads, scale, mem_ref, cols_ref, lg_ref, q_ref, g_ref, pay_ref, gt_ref, gc_ref
-):
+    heads, scale, me_ref, mine_ref, pair_ref, got_ref, coef_ref, cols_ref, lg_ref, q_ref, g_ref,
+    out_ref, mem_ref, tile_ref, gt_ref, gc_ref,
+):
+    core = me_ref[0] % 2
     n = q_ref.shape[0]
     dk = q_ref.shape[1] // heads
     dv = g_ref.shape[1] // heads
+    count = got_ref.shape[0]
+    reps = dv // 128
+    mem_ref[pl.ds(core * count, count)] = mine_ref[...]
+    mem_ref[pl.ds((1 - core) * count, count)] = pair_ref[...]
     gc = jnp.zeros((n, 128), F32)
     for h in range(heads):
-        memory = mem_ref[dk // 8 * h : dk // 8 * (h + 1), 0:8, :].reshape(dk, dv)
+        memory = mem_ref[dk // 8 * h : dk // 8 * (h + 1)].reshape(dk, dv)
         crossing = dot_right(q_ref[:, dk * h : dk * (h + 1)], memory, 1, 0)
         along = g_ref[:, dv * h : dv * (h + 1)].astype(F32) * crossing
         gc = put(gc, jnp.sum(along, axis=1, keepdims=True), h)
@@ -273,31 +372,35 @@
         )
         for h in range(heads)
     ]
-    pay_ref[...] = jnp.broadcast_to(jnp.concatenate(vectors, axis=0)[None], pay_ref.shape)
-
-
-def grads_kernel(
-    heads, scale, mem_ref, cols_ref, small_ref, kl_ref, gt_ref, gc_ref, wl_ref, pc_ref, gv_ref,
-    q_ref, k_ref, v_ref, g_ref,
-    gq_ref, gvalue_ref, gk_ref, row_ref, cc_ref, cold_ref, pass_ref,
+    tile = jnp.concatenate(vectors + [jnp.zeros((8 - heads, 128), F32)], axis=0)
+    tile_ref[...] = tile
+    out_ref[:, :, dv:] = jnp.broadcast_to(tile[None], (count, 8, 128))
+
+    def backward(i, state):
+        j = count - 1 - i
+        out_ref[j, :, :dv] = state
+        step = wide(coef_ref, 3, j, reps) * got_ref[j, :, dv:]
+        return wide(coef_ref, 2, j, reps) * state + step
+
+    lax.fori_loop(0, count, backward, jnp.zeros((8, dv), F32), unroll=8)
+
+
+def inner_kernel(
+    heads, scale, mem_ref, cols_ref, small_ref, gt_ref, gc_ref, wl_ref, pc_ref, gv_ref,
+    q_ref, k_ref, g_ref,
+    gq_ref, gvalue_ref, gk_ref, row_ref, cold_ref,
 ):
     n = q_ref.shape[0]
     dk = q_ref.shape[1] // heads
     dv = g_ref.shape[1] // heads
     gt, gc = gt_ref[...], gc_ref[...]
     inside, cross, inverse, qn = cols_ref[0], cols_ref[1], cols_ref[2], cols_ref[5]
-    key_scale = jnp.exp(kl_ref[...] + small_ref[heads : heads + 1])
     row_part = scale * cross * (inverse * gc + gt * qn)
-    column_cross = jnp.zeros((n, 128), F32)
-    through = jnp.zeros((1, 128), F32)
     for h in range(heads):
         ks, vs = slice(dk * h, dk * (h + 1)), slice(dv * h, dv * (h + 1))
         one = slice(h, h + 1)
-        q, k, v, g = q_ref[:, ks], k_ref[:, ks], v_ref[:, vs], g_ref[:, vs]
-        slab = slice(dk // 8 * h, dk // 8 * (h + 1))
-        memory = mem_ref[slab, 0:8, :].reshape(dk, dv)
-        following = mem_ref[slab, 8:16, :].reshape(dk, dv)
-        follow_high, follow_low = split(following)
+        q, k, g = q_ref[:, ks], k_ref[:, ks], g_ref[:, vs]
+        memory = mem_ref[dk // 8 * h : dk // 8 * (h + 1)].reshape(dk, dv)
         factor = inside[:, one] * (inverse[:, one] * gv_ref[h] + gt[:, one])
         pair_grad = factor * pc_ref[h]
         cold_ref[one, :] = scale * jnp.sum(pair_grad, axis=0, keepdims=True)
@@ -310,42 +413,80 @@
             inverse[:, one] * dot_right(g, memory, 1, 1) + gt[:, one] * small_ref[one]
         )
         gq_ref[:, ks] = (scale * grad_query).astype(BF16)
-        grad_key = dot(score_high, q, 0, 0) + dot(score_low, q, 0, 0)
-        carried = dot(v, follow_high, 1, 1) + dot(v, follow_low, 1, 1)
-        gk_ref[:, ks] = scale * grad_key + key_scale[:, one] * carried
-        carried = dot(k, follow_high, 1, 0) + dot(k, follow_low, 1, 0)
-        along = jnp.sum(v.astype(F32) * carried, axis=1, keepdims=True)
-        column_cross = put(column_cross, key_scale[:, one] * along, h)
+        gk_ref[:, ks] = scale * (dot(score_high, q, 0, 0) + dot(score_low, q, 0, 0))
         coupled = pc_ref[h] * (scale * inside[:, one] * inverse[:, one])
-        grad_value = dot_left(coupled, g, 0, 0) + key_scale[:, one] * carried
-        gvalue_ref[:, vs] = grad_value.astype(BF16)
-        product = jnp.sum(jnp.sum(memory * following, axis=0, keepdims=True), axis=1, keepdims=True)
-        through = put(through, product, h)
+        gvalue_ref[:, vs] = dot_left(coupled, g, 0, 0)
     row_ref[...] = row_part
-    cc_ref[...] = column_cross
     cold_ref[heads:, :] = jnp.zeros((8 - heads, n), F32)
-    pass_ref[...] = jnp.broadcast_to(through, pass_ref.shape)
+
+
+def after_kernel(
+    heads, me_ref, got_ref, later_ref, small_ref, dual_ref, pair_ref, tile_ref,
+    give_ref, mine_ref, sum_ref,
+):
+    core = me_ref[0] % 2
+    count, dv = mine_ref.shape[0], dual_ref.shape[2]
+    per_head = count // (heads // 2)
+    vectors = [
+        jnp.sum(later_ref[:, h : h + 1] * got_ref[:, h, dv:], axis=0, keepdims=True)
+        for h in range(heads)
+    ]
+    tile = jnp.concatenate(vectors + [tile_ref[:heads]], axis=0)
+    sum_ref[...] = tile
+    give_ref[count] = jnp.concatenate([tile, jnp.zeros((8, dv - 128), F32)], axis=1)
+
+    def fill(even_ref, odd_ref, odd_own):
+        for i in range(heads // 2):
+            at = core * (heads // 2) + i
+            slab = slice(i * per_head, (i + 1) * per_head)
+            after = got_ref[slab, :, :dv]
+            odd_ref[slab] = after
+            even_ref[slab] = pick(small_ref[8:9], at) * after + pick(small_ref[9:10], at) * odd_own(i)
+
+    @pl.when(core == 0)
+    def _():
+        fill(mine_ref, give_ref, lambda i: pair_ref[i * per_head : (i + 1) * per_head])
+
+    @pl.when(core == 1)
+    def _():
+        fill(give_ref, mine_ref, lambda i: dual_ref[count + i * per_head : count + (i + 1) * per_head])
 
 
 def weights_kernel(
-    heads, got_ref, later_ref, small_ref, kl_ref, rows_ref, row_ref, cc_ref, cold_ref, pass_ref,
-    gk_ref, k_ref, x_ref, gkey_ref, pay_ref,
-):
+    heads, me_ref, mine_ref, pair_ref, sum_ref, mem_ref, small_ref, kl_ref, rows_ref, row_ref, cold_ref,
+    k_ref, v_ref, x_ref,
+    after_ref, vector_ref, carried_ref, pay_ref,
+):
+    core = me_ref[0] % 2
     n = k_ref.shape[0]
     dk = k_ref.shape[1] // heads
+    dv = v_ref.shape[1] // heads
+    count = mine_ref.shape[0]
+    after_ref[pl.ds(core * count, count)] = mine_ref[...]
+    after_ref[pl.ds((1 - core) * count, count)] = pair_ref[:count]
+    mine, other = sum_ref[...], pair_ref[count, :, :128]
     key_scale = jnp.exp(kl_ref[...] + small_ref[heads : heads + 1])
-    later = later_ref[...]
-    column_cross = cc_ref[...]
-    through = pass_ref[:1]
-    for h in range(heads):
-        ks, one = slice(dk * h, dk * (h + 1)), slice(h, h + 1)
-        vector = jnp.sum(later[:, one] * got_ref[:, h, :], axis=0, keepdims=True)
-        k = k_ref[:, ks].astype(F32)
-        along = jnp.sum(k * vector, axis=1, keepdims=True)
-        column_cross = column_cross + put(jnp.zeros((n, 128), F32), key_scale[:, one] * along, h)
-        gkey_ref[:, ks] = (gk_ref[:, ks] + key_scale[:, one] * vector).astype(BF16)
-        product = jnp.sum(small_ref[one] * vector, axis=1, keepdims=True)
-        through = through + put(jnp.zeros((1, 128), F32), product, h)
+    column_cross = jnp.zeros((n, 128), F32)
+    through = jnp.zeros((1, 128), F32)
+    vectors = []
+    for h in range(heads):
+        ks, vs, one = slice(dk * h, dk * (h + 1)), slice(dv * h, dv * (h + 1)), slice(h, h + 1)
+        slab = slice(dk // 8 * h, dk // 8 * (h + 1))
+        odd = mine[one] + other[one]
+        even = small_ref[8:9, one] * odd + small_ref[9:10, one] * other[heads + h : heads + h + 1]
+        vector = jnp.where(core == 0, even, odd)
+        vectors.append(vector)
+        following = after_ref[slab].reshape(dk, dv)
+        carried = dot_right(k_ref[:, ks], following, 1, 0)
+        carried_ref[:, vs] = carried
+        along = jnp.sum(v_ref[:, vs].astype(F32) * carried, axis=1, keepdims=True)
+        along = along + jnp.sum(k_ref[:, ks].astype(F32) * vector, axis=1, keepdims=True)
+        column_cross = put(column_cross, key_scale[:, one] * along, h)
+        product = jnp.sum(mem_ref[slab].reshape(dk, dv) * following, axis=0, keepdims=True)
+        product = jnp.sum(product, axis=1, keepdims=True)
+        product = product + jnp.sum(small_ref[one] * vector, axis=1, keepdims=True)
+        through = put(through, product, h)
+    vector_ref[...] = jnp.concatenate(vectors + [jnp.zeros((8 - heads, 128), F32)], axis=0)
     through = through * small_ref[heads + 1 : heads + 2]
     row = row_ref[...].T[:8]
     crossing = column_cross.T[:8]
@@ -367,6 +508,21 @@
         pay_ref[tiles + c] = result[heads:, 128 * c : 128 * (c + 1)]
 
 
+def finish_kernel(
+    heads, after_ref, vector_ref, carried_ref, small_ref, kl_ref, gk_ref, gvalue_ref, v_ref,
+    gkey_ref, out_ref,
+):
+    dk = gk_ref.shape[1] // heads
+    dv = v_ref.shape[1] // heads
+    key_scale = jnp.exp(kl_ref[...] + small_ref[heads : heads + 1])
+    for h in range(heads):
+        ks, vs, one = slice(dk * h, dk * (h + 1)), slice(dv * h, dv * (h + 1)), slice(h, h + 1)
+        following = after_ref[dk // 8 * h : dk // 8 * (h + 1)].reshape(dk, dv)
+        carried = dot_right(v_ref[:, vs], following, 1, 1) + vector_ref[one]
+        gkey_ref[:, ks] = (gk_ref[:, ks] + key_scale[:, one] * carried).astype(BF16)
+        out_ref[:, vs] = (gvalue_ref[:, vs] + key_scale[:, one] * carried_ref[:, vs]).astype(BF16)
+
+
 def sum_kernel(got_ref, out_ref):
     total = jnp.sum(got_ref[...], axis=0, keepdims=True)
     out_ref[...] = jnp.broadcast_to(total, out_ref.shape)
@@ -386,12 +542,11 @@
         out_shape=shapes,
         in_specs=[SMEM if i in scalars else VMEM for i in range(len(args))],
         out_specs=[VMEM] * len(shapes),
-        compiler_params=pltpu.CompilerParams(vmem_limit_bytes=40 * 1024 * 1024),
     )(*args)
 
 
-def exchange(x, axis):
-    return lax.all_to_all(x, axis, 0, 0)
+def exchange(x, axis, groups=None):
+    return lax.all_to_all(x, axis, 0, 0, axis_index_groups=groups)
 
 
 def local(
@@ -402,53 +557,89 @@
     n = q.shape[0]
     dk, dv = q.shape[1] // heads, v.shape[1] // heads
     scale = dk ** (-0.5)
-    count = lax.axis_size("ctx")
+    devices = lax.axis_size("ctx")
+    count = devices // 2
     me = lax.axis_index("ctx").astype(jnp.int32).reshape(1)
     part = functools.partial
     cols = (n, 128)
-    pay, memory, rows, lc, dc, kl = call(
+    slabs = heads * dk // 8
+    cores = [[2 * i + c for i in range(count)] for c in range(2)]
+
+    def to_pair(a):
+        return lax.ppermute(a, "ctx", [(i, i ^ 1) for i in range(devices)])
+
+    give, memory, tile, rows, lc, dc, kl = call(
         part(gates_kernel, heads),
-        [(count, 8, 128), (count, 8, dv), (16, n), cols, cols, cols],
-        x, w_input.T, w_forget.T, b_input, b_forget, doc_pos, k, v,
-        scalars=(3, 4),
-    )
-    got = exchange(pay, "ctx")
+        [(slabs // 2 + 1, 8, dv), (slabs, 8, dv), (8, 128), (16, n), cols, cols, cols],
+        me, x, w_input.T, w_forget.T, b_input, b_forget, doc_pos, k, v,
+        scalars=(0, 4, 5),
+    )
+    pair_memory = to_pair(give)
+    (pay,) = call(
+        part(first_kernel, heads), [(count, 8, dv + 128)], me, memory, tile, pair_memory, scalars=(0,)
+    )
+    first = exchange(pay, "ctx", cores)
     wl, pc, gv, rm, ls, lg = call(
         part(pairs_kernel, heads),
         [(heads, n, n)] * 3 + [cols] * 3,
         rows, lc, dc, q, k, v, g,
     )
-    pay, coef, later, small, tokens = call(
+    give, dual, coef, later, small, tokens = call(
         part(dual_kernel, heads, scale),
-        [(count, 16, dv), (4, count, 128), (count, 128), (8, 128), (6, n, 128)],
-        me, got, memory, lc, dc, rm, ls, q, g,
+        [(count, 8, dv), (slabs, 8, dv), (4, count, 128), (count, 128), (16, 128), (6, n, 128)],
+        me, first, tile, pair_memory[slabs // 2 :], lc, dc, rm, ls, q, g,
         scalars=(0,),
     )
+    pair_dual = to_pair(give)
+    (pay,) = call(
+        part(second_kernel, heads),
+        [(count, 8, 2 * dv)],
+        me, first, coef, small, dual, pair_dual,
+        scalars=(0,),
+    )
+    second = exchange(pay, "ctx", cores)
+    give, mine = call(
+        part(halves_kernel, heads),
+        [(count, 8, dv)] * 2,
+        me, second, memory, pair_memory, small,
+        scalars=(0,),
+    )
+    pair = to_pair(give)
+    pay, states, tile, gt, gc = call(
+        part(vector_kernel, heads, scale),
+        [(count, 8, dv + 128), (slabs, 8, dv), (8, 128), cols, cols],
+        me, mine, pair, second, coef, tokens, lg, q, g,
+        scalars=(0,),
+    )
+    third = exchange(pay, "ctx", cores)
+    grad_q, gvalue, gk, row, cold = call(
+        part(inner_kernel, heads, scale),
+        [jax.ShapeDtypeStruct(q.shape, BF16), v.shape, k.shape, cols, (8, n)],
+        states, tokens, small, gt, gc, wl, pc, gv, q, k, g,
+    )
+    give, mine, tile = call(
+        part(after_kernel, heads),
+        [(count + 1, 8, dv), (count, 8, dv), (8, 128)],
+        me, third, later, small, dual, pair_dual, tile,
+        scalars=(0,),
+    )
+    pair = to_pair(give)
+    chunks = 2 * x.shape[1] // 128
+    following, vector, carried, pay = call(
+        part(weights_kernel, heads),
+        [(slabs, 8, dv), (8, 128), v.shape, (chunks, heads, 128)],
+        me, mine, pair, tile, states, small, kl, rows, row, cold, k, v, x,
+        scalars=(0,),
+    )
     got = exchange(pay, "ctx")
-    (pay,) = call(scan_kernel, [(count, 16, dv)], got, coef)
-    states = exchange(pay, "ctx")
-    pay, gt, gc = call(
-        part(vector_kernel, heads, scale), [(count, heads, 128), cols, cols], states, tokens, lg, q, g
-    )
-    got = exchange(pay, "ctx")
-    grad_q, grad_v, gk, row, cc, cold, through = call(
-        part(grads_kernel, heads, scale),
-        [
-            jax.ShapeDtypeStruct(q.shape, BF16), jax.ShapeDtypeStruct(v.shape, BF16),
-            k.shape, cols, cols, (8, n), (8, 128),
-        ],
-        states, tokens, small, kl, gt, gc, wl, pc, gv, q, k, v, g,
-    )
-    chunks = 2 * x.shape[1] // 128
-    grad_k, pay = call(
-        part(weights_kernel, heads),
-        [jax.ShapeDtypeStruct(k.shape, BF16), (chunks, heads, 128)],
-        got, later, small, kl, rows, row, cc, cold, through, gk, k, x,
-    )
-    got = exchange(pay, "ctx")
+    grad_k, grad_v = call(
+        part(finish_kernel, heads),
+        [jax.ShapeDtypeStruct(k.shape, BF16), jax.ShapeDtypeStruct(v.shape, BF16)],
+        following, vector, carried, small, kl, gk, gvalue, v,
+    )
     (pay,) = call(sum_kernel, [(lax.axis_size("dp"), heads, 128)], got)
     got = exchange(pay, "dp")
-    (pay,) = call(sum_kernel, [(count, heads, 128)], got)
+    (pay,) = call(sum_kernel, [(devices, heads, 128)], got)
     got = exchange(pay, "ctx")
     first, second = call(place_kernel, [(heads, x.shape[1])] * 2, got)
     return (grad_q[None], grad_k[None], grad_v[None], first.T, second.T)

time: 189 us -> 161 us (0.85)
  blocking collectives: 112 us -> 64.6 us
  Pallas kernels: 14.7 us -> 43.9 us
  local copies, waits for them, and re-layouts: 33.7 us -> 5.5 us
  waiting for transfers between devices: 6.88 us -> 20.4 us
  starting transfers between devices: 19.6 us -> 25.1 us
    all_to_all x5 -> x4, blocking collectives: 112 us -> 64.6 us  [exchange(): return lax.all_to_all(x, axis, 0, 0, axis_index_groups=groups)]
    unnamed x90 -> x12, local copies, waits for them, and re-layouts: 33.7 us -> 4.21 us
    pallas_call x10 -> x14, Pallas kernels: 14.7 us -> 43.9 us  [call(): pl.pallas_call(body, out_shape=shapes, in_specs=[SMEM if i in scalars els...]
    ppermute x0 -> x4, starting transfers between devices: none -> 9.92 us  [to_pair(): return lax.ppermute(a, 'ctx', [(i, i ^ 1) for i in range(devices)])]
    all_to_all x2, waiting for transfers between devices: 6.88 us -> 16.2 us  [exchange(): return lax.all_to_all(x, axis, 0, 0, axis_index_groups=groups)]
    all_to_all x2, starting transfers between devices: 19.6 us -> 15.2 us  [exchange(): return lax.all_to_all(x, axis, 0, 0, axis_index_groups=groups)]
    ppermute x0 -> x4, waiting for transfers between devices: none -> 4.13 us  [to_pair(): return lax.ppermute(a, 'ctx', [(i, i ^ 1) for i in range(devices)])]
  transfers between devices with their start and end apart: 2 -> 6, of which waited for: 1 -> 5; matrix products, arithmetic and copies ran while one was open for 0% -> 1% of each run, Pallas kernels for 3% -> 9%
where the time goes in v2:
time: 161 us; the launch traced here: 160 us
  blocking collectives  64.6 us (40%)
  Pallas kernels  43.9 us (27%)
  starting transfers between devices  25.1 us (16%)
  waiting for transfers between devices  20.4 us (13%)
  local copies, waits for them, and re-layouts  5.5 us (3%)
    all_to_all x4, blocking collectives, exchange(): return lax.all_to_all(x, axis, 0, 0, axis_index_groups=groups)  64.6 us
    pallas_call x14, Pallas kernels, call(): pl.pallas_call(body, out_shape=shapes, in_specs=[SMEM if i in scalars els...  43.9 us
    all_to_all x2, waiting for transfers between devices, exchange(): return lax.all_to_all(x, axis, 0, 0, axis_index_groups=groups)  16.2 us
    all_to_all x2, starting transfers between devices, exchange(): return lax.all_to_all(x, axis, 0, 0, axis_index_groups=groups)  15.2 us
    ppermute x4, starting transfers between devices, to_pair(): return lax.ppermute(a, 'ctx', [(i, i ^ 1) for i in range(devices)])  9.92 us
    unnamed x12, local copies, waits for them, and re-layouts  4.21 us
    ppermute x4, waiting for transfers between devices, to_pair(): return lax.ppermute(a, 'ctx', [(i, i ^ 1) for i in range(devices)])  4.13 us
  transfers between devices with their start and end apart: 6, of which 5 were waited for; matrix products, arithmetic and copies ran while one was open for 1% of the time, Pallas kernels for 9%

profile of v2, /device:TPU:1, one launch (start us, length us, event | category | flops | bytes accessed | tf_op | source)
XLA Modules:
  0.0 160.1 jit_solution(6237474583627823316)
XLA Ops:
  0.6 4.4 %shard_map.137 = (f32[33,8,256]{2,1,0:T(8,128)}, f32[64,8,256]{2,1,0:T(8,128)}, f32[8,128]{1,0:T(8,128)}, f32[16,256]{1,0:T(8,128)}, f32[256,128]{1,0:T(8,128)}, /*index=5*/f32[256,128]{1,0:T(8,128)}, f32[256,128]{1,0:T(8,128)}) custom-call(s32[1]{0:T(128)} %bitcast.me_ref, bf16[256,4096]{1,0:T(8,128)(2,1)} %bitcast.13, bf16[4,4096]{1,0:T(4,128)(2,1)} %bitcast.31, ...), custom_call_target="tpu_custom_call" | custom-call | tf_op jit(solution)/shard_map/pallas_call | solution.py:540
  5.1 3.3 %collective-permute-start = (f32[33,8,256]{2,1,0:T(8,128)}, f32[33,8,256]{2,1,0:T(8,128)S(1)}, u32[]{:S(2)}, u32[]{:S(2)}) collective-permute-start(f32[33,8,256]{2,1,0:T(8,128)} %get-tuple-element.49), channel_id=1, source_target_pairs={{0,4},{4,0},{8,12},{12,8},{16,20},{20,16},{24,28},{28,24},{32,36},... | collective-permute-start | bytes 811016 | tf_op jit(solution)/shard_map/ppermute | solution.py:569
  8.4 1.4 collective-permute-done.got_ref.pair_ref
  9.8 0.7 copy-done.1
  10.5 2.0 %shard_map.138 = f32[32,8,384]{2,1,0:T(8,128)} custom-call(s32[1]{0:T(128)} %bitcast.me_ref, f32[64,8,256]{2,1,0:T(8,128)} %get-tuple-element.47.mem_ref, f32[8,128]{1,0:T(8,128)} %get-tuple-element.48.tile_ref, f32[33,8,256]{2,1,0:T(8,128)} %copy-done.1), custom_call_target="tpu_custom_call" | custom-call | tf_op jit(solution)/shard_map/pallas_call | solution.py:540
  12.5 9.3 %all-to-all-start = ((f32[32,8,384]{2,1,0:T(8,128)}), f32[32,8,384]{2,1,0:T(8,128)S(1)}, u32[]{:S(2)}, u32[]{:S(2)}) async-start(f32[32,8,384]{2,1,0:T(8,128)} %shard_map.138), calls=%async_computation | async-start | bytes 786432 | tf_op jit(solution)/shard_map/all_to_all | solution.py:549
  21.8 4.4 %shard_map.139 = (f32[4,256,256]{2,1,0:T(8,128)}, f32[4,256,256]{2,1,0:T(8,128)}, f32[4,256,256]{2,1,0:T(8,128)}, f32[256,128]{1,0:T(8,128)}, f32[256,128]{1,0:T(8,128)}, /*index=5*/f32[256,128]{1,0:T(8,128)}) custom-call(f32[16,256]{1,0:T(8,128)} %get-tuple-element.52.rows_ref, f32[256,128]{1,0:T(8,128)} %get-tuple-element.50.lc_ref, ...), custom_call_target="tpu_custom_call" | custom-call | tf_op jit(solution)/shard_map/pallas_call | solution.py:540
  26.2 1.3 slice.4.pair_ref
  27.5 8.2 %all-to-all-done.got_ref = f32[32,8,384]{2,1,0:T(8,128)S(1)} async-done(((f32[32,8,384]{2,1,0:T(8,128)}), f32[32,8,384]{2,1,0:T(8,128)S(1)}, u32[]{:S(2)}, u32[]{:S(2)}) %all-to-all-start) | async-done | bytes 393248 | tf_op jit(solution)/shard_map/all_to_all | solution.py:549
  35.7 0.8 copy-done
  36.5 3.6 %shard_map.140 = (f32[32,8,256]{2,1,0:T(8,128)}, f32[64,8,256]{2,1,0:T(8,128)}, f32[4,32,128]{2,1,0:T(8,128)}, f32[32,128]{1,0:T(8,128)}, f32[16,128]{1,0:T(8,128)}, /*index=5*/f32[6,256,128]{2,1,0:T(8,128)}) custom-call(s32[1]{0:T(128)} %bitcast.me_ref, f32[32,8,384]{2,1,0:T(8,128)} %copy-done, f32[8,128]{1,0:T(8,128)} %get-tuple-element.48.tile_ref, ...), custom_call_target="tpu_custom_call" | custom-call | tf_op jit(solution)/shard_map/pallas_call | solution.py:540
  40.0 2.4 %collective-permute-start.1 = (f32[32,8,256]{2,1,0:T(8,128)}, f32[32,8,256]{2,1,0:T(8,128)S(1)}, u32[]{:S(2)}, u32[]{:S(2)}) collective-permute-start(f32[32,8,256]{2,1,0:T(8,128)} %get-tuple-element.58), channel_id=1, source_target_pairs={{0,4},{4,0},{8,12},{12,8},{16,20},{20,16},{24,28},{28,24},{32,36},... | collective-permute-start | bytes 786440 | tf_op jit(solution)/shard_map/ppermute | solution.py:569
  42.4 1.4 collective-permute-done.1.pair_ref
  44.5 2.3 %shard_map.141 = f32[32,8,512]{2,1,0:T(8,128)} custom-call(s32[1]{0:T(128)} %bitcast.me_ref, f32[32,8,384]{2,1,0:T(8,128)} %copy-done, f32[4,32,128]{2,1,0:T(8,128)} %get-tuple-element.55.coef_ref, f32[16,128]{1,0:T(8,128)} %get-tuple-element.56.small_ref, f32[64,8,256]{2,1,0:T(8,128)} %get-tuple-element.57.dual_ref, f32[32,8,256]{2,1,0:T(8,128)} %copy-done.2), custom_call_target="tpu_custom_call" | custom-call | tf_op jit(solution)/shard_map/pallas_call | solution.py:540
  46.8 21.2 %all_to_all.30.got_ref = f32[32,8,512]{2,1,0:T(8,128)} all-to-all(f32[32,8,512]{2,1,0:T(8,128)} %shard_map.141), channel_id=1, replica_groups={{0,8,16,24,32,40,48,56,64,72,80,88,96,104,112,120,128,136,144,152,160,1..., dimensions={0} | all-to-all | bytes 1048576 | tf_op jit(solution)/shard_map/all_to_all | solution.py:549
  68.0 2.2 %shard_map.142 = (f32[32,8,256]{2,1,0:T(8,128)}, f32[32,8,256]{2,1,0:T(8,128)}) custom-call(s32[1]{0:T(128)} %bitcast.me_ref, f32[32,8,512]{2,1,0:T(8,128)} %all_to_all.30.got_ref, f32[64,8,256]{2,1,0:T(8,128)} %get-tuple-element.47.mem_ref, f32[33,8,256]{2,1,0:T(8,128)} %copy-done.1, f32[16,128]{1,0:T(8,128)} %get-tuple-element.56.small_ref), custom_call_target="tpu_custom_call" | custom-call | tf_op jit(solution)/shard_map/pallas_call | solution.py:540
  70.2 2.0 %collective-permute-start.2 = (f32[32,8,256]{2,1,0:T(8,128)}, f32[32,8,256]{2,1,0:T(8,128)S(1)}, u32[]{:S(2)}, u32[]{:S(2)}) collective-permute-start(f32[32,8,256]{2,1,0:T(8,128)} %get-tuple-element.60), channel_id=1, source_target_pairs={{0,4},{4,0},{8,12},{12,8},{16,20},{20,16},{24,28},{28,24},{32,36},... | collective-permute-start | bytes 786440 | tf_op jit(solution)/shard_map/ppermute | solution.py:569
  72.2 1.4 collective-permute-done.2.pair_ref
  74.2 3.7 %shard_map.143 = (f32[32,8,384]{2,1,0:T(8,128)}, f32[64,8,256]{2,1,0:T(8,128)}, f32[8,128]{1,0:T(8,128)}, f32[256,128]{1,0:T(8,128)}, f32[256,128]{1,0:T(8,128)}) custom-call(s32[1]{0:T(128)} %bitcast.me_ref, f32[32,8,256]{2,1,0:T(8,128)} %get-tuple-element.59.mine_ref, f32[32,8,256]{2,1,0:T(8,128)} %copy-done.5, f32[32,8,512]{2,1,0:T(8,128)} %all_to_all.30.got_ref, ...), custom_call_target="tpu_custom_call" | custom-call | tf_op jit(solution)/shard_map/pallas_call | solution.py:540
  78.0 18.6 %all_to_all.31.got_ref = f32[32,8,384]{2,1,0:T(8,128)} all-to-all(f32[32,8,384]{2,1,0:T(8,128)} %get-tuple-element.70), channel_id=1, replica_groups={{0,8,16,24,32,40,48,56,64,72,80,88,96,104,112,120,128,136,144,152,160,1..., dimensions={0} | all-to-all | bytes 786432 | tf_op jit(solution)/shard_map/all_to_all | solution.py:549
  96.5 2.3 %shard_map.145 = (f32[33,8,256]{2,1,0:T(8,128)}, f32[32,8,256]{2,1,0:T(8,128)}, f32[8,128]{1,0:T(8,128)}) custom-call(s32[1]{0:T(128)} %bitcast.me_ref, f32[32,8,384]{2,1,0:T(8,128)} %all_to_all.31.got_ref, f32[32,128]{1,0:T(8,128)} %get-tuple-element.71.later_ref, f32[16,128]{1,0:T(8,128)} %get-tuple-element.56.small_ref, ...), custom_call_target="tpu_custom_call" | custom-call | tf_op jit(solution)/shard_map/pallas_call | solution.py:540
  98.8 2.2 %collective-permute-start.3 = (f32[33,8,256]{2,1,0:T(8,128)}, f32[33,8,256]{2,1,0:T(8,128)S(1)}, u32[]{:S(2)}, u32[]{:S(2)}) collective-permute-start(f32[33,8,256]{2,1,0:T(8,128)} %get-tuple-element.74), channel_id=1, source_target_pairs={{0,4},{4,0},{8,12},{12,8},{16,20},{20,16},{24,28},{28,24},{32,36},... | collective-permute-start | bytes 811016 | tf_op jit(solution)/shard_map/ppermute | solution.py:569
  101.1 6.1 %shard_map.144 = (bf16[256,512]{1,0:T(8,128)(2,1)}, f32[256,1024]{1,0:T(8,128)}, f32[256,512]{1,0:T(8,128)}, f32[256,128]{1,0:T(8,128)}, f32[8,256]{1,0:T(8,128)}) custom-call(f32[64,8,256]{2,1,0:T(8,128)} %get-tuple-element.63.mem_ref, f32[6,256,128]{2,1,0:T(8,128)} %get-tuple-element.61.cols_ref, f32[16,128]{1,0:T(8,128)} %get-tuple-element.56.small_ref, ...), custom_call_target="tpu_custom_call" | custom-call | tf_op jit(solution)/shard_map/pallas_call | solution.py:540
  107.8 5.1 %shard_map.146 = (f32[64,8,256]{2,1,0:T(8,128)}, f32[8,128]{1,0:T(8,128)}, f32[256,1024]{1,0:T(8,128)}, f32[64,4,128]{2,1,0:T(4,128)}) custom-call(s32[1]{0:T(128)} %bitcast.me_ref, f32[32,8,256]{2,1,0:T(8,128)} %get-tuple-element.73.mine_ref, f32[33,8,256]{2,1,0:T(8,128)} %copy-done.4, f32[8,128]{1,0:T(8,128)} %get-tuple-element.75.sum_ref, ...), custom_call_target="tpu_custom_call" | custom-call | tf_op jit(solution)/shard_map/pallas_call | solution.py:540
  112.9 16.3 %all_to_all.32.got_ref = f32[64,4,128]{2,1,0:T(4,128)} all-to-all(f32[64,4,128]{2,1,0:T(4,128)} %get-tuple-element.86), channel_id=1, replica_groups=mesh['ctx'=64,'dp'=4] {'ctx'}, dimensions={0} | all-to-all | bytes 262144 | tf_op jit(solution)/shard_map/all_to_all | solution.py:549
  129.2 1.6 shard_map.148
  130.8 8.5 %all_to_all.33.got_ref = f32[4,4,128]{2,1,0:T(4,128)} all-to-all(f32[4,4,128]{2,1,0:T(4,128)} %shard_map.148), channel_id=1, replica_groups=mesh['ctx'=64,'dp'=4] {'dp'}, dimensions={0} | all-to-all | bytes 16384 | tf_op jit(solution)/shard_map/all_to_all | solution.py:549
  139.3 1.4 shard_map.149
  140.6 5.9 %all-to-all-start.5 = ((f32[64,4,128]{2,1,0:T(4,128)}), f32[64,4,128]{2,1,0:T(4,128)S(1)}, u32[]{:S(2)}, u32[]{:S(2)}) async-start(f32[64,4,128]{2,1,0:T(4,128)} %shard_map.149), calls=%async_computation.5 | async-start | bytes 262144 | tf_op jit(solution)/shard_map/all_to_all | solution.py:549
  146.5 3.3 %shard_map.147 = (bf16[256,512]{1,0:T(8,128)(2,1)}, bf16[256,1024]{1,0:T(8,128)(2,1)}) custom-call(f32[64,8,256]{2,1,0:T(8,128)} %get-tuple-element.79.after_ref, f32[8,128]{1,0:T(8,128)} %get-tuple-element.80.vector_ref, f32[256,1024]{1,0:T(8,128)} %get-tuple-element.81.carried_ref, f32[16,128]{1,0:T(8,128)} %get-tuple-element.56.small_ref, ...), custom_call_target="tpu_custom_call" | custom-call | tf_op jit(solution)/shard_map/pallas_call | solution.py:540
  149.8 8.1 %all-to-all-done.5.got_ref = f32[64,4,128]{2,1,0:T(4,128)S(1)} async-done(((f32[64,4,128]{2,1,0:T(4,128)}), f32[64,4,128]{2,1,0:T(4,128)S(1)}, u32[]{:S(2)}, u32[]{:S(2)}) %all-to-all-start.5) | async-done | bytes 131104 | tf_op jit(solution)/shard_map/all_to_all | solution.py:549
  158.5 1.6 shard_map.150
  (11 shorter events, 2.8 us)
Async XLA Ops:
  5.1 4.7 %collective-permute-start = (f32[33,8,256]{2,1,0:T(8,128)}, f32[33,8,256]{2,1,0:T(8,128)S(1)}, u32[]{:S(2)}, u32[]{:S(2)}) collective-permute-start(f32[33,8,256]{2,1,0:T(8,128)} %get-tuple-element.49), channel_id=1, source_target_pairs={{0,4},{4,0},{8,12},{12,8},{16,20},{20,16},{24,28},{28,24},{32,36},... | collective-permute-start | bytes 811016 | tf_op jit(solution)/shard_map/ppermute | solution.py:569
  9.8 0.7 copy-start.1
  12.5 23.2 %all-to-all-start = ((f32[32,8,384]{2,1,0:T(8,128)}), f32[32,8,384]{2,1,0:T(8,128)S(1)}, u32[]{:S(2)}, u32[]{:S(2)}) async-start(f32[32,8,384]{2,1,0:T(8,128)} %shard_map.138), calls=%async_computation | async-start | bytes 786432 | tf_op jit(solution)/shard_map/all_to_all | solution.py:549
  35.7 0.8 copy-start
  40.0 3.7 %collective-permute-start.1 = (f32[32,8,256]{2,1,0:T(8,128)}, f32[32,8,256]{2,1,0:T(8,128)S(1)}, u32[]{:S(2)}, u32[]{:S(2)}) collective-permute-start(f32[32,8,256]{2,1,0:T(8,128)} %get-tuple-element.58), channel_id=1, source_target_pairs={{0,4},{4,0},{8,12},{12,8},{16,20},{20,16},{24,28},{28,24},{32,36},... | collective-permute-start | bytes 786440 | tf_op jit(solution)/shard_map/ppermute | solution.py:569
  43.8 0.7 copy-start.2
  70.2 3.4 %collective-permute-start.2 = (f32[32,8,256]{2,1,0:T(8,128)}, f32[32,8,256]{2,1,0:T(8,128)S(1)}, u32[]{:S(2)}, u32[]{:S(2)}) collective-permute-start(f32[32,8,256]{2,1,0:T(8,128)} %get-tuple-element.60), channel_id=1, source_target_pairs={{0,4},{4,0},{8,12},{12,8},{16,20},{20,16},{24,28},{28,24},{32,36},... | collective-permute-start | bytes 786440 | tf_op jit(solution)/shard_map/ppermute | solution.py:569
  73.5 0.7 copy-start.5
  98.8 8.3 %collective-permute-start.3 = (f32[33,8,256]{2,1,0:T(8,128)}, f32[33,8,256]{2,1,0:T(8,128)S(1)}, u32[]{:S(2)}, u32[]{:S(2)}) collective-permute-start(f32[33,8,256]{2,1,0:T(8,128)} %get-tuple-element.74), channel_id=1, source_target_pairs={{0,4},{4,0},{8,12},{12,8},{16,20},{20,16},{24,28},{28,24},{32,36},... | collective-permute-start | bytes 811016 | tf_op jit(solution)/shard_map/ppermute | solution.py:569
  107.1 0.7 copy-start.4
  140.6 17.2 %all-to-all-start.5 = ((f32[64,4,128]{2,1,0:T(4,128)}), f32[64,4,128]{2,1,0:T(4,128)S(1)}, u32[]{:S(2)}, u32[]{:S(2)}) async-start(f32[64,4,128]{2,1,0:T(4,128)} %shard_map.149), calls=%async_computation.5 | async-start | bytes 262144 | tf_op jit(solution)/shard_map/all_to_all | solution.py:549
  157.9 0.7 copy-start.3

commit v3 on v2

--- a/solution.py
+++ b/solution.py
@@ -11,8 +11,6 @@
 BIG = 1e30
 F32 = jnp.float32
 BF16 = jnp.bfloat16
-VMEM = pl.BlockSpec(memory_space=pltpu.VMEM)
-SMEM = pl.BlockSpec(memory_space=pltpu.SMEM)
 
 
 def dot(a, b, ca, cb):
@@ -60,7 +58,7 @@
 
 def gates_kernel(
     heads, me_ref, x_ref, wi_ref, wf_ref, bi_ref, bf_ref, pos_ref, k_ref, v_ref,
-    give_ref, mem_ref, tile_ref, rows_ref, lc_ref, dc_ref, kl_ref,
+    give_ref, mem_ref, tile_ref, rows_ref, cols_ref,
 ):
     core = me_ref[0] % 2
     n = x_ref.shape[0]
@@ -85,11 +83,11 @@
     ig = column_of(in_gate)
     lc = column_of(lc_row)
     dc = jnp.broadcast_to(dc_row, (128, n)).T
-    lc_ref[...] = lc
-    dc_ref[...] = dc
     total, last = lc[n - 1 :], dc[n - 1 :]
     key_log = jnp.where(dc == last, total - lc + ig, NEG)
-    kl_ref[...] = key_log
+    cols_ref[...] = pack([lc, key_log, dc], heads)
+    rows_ref.send()
+    cols_ref.send()
     own_max = jnp.max(key_log, axis=0, keepdims=True)
     weight = jnp.exp(key_log - own_max)
     vectors = []
@@ -110,7 +108,7 @@
     give_ref[half] = jnp.concatenate([tile, jnp.zeros((8, dv - 128), F32)], axis=1)
 
 
-def first_kernel(heads, me_ref, mem_ref, tile_ref, got_ref, out_ref):
+def first_kernel(heads, me_ref, mem_ref, tile_ref, got_ref, out_ref, even_ref, even_tile_ref):
     core = me_ref[0] % 2
     half, dv = out_ref.shape[0], mem_ref.shape[2]
     mine, other = tile_ref[...], got_ref[half, :, :128]
@@ -133,18 +131,22 @@
         at = core * (heads // 2) + i
         slab = slice(i * per_head, (i + 1) * per_head)
         own = mem_ref[pl.ds(core * half + i * per_head, per_head)]
-        out_ref[slab, :, :dv] = pick(weight_mine, at) * own + pick(weight_other, at) * got_ref[slab]
+        other = got_ref[slab]
+        out_ref[slab, :, :dv] = pick(weight_mine, at) * own + pick(weight_other, at) * other
+        even_ref[slab] = jnp.where(core == 0, own, other)
+    even_tile_ref[...] = even
 
 
 def pairs_kernel(
-    heads, rows_ref, lc_ref, dc_ref, q_ref, k_ref, v_ref, g_ref,
-    wl_ref, pc_ref, gv_ref, rm_ref, ls_ref, lg_ref,
+    heads, rows_ref, cols_ref, q_ref, k_ref, v_ref, g_ref,
+    wl_ref, pc_ref, gv_ref, sums_ref,
 ):
     n = q_ref.shape[0]
     dk = k_ref.shape[1] // heads
     dv = v_ref.shape[1] // heads
-    lc, dc = lc_ref[...], dc_ref[...]
-    mask = (iota((n, n), 0) >= iota((n, n), 1)) & (dc[:, :1] == rows_ref[3 * heads : 3 * heads + 1])
+    lc = cols_ref[...]
+    dc = lc[:, 2 * heads : 2 * heads + 1]
+    mask = (iota((n, n), 0) >= iota((n, n), 1)) & (dc == rows_ref[3 * heads : 3 * heads + 1])
     rm = jnp.zeros((n, 128), F32)
     ls, lg = rm, rm
     for h in range(heads):
@@ -161,9 +163,7 @@
         rm = put(rm, row_max, h)
         ls = put(ls, jnp.sum(coupled, axis=1, keepdims=True), h)
         lg = put(lg, jnp.sum(coupled * grad_pair, axis=1, keepdims=True), h)
-    rm_ref[...] = rm
-    ls_ref[...] = ls
-    lg_ref[...] = lg
+    sums_ref[...] = pack([rm, ls, lg], heads)
 
 
 def shift_down(x, d, fill):
@@ -176,8 +176,8 @@
 
 
 def dual_kernel(
-    heads, scale, me_ref, got_ref, tile_ref, pair_ref, lc_ref, dc_ref, rm_ref, ls_ref, q_ref, g_ref,
-    give_ref, dual_ref, coef_ref, later_ref, small_ref, cols_ref,
+    heads, scale, me_ref, got_ref, tile_ref, cols_ref, sums_ref, q_ref, g_ref,
+    give_ref, dual_ref, coef_ref, now_ref, coef_later_ref, later_ref, small_ref, tokens_ref,
 ):
     count = got_ref.shape[0]
     n = q_ref.shape[0]
@@ -219,7 +219,8 @@
     )
     for i, c in enumerate(coefs):
         mine = jnp.sum(jnp.where(lane == my_head, c, 0.0), axis=1, keepdims=True)
-        coef_ref[i] = jnp.broadcast_to(mine, c.shape)
+        (coef_ref if i < 2 else coef_later_ref)[i % 2] = jnp.broadcast_to(mine, c.shape)
+    coef_later_ref.send()
 
     def here(x):
         return jnp.sum(jnp.where(row == chip, x, 0.0), axis=0, keepdims=True)
@@ -242,14 +243,15 @@
     later_ref[...] = jnp.where(
         row > chip, jnp.exp(jnp.minimum(source + between - here(later_odd), 0.0)), 0.0
     )
-    even_tile = jnp.where(core == 0, tile_ref[...], pair_ref[0, :, :128])
+    later_ref.send()
+    even_tile = tile_ref[...]
     vectors = []
     for h in range(heads):
         one = slice(h, h + 1)
         vector = jnp.sum(weight[:, one] * got_ref[:, h, dv:], axis=0, keepdims=True)
         second = keep[:, one] * vector + add[:, one] * even_tile[one]
         vectors.append(jnp.where(core == 0, vector, second))
-    small_ref[...] = jnp.concatenate(
+    small = jnp.concatenate(
         vectors
         + [
             later_me,
@@ -265,41 +267,52 @@
         axis=0,
     )
 
-    lc, open_query = lc_ref[...], dc_ref[...] < 0.5
+    small_ref[...] = small
+    small_ref.send()
+    now_ref[...] = small
+    lc = cols_ref[...]
+    open_query = lc[:, 2 * heads : 2 * heads + 1] < 0.5
+    sums = sums_ref[...]
     cross_log = jnp.where(open_query, lc + in_me, NEG)
-    row_max = jnp.maximum(rm_ref[...], cross_log)
-    inside = jnp.exp(rm_ref[...] - row_max)
+    row_max = jnp.maximum(sums, cross_log)
+    inside = jnp.exp(sums - row_max)
     cross = jnp.exp(cross_log - row_max)
     qn = jnp.zeros((n, 128), F32)
     for h in range(heads):
         along = q_ref[:, dk * h : dk * (h + 1)].astype(F32) * vectors[h]
         qn = put(qn, jnp.sum(along, axis=1, keepdims=True), h)
-    sums = scale * (ls_ref[...] * inside + cross * qn)
+    sums = scale * (unpack(sums, 1, heads) * inside + cross * qn)
     floor = jnp.exp(-row_max)
     size = jnp.abs(sums)
     inverse = 1.0 / jnp.maximum(size, floor)
     active = jnp.where(size > floor, jnp.where(sums > 0.0, 1.0, -1.0), 0.0)
     query_weight = jnp.where(open_query, jnp.exp(jnp.minimum(lc - row_max - dual_me, 0.0)), 0.0)
-    cols_ref[0] = inside
-    cols_ref[1] = cross
-    cols_ref[2] = inverse
-    cols_ref[3] = active
-    cols_ref[4] = query_weight
-    cols_ref[5] = qn
+    tokens_ref[...] = pack([inside, cross, inverse, active, query_weight, qn], heads)
+    tokens_ref.send()
     grad_weight = query_weight * inverse * scale
+    half = give_ref.shape[0]
+    per_head = dk // 8
     for h in range(heads):
         weighted = g_ref[:, dv * h : dv * (h + 1)].astype(F32) * grad_weight[:, h : h + 1]
-        memory = dot_right(q_ref[:, dk * h : dk * (h + 1)], weighted, 0, 0)
-        dual_ref[dk // 8 * h : dk // 8 * (h + 1)] = memory.reshape(dk // 8, 8, dv)
-    half = give_ref.shape[0]
-    give_ref[...] = dual_ref[pl.ds((1 - core) * half, half)]
+        memory = dot_right(q_ref[:, dk * h : dk * (h + 1)], weighted, 0, 0).reshape(per_head, 8, dv)
+        slab = slice(per_head * h % half, per_head * h % half + per_head)
+
+        @pl.when(core == h // (heads // 2))
+        def _():
+            dual_ref[slab] = memory
+
+        @pl.when(core != h // (heads // 2))
+        def _():
+            give_ref[slab] = memory
 
 
 def wide(coef_ref, i, j, reps):
     return jnp.concatenate([coef_ref[i, pl.ds(j, 1), :]] * reps, axis=1)
 
 
-def second_kernel(heads, me_ref, got_ref, coef_ref, small_ref, dual_ref, pair_ref, out_ref):
+def second_kernel(
+    heads, me_ref, got_ref, coef_ref, small_ref, dual_ref, pair_ref, out_ref, odd_ref
+):
     core = me_ref[0] % 2
     count, dv = got_ref.shape[0], dual_ref.shape[2]
     reps = dv // 128
@@ -309,7 +322,6 @@
         step = wide(coef_ref, 1, j, reps) * got_ref[j, :, :dv]
         return wide(coef_ref, 0, j, reps) * state + step
 
-    lax.fori_loop(0, count, forward, jnp.zeros((8, dv), F32), unroll=8)
     even, odd = small_ref[10:11], small_ref[11:12]
     weight_mine = jnp.where(core == 0, even, odd)
     weight_other = jnp.where(core == 0, odd, even)
@@ -317,35 +329,39 @@
     for i in range(heads // 2):
         at = core * (heads // 2) + i
         slab = slice(i * per_head, (i + 1) * per_head)
-        own = dual_ref[pl.ds(core * count + i * per_head, per_head)]
-        out_ref[slab, :, dv:] = pick(weight_mine, at) * own + pick(weight_other, at) * pair_ref[slab]
-
-
-def halves_kernel(heads, me_ref, got_ref, mem_ref, pair_ref, small_ref, give_ref, mine_ref):
+        own, other = dual_ref[slab], pair_ref[slab]
+        out_ref[slab, :, dv:] = pick(weight_mine, at) * own + pick(weight_other, at) * other
+        odd_ref[slab] = jnp.where(core == 0, other, own)
+    odd_ref.send()
+    lax.fori_loop(0, count, forward, jnp.zeros((8, dv), F32), unroll=8)
+
+
+def halves_kernel(heads, me_ref, got_ref, even_ref, small_ref, give_ref, mine_ref):
     core = me_ref[0] % 2
-    count, dv = give_ref.shape[0], mem_ref.shape[2]
+    count, dv = give_ref.shape[0], give_ref.shape[2]
     per_head = count // (heads // 2)
-
-    def fill(even_ref, odd_ref, even_own):
+    even, small = even_ref.ready(), small_ref[...]
+
+    def fill(to_even_ref, to_odd_ref):
         for i in range(heads // 2):
             at = core * (heads // 2) + i
             slab = slice(i * per_head, (i + 1) * per_head)
             before = got_ref[slab, :, :dv]
-            even_ref[slab] = before
-            odd_ref[slab] = pick(small_ref[6:7], at) * before + pick(small_ref[7:8], at) * even_own(slab)
+            to_even_ref[slab] = before
+            to_odd_ref[slab] = pick(small[6:7], at) * before + pick(small[7:8], at) * even[slab]
 
     @pl.when(core == 0)
     def _():
-        fill(mine_ref, give_ref, lambda slab: mem_ref[slab])
+        fill(mine_ref, give_ref)
 
     @pl.when(core == 1)
     def _():
-        fill(give_ref, mine_ref, lambda slab: pair_ref[slab])
+        fill(give_ref, mine_ref)
 
 
 def vector_kernel(
-    heads, scale, me_ref, mine_ref, pair_ref, got_ref, coef_ref, cols_ref, lg_ref, q_ref, g_ref,
-    out_ref, mem_ref, tile_ref, gt_ref, gc_ref,
+    heads, scale, me_ref, mine_ref, pair_ref, got_ref, coef_ref, cols_ref, sums_ref, q_ref, g_ref,
+    out_ref, mem_ref, tile_ref, gt_ref,
 ):
     core = me_ref[0] % 2
     n = q_ref.shape[0]
@@ -355,17 +371,19 @@
     reps = dv // 128
     mem_ref[pl.ds(core * count, count)] = mine_ref[...]
     mem_ref[pl.ds((1 - core) * count, count)] = pair_ref[...]
+    mem_ref.send()
     gc = jnp.zeros((n, 128), F32)
     for h in range(heads):
         memory = mem_ref[dk // 8 * h : dk // 8 * (h + 1)].reshape(dk, dv)
         crossing = dot_right(q_ref[:, dk * h : dk * (h + 1)], memory, 1, 0)
         along = g_ref[:, dv * h : dv * (h + 1)].astype(F32) * crossing
         gc = put(gc, jnp.sum(along, axis=1, keepdims=True), h)
-    inverse = cols_ref[2]
-    gt = -scale * (lg_ref[...] * cols_ref[0] + cols_ref[1] * gc) * inverse * inverse * cols_ref[3]
-    gt_ref[...] = gt
-    gc_ref[...] = gc
-    weight = cols_ref[4] * gt * scale
+    tokens = cols_ref[...]
+    inside, cross, inverse, active, query_weight = (unpack(tokens, i, heads) for i in range(5))
+    gt = -scale * (unpack(sums_ref[...], 2, heads) * inside + cross * gc) * inverse * inverse * active
+    gt_ref[...] = pack([gt, gc], heads)
+    gt_ref.send()
+    weight = query_weight * gt * scale
     vectors = [
         jnp.sum(
             q_ref[:, dk * h : dk * (h + 1)].astype(F32) * weight[:, h : h + 1], axis=0, keepdims=True
@@ -374,27 +392,31 @@
     ]
     tile = jnp.concatenate(vectors + [jnp.zeros((8 - heads, 128), F32)], axis=0)
     tile_ref[...] = tile
+    tile_ref.send()
     out_ref[:, :, dv:] = jnp.broadcast_to(tile[None], (count, 8, 128))
+
+    coef = coef_ref.ready()
 
     def backward(i, state):
         j = count - 1 - i
         out_ref[j, :, :dv] = state
-        step = wide(coef_ref, 3, j, reps) * got_ref[j, :, dv:]
-        return wide(coef_ref, 2, j, reps) * state + step
+        step = wide(coef, 1, j, reps) * got_ref[j, :, dv:]
+        return wide(coef, 0, j, reps) * state + step
 
     lax.fori_loop(0, count, backward, jnp.zeros((8, dv), F32), unroll=8)
 
 
 def inner_kernel(
-    heads, scale, mem_ref, cols_ref, small_ref, gt_ref, gc_ref, wl_ref, pc_ref, gv_ref,
+    heads, scale, mem_ref, cols_ref, small_ref, gt_ref, wl_ref, pc_ref, gv_ref,
     q_ref, k_ref, g_ref,
     gq_ref, gvalue_ref, gk_ref, row_ref, cold_ref,
 ):
     n = q_ref.shape[0]
     dk = q_ref.shape[1] // heads
     dv = g_ref.shape[1] // heads
-    gt, gc = gt_ref[...], gc_ref[...]
-    inside, cross, inverse, qn = cols_ref[0], cols_ref[1], cols_ref[2], cols_ref[5]
+    gt, tokens = gt_ref[...], cols_ref[...]
+    gc = unpack(gt, 1, heads)
+    inside, cross, inverse, qn = (unpack(tokens, i, heads) for i in (0, 1, 2, 5))
     row_part = scale * cross * (inverse * gc + gt * qn)
     for h in range(heads):
         ks, vs = slice(dk * h, dk * (h + 1)), slice(dv * h, dv * (h + 1))
@@ -421,11 +443,11 @@
 
 
 def after_kernel(
-    heads, me_ref, got_ref, later_ref, small_ref, dual_ref, pair_ref, tile_ref,
+    heads, me_ref, got_ref, later_ref, small_ref, odd_ref, tile_ref, unused_ref,
     give_ref, mine_ref, sum_ref,
 ):
     core = me_ref[0] % 2
-    count, dv = mine_ref.shape[0], dual_ref.shape[2]
+    count, dv = mine_ref.shape[0], mine_ref.shape[2]
     per_head = count // (heads // 2)
     vectors = [
         jnp.sum(later_ref[:, h : h + 1] * got_ref[:, h, dv:], axis=0, keepdims=True)
@@ -434,28 +456,29 @@
     tile = jnp.concatenate(vectors + [tile_ref[:heads]], axis=0)
     sum_ref[...] = tile
     give_ref[count] = jnp.concatenate([tile, jnp.zeros((8, dv - 128), F32)], axis=1)
-
-    def fill(even_ref, odd_ref, odd_own):
+    odd, small = odd_ref.ready(), small_ref[...]
+
+    def fill(to_even_ref, to_odd_ref):
         for i in range(heads // 2):
             at = core * (heads // 2) + i
             slab = slice(i * per_head, (i + 1) * per_head)
             after = got_ref[slab, :, :dv]
-            odd_ref[slab] = after
-            even_ref[slab] = pick(small_ref[8:9], at) * after + pick(small_ref[9:10], at) * odd_own(i)
+            to_odd_ref[slab] = after
+            to_even_ref[slab] = pick(small[8:9], at) * after + pick(small[9:10], at) * odd[slab]
 
     @pl.when(core == 0)
     def _():
-        fill(mine_ref, give_ref, lambda i: pair_ref[i * per_head : (i + 1) * per_head])
+        fill(mine_ref, give_ref)
 
     @pl.when(core == 1)
     def _():
-        fill(give_ref, mine_ref, lambda i: dual_ref[count + i * per_head : count + (i + 1) * per_head])
+        fill(give_ref, mine_ref)
 
 
 def weights_kernel(
-    heads, me_ref, mine_ref, pair_ref, sum_ref, mem_ref, small_ref, kl_ref, rows_ref, row_ref, cold_ref,
-    k_ref, v_ref, x_ref,
-    after_ref, vector_ref, carried_ref, pay_ref,
+    heads, me_ref, mine_ref, pair_ref, sum_ref, small_ref, cols_ref, k_ref, v_ref, mem_ref, row_ref,
+    cold_ref, rows_ref, x_ref,
+    after_ref, vector_ref, pay_ref,
 ):
     core = me_ref[0] % 2
     n = k_ref.shape[0]
@@ -464,8 +487,9 @@
     count = mine_ref.shape[0]
     after_ref[pl.ds(core * count, count)] = mine_ref[...]
     after_ref[pl.ds((1 - core) * count, count)] = pair_ref[:count]
+    after_ref.send()
     mine, other = sum_ref[...], pair_ref[count, :, :128]
-    key_scale = jnp.exp(kl_ref[...] + small_ref[heads : heads + 1])
+    key_scale = jnp.exp(unpack(cols_ref[...], 1, heads) + small_ref[heads : heads + 1])
     column_cross = jnp.zeros((n, 128), F32)
     through = jnp.zeros((1, 128), F32)
     vectors = []
@@ -478,7 +502,6 @@
         vectors.append(vector)
         following = after_ref[slab].reshape(dk, dv)
         carried = dot_right(k_ref[:, ks], following, 1, 0)
-        carried_ref[:, vs] = carried
         along = jnp.sum(v_ref[:, vs].astype(F32) * carried, axis=1, keepdims=True)
         along = along + jnp.sum(k_ref[:, ks].astype(F32) * vector, axis=1, keepdims=True)
         column_cross = put(column_cross, key_scale[:, one] * along, h)
@@ -487,6 +510,7 @@
         product = product + jnp.sum(small_ref[one] * vector, axis=1, keepdims=True)
         through = put(through, product, h)
     vector_ref[...] = jnp.concatenate(vectors + [jnp.zeros((8 - heads, 128), F32)], axis=0)
+    vector_ref.send()
     through = through * small_ref[heads + 1 : heads + 2]
     row = row_ref[...].T[:8]
     crossing = column_cross.T[:8]
@@ -509,18 +533,20 @@
 
 
 def finish_kernel(
-    heads, after_ref, vector_ref, carried_ref, small_ref, kl_ref, gk_ref, gvalue_ref, v_ref,
+    heads, after_ref, vector_ref, small_ref, cols_ref, gk_ref, gvalue_ref, k_ref, v_ref,
     gkey_ref, out_ref,
 ):
     dk = gk_ref.shape[1] // heads
     dv = v_ref.shape[1] // heads
-    key_scale = jnp.exp(kl_ref[...] + small_ref[heads : heads + 1])
+    key_scale = jnp.exp(unpack(cols_ref[...], 1, heads) + small_ref[heads : heads + 1])
     for h in range(heads):
         ks, vs, one = slice(dk * h, dk * (h + 1)), slice(dv * h, dv * (h + 1)), slice(h, h + 1)
         following = after_ref[dk // 8 * h : dk // 8 * (h + 1)].reshape(dk, dv)
-        carried = dot_right(v_ref[:, vs], following, 1, 1) + vector_ref[one]
+        high, low = split(following)
+        carried = dot(v_ref[:, vs], high, 1, 1) + dot(v_ref[:, vs], low, 1, 1) + vector_ref[one]
         gkey_ref[:, ks] = (gk_ref[:, ks] + key_scale[:, one] * carried).astype(BF16)
-        out_ref[:, vs] = (gvalue_ref[:, vs] + key_scale[:, one] * carried_ref[:, vs]).astype(BF16)
+        carried = dot(k_ref[:, ks], high, 1, 0) + dot(k_ref[:, ks], low, 1, 0)
+        out_ref[:, vs] = (gvalue_ref[:, vs] + key_scale[:, one] * carried).astype(BF16)
 
 
 def sum_kernel(got_ref, out_ref):
@@ -535,14 +561,101 @@
         second_ref[:, 128 * c : 128 * (c + 1)] = got_ref[tiles + c]
 
 
-def call(body, shapes, *args, scalars=()):
-    shapes = [s if isinstance(s, jax.ShapeDtypeStruct) else jax.ShapeDtypeStruct(s, F32) for s in shapes]
+class Fetched:
+    def __init__(self, copy, ref):
+        self.copy, self.ref, self.waited = copy, ref, False
+
+    def ready(self):
+        if not self.waited:
+            self.copy.wait()
+            self.waited = True
+        return self.ref
+
+    @property
+    def shape(self):
+        return self.ref.shape
+
+    def __getitem__(self, at):
+        return self.ready()[at]
+
+
+class Stored:
+    def __init__(self, copy, ref):
+        self.copy, self.ref, self.sent = copy, ref, False
+
+    @property
+    def shape(self):
+        return self.ref.shape
+
+    def send(self):
+        if not self.sent:
+            self.copy.start()
+            self.sent = True
+
+    def __getitem__(self, at):
+        return self.ref[at]
+
+    def __setitem__(self, at, value):
+        self.ref[at] = value
+
+
+def call(body, outs, ins, limit=24):
+    outs = [(k, o if isinstance(o, jax.ShapeDtypeStruct) else jax.ShapeDtypeStruct(o, F32)) for k, o in outs]
+    spaces = {"s": pltpu.SMEM, "v": pltpu.VMEM, "h": pltpu.HBM, "m": pltpu.HBM, "a": pltpu.HBM}
+    scratch = [
+        (pltpu.SMEM if k == "m" else pltpu.VMEM)(a.shape, a.dtype) for k, a in ins + outs if k in "hm"
+    ]
+    scratch.append(pltpu.SemaphoreType.DMA((max(len(scratch), 1),)))
+
+    def kernel(*refs):
+        given, rest = refs[: len(ins)], refs[len(ins) :]
+        results, buffers, sems = rest[: len(outs)], rest[len(outs) : -1], rest[-1]
+        taken, made, used = [], [], 0
+        for (kind, _), ref in zip(ins, given):
+            if kind in "hm":
+                copy = pltpu.make_async_copy(ref, buffers[used], sems.at[used])
+                copy.start()
+                ref = Fetched(copy, buffers[used])
+                used += 1
+            taken.append(ref)
+        for (kind, _), ref in zip(outs, results):
+            if kind == "h":
+                copy = pltpu.make_async_copy(buffers[used], ref, sems.at[used])
+                ref = Stored(copy, buffers[used])
+                used += 1
+            made.append(ref)
+        body(*taken, *made)
+        for ref in taken:
+            if isinstance(ref, Fetched):
+                ref.ready()
+        for ref in made:
+            if isinstance(ref, Stored):
+                ref.send()
+        for ref in made:
+            if isinstance(ref, Stored):
+                ref.copy.wait()
+
     return pl.pallas_call(
-        body,
-        out_shape=shapes,
-        in_specs=[SMEM if i in scalars else VMEM for i in range(len(args))],
-        out_specs=[VMEM] * len(shapes),
-    )(*args)
+        kernel,
+        out_shape=[pltpu.HBM(o.shape, o.dtype) if k == "h" else o for k, o in outs],
+        in_specs=[pl.BlockSpec(memory_space=spaces[k]) for k, _ in ins],
+        out_specs=[pl.BlockSpec(memory_space=spaces[k]) for k, _ in outs],
+        scratch_shapes=scratch,
+        compiler_params=pltpu.CompilerParams(vmem_limit_bytes=limit * 1024 * 1024),
+    )(*[pltpu.with_memory_space_constraint(a, pltpu.HBM) if k in "hma" else a for k, a in ins])
+
+
+def pack(items, heads):
+    total = None
+    for i, x in enumerate(items):
+        x = jnp.where(iota(x.shape, 1) < heads, x, 0.0)
+        x = pltpu.roll(x, heads * i, 1) if i else x
+        total = x if total is None else total + x
+    return total
+
+
+def unpack(x, i, heads):
+    return pltpu.roll(x, 128 - heads * i, 1) if i else x
 
 
 def exchange(x, axis, groups=None):
@@ -568,80 +681,87 @@
     def to_pair(a):
         return lax.ppermute(a, "ctx", [(i, i ^ 1) for i in range(devices)])
 
-    give, memory, tile, rows, lc, dc, kl = call(
+    low = jax.ShapeDtypeStruct
+
+    def given(kinds, *arrays):
+        return list(zip(kinds, arrays, strict=True))
+
+    give, memory, tile, rows, token_cols = call(
         part(gates_kernel, heads),
-        [(slabs // 2 + 1, 8, dv), (slabs, 8, dv), (8, 128), (16, n), cols, cols, cols],
-        me, x, w_input.T, w_forget.T, b_input, b_forget, doc_pos, k, v,
-        scalars=(0, 4, 5),
-    )
-    pair_memory = to_pair(give)
-    (pay,) = call(
-        part(first_kernel, heads), [(count, 8, dv + 128)], me, memory, tile, pair_memory, scalars=(0,)
+        given("vvvhh", (slabs // 2 + 1, 8, dv), (slabs, 8, dv), (8, 128), (16, n), cols),
+        given("shhhmmhhh", me, x, w_input.T, w_forget.T, b_input, b_forget, doc_pos, k, v),
+    )
+    pair = to_pair(give)
+    pay, even_memory, even_tile = call(
+        part(first_kernel, heads),
+        given("vhh", (count, 8, dv + 128), (count, 8, dv), (8, 128)),
+        given("svvv", me, memory, tile, pair),
     )
     first = exchange(pay, "ctx", cores)
-    wl, pc, gv, rm, ls, lg = call(
+    wl, pc, gv, sums = call(
         part(pairs_kernel, heads),
-        [(heads, n, n)] * 3 + [cols] * 3,
-        rows, lc, dc, q, k, v, g,
-    )
-    give, dual, coef, later, small, tokens = call(
+        given("hhhh", *[(heads, n, n)] * 3, cols),
+        given("hhhhhh", rows, token_cols, q, k, v, g),
+    )
+    give, dual, coef, now, coef_later, later, small, tokens = call(
         part(dual_kernel, heads, scale),
-        [(count, 8, dv), (slabs, 8, dv), (4, count, 128), (count, 128), (16, 128), (6, n, 128)],
-        me, first, tile, pair_memory[slabs // 2 :], lc, dc, rm, ls, q, g,
-        scalars=(0,),
-    )
-    pair_dual = to_pair(give)
-    (pay,) = call(
+        given(
+            "vvvvhhhh", (count, 8, dv), (count, 8, dv), (2, count, 128), (16, 128),
+            (2, count, 128), (count, 128), (16, 128), cols,
+        ),
+        given("svhhhhh", me, first, even_tile, token_cols, sums, q, g),
+    )
+    pair = to_pair(give)
+    pay, odd_dual = call(
         part(second_kernel, heads),
-        [(count, 8, 2 * dv)],
-        me, first, coef, small, dual, pair_dual,
-        scalars=(0,),
+        given("vh", (count, 8, 2 * dv), (count, 8, dv)),
+        given("svvvvv", me, first, coef, now, dual, pair),
     )
     second = exchange(pay, "ctx", cores)
     give, mine = call(
         part(halves_kernel, heads),
-        [(count, 8, dv)] * 2,
-        me, second, memory, pair_memory, small,
-        scalars=(0,),
+        given("vv", (count, 8, dv), (count, 8, dv)),
+        given("svhh", me, second, even_memory, small),
     )
     pair = to_pair(give)
-    pay, states, tile, gt, gc = call(
+    pay, states, tile, gt = call(
         part(vector_kernel, heads, scale),
-        [(count, 8, dv + 128), (slabs, 8, dv), (8, 128), cols, cols],
-        me, mine, pair, second, coef, tokens, lg, q, g,
-        scalars=(0,),
+        given("vhhh", (count, 8, dv + 128), (slabs, 8, dv), (8, 128), cols),
+        given("svvvhhhhh", me, mine, pair, second, coef_later, tokens, sums, q, g),
     )
     third = exchange(pay, "ctx", cores)
     grad_q, gvalue, gk, row, cold = call(
         part(inner_kernel, heads, scale),
-        [jax.ShapeDtypeStruct(q.shape, BF16), v.shape, k.shape, cols, (8, n)],
-        states, tokens, small, gt, gc, wl, pc, gv, q, k, g,
-    )
-    give, mine, tile = call(
+        given("hhhhh", low(q.shape, BF16), v.shape, k.shape, cols, (8, n)),
+        given("hhhhhhhhhh", states, tokens, small, gt, wl, pc, gv, q, k, g),
+    )
+    give, mine, sums = call(
         part(after_kernel, heads),
-        [(count + 1, 8, dv), (count, 8, dv), (8, 128)],
-        me, third, later, small, dual, pair_dual, tile,
-        scalars=(0,),
+        given("vvv", (count + 1, 8, dv), (count, 8, dv), (8, 128)),
+        given("svhhhha", me, third, later, small, odd_dual, tile, gk),
     )
     pair = to_pair(give)
     chunks = 2 * x.shape[1] // 128
-    following, vector, carried, pay = call(
+    following, vector, pay = call(
         part(weights_kernel, heads),
-        [(slabs, 8, dv), (8, 128), v.shape, (chunks, heads, 128)],
-        me, mine, pair, tile, states, small, kl, rows, row, cold, k, v, x,
-        scalars=(0,),
+        given("hhv", (slabs, 8, dv), (8, 128), (chunks, heads, 128)),
+        given(
+            "svvvhhhhhhhhh", me, mine, pair, sums, small, token_cols, k, v, states, row, cold, rows, x
+        ),
     )
     got = exchange(pay, "ctx")
     grad_k, grad_v = call(
         part(finish_kernel, heads),
-        [jax.ShapeDtypeStruct(k.shape, BF16), jax.ShapeDtypeStruct(v.shape, BF16)],
-        following, vector, carried, small, kl, gk, gvalue, v,
-    )
-    (pay,) = call(sum_kernel, [(lax.axis_size("dp"), heads, 128)], got)
+        given("hh", low(k.shape, BF16), low(v.shape, BF16)),
+        given("hhhhhhhh", following, vector, small, token_cols, gk, gvalue, k, v),
+    )
+    (pay,) = call(sum_kernel, given("v", (lax.axis_size("dp"), heads, 128)), given("v", got))
     got = exchange(pay, "dp")
-    (pay,) = call(sum_kernel, [(devices, heads, 128)], got)
+    (pay,) = call(sum_kernel, given("v", (devices, heads, 128)), given("v", got))
     got = exchange(pay, "ctx")
-    first, second = call(place_kernel, [(heads, x.shape[1])] * 2, got)
+    first, second = call(
+        place_kernel, given("vv", (heads, x.shape[1]), (heads, x.shape[1])), given("v", got)
+    )
     return (grad_q[None], grad_k[None], grad_v[None], first.T, second.T)
 
 

time: 161 us -> 140 us (0.87)
  blocking collectives: 64.6 us -> 44.3 us
  waiting for transfers between devices: 20.4 us -> 29.2 us
  Pallas kernels: 43.9 us -> 35.2 us
  local copies, waits for them, and re-layouts: 5.5 us -> 0 us
  starting transfers between devices: 25.1 us -> 30.2 us
    all_to_all x4 -> x3, blocking collectives: 64.6 us -> 44.3 us  [exchange(): return lax.all_to_all(x, axis, 0, 0, axis_index_groups=groups)]
    pallas_call x14, Pallas kernels: 43.9 us -> 35.2 us  [call(): pl.pallas_call(kernel, out_shape=[pltpu.HBM(o.shape, o.dtype) if k == 'h'...]
    all_to_all x2 -> x3, waiting for transfers between devices: 16.2 us -> 24.5 us  [exchange(): return lax.all_to_all(x, axis, 0, 0, axis_index_groups=groups)]
    all_to_all x2 -> x3, starting transfers between devices: 15.2 us -> 19.5 us  [exchange(): return lax.all_to_all(x, axis, 0, 0, axis_index_groups=groups)]
    unnamed x12 -> x0, local copies, waits for them, and re-layouts: 4.21 us -> none
  transfers between devices with their start and end apart: 6 -> 7, of which waited for: 5 -> 7; matrix products, arithmetic and copies ran while one was open for 1% -> 0% of each run, Pallas kernels for 9% -> 10%
where the time goes in v3:
time: 140 us
  blocking collectives  44.3 us (32%)
  Pallas kernels  35.2 us (25%)
  starting transfers between devices  30.2 us (22%)
  waiting for transfers between devices  29.2 us (21%)
    all_to_all x3, blocking collectives, exchange(): return lax.all_to_all(x, axis, 0, 0, axis_index_groups=groups)  44.3 us
    pallas_call x14, Pallas kernels, call(): pl.pallas_call(kernel, out_shape=[pltpu.HBM(o.shape, o.dtype) if k == 'h'...  35.2 us
    all_to_all x3, waiting for transfers between devices, exchange(): return lax.all_to_all(x, axis, 0, 0, axis_index_groups=groups)  24.5 us
    all_to_all x3, starting transfers between devices, exchange(): return lax.all_to_all(x, axis, 0, 0, axis_index_groups=groups)  19.5 us
    ppermute x4, starting transfers between devices, to_pair(): return lax.ppermute(a, 'ctx', [(i, i ^ 1) for i in range(devices)])  10.6 us
    ppermute x4, waiting for transfers between devices, to_pair(): return lax.ppermute(a, 'ctx', [(i, i ^ 1) for i in range(devices)])  4.67 us
  transfers between devices with their start and end apart: 7, of which 7 were waited for; matrix products, arithmetic and copies ran while one was open for 0% of the time, Pallas kernels for 10%

profile of v3, /device:TPU:1, one launch (start us, length us, event | category | flops | bytes accessed | tf_op | source)
XLA Modules:
  0.0 139.8 jit_solution(12386689253987672698)
XLA Ops:
  0.6 3.9 %shard_map.137 = (f32[33,8,256]{2,1,0:T(8,128)S(1)}, f32[64,8,256]{2,1,0:T(8,128)S(1)}, f32[8,128]{1,0:T(8,128)S(1)}, f32[16,256]{1,0:T(8,128)}, f32[256,128]{1,0:T(8,128)}) custom-call(s32[1]{0:T(128)} %bitcast.refs_0_, bf16[256,4096]{1,0:T(8,128)(2,1)} %bitcast.17, bf16[4,4096]{1,0:T(4,128)(2,1)} %bitcast.32, bf16[4,4096]{1,0:T(4,128)(2,1)} %bitcast.33, ...), custom_call_target="tpu_custom_call" | custom-call | tf_op jit(solution)/shard_map/pallas_call | solution.py:638
  4.6 3.3 %collective-permute-start = (f32[33,8,256]{2,1,0:T(8,128)S(1)}, f32[33,8,256]{2,1,0:T(8,128)S(1)}, u32[]{:S(2)}, u32[]{:S(2)}) collective-permute-start(f32[33,8,256]{2,1,0:T(8,128)S(1)} %get-tuple-element.50), channel_id=1, source_target_pairs={{0,4},{4,0},{8,12},{12,8},{16,20},{20,16},{24,28},{28,24},{32,36},... | collective-permute-start | bytes 811016 | tf_op jit(solution)/shard_map/ppermute | solution.py:682
  7.9 1.2 collective-permute-done.refs_3_
  9.1 1.5 %shard_map.138 = (f32[32,8,384]{2,1,0:T(8,128)}, f32[32,8,256]{2,1,0:T(8,128)}, f32[8,128]{1,0:T(8,128)}) custom-call(s32[1]{0:T(128)} %bitcast.refs_0_, f32[64,8,256]{2,1,0:T(8,128)S(1)} %get-tuple-element.48.refs_1_, f32[8,128]{1,0:T(8,128)S(1)} %get-tuple-element.49.refs_2_, f32[33,8,256]{2,1,0:T(8,128)S(1)} %collective-permute-done.refs_3_), custom_call_target="tpu_custom_call" | custom-call | tf_op jit(solution)/shard_map/pallas_call | solution.py:638
  10.6 9.3 %all-to-all-start = ((f32[32,8,384]{2,1,0:T(8,128)}), f32[32,8,384]{2,1,0:T(8,128)S(1)}, u32[]{:S(2)}, u32[]{:S(2)}) async-start(f32[32,8,384]{2,1,0:T(8,128)} %get-tuple-element.51), calls=%async_computation | async-start | bytes 786432 | tf_op jit(solution)/shard_map/all_to_all | solution.py:662
  19.9 4.3 %shard_map.139 = (f32[4,256,256]{2,1,0:T(8,128)}, f32[4,256,256]{2,1,0:T(8,128)}, f32[4,256,256]{2,1,0:T(8,128)}, f32[256,128]{1,0:T(8,128)}) custom-call(f32[16,256]{1,0:T(8,128)} %get-tuple-element.54.refs_0_.refs_11_, f32[256,128]{1,0:T(8,128)} %get-tuple-element.53.refs_1_.refs_3_.refs_5_, bf16[256,512]{1,0:T(8,128)(2,1)} %bitcast.28, ...), custom_call_target="tpu_custom_call" | custom-call | tf_op jit(solution)/shard_map/pallas_call | solution.py:638
  24.2 9.6 %all-to-all-done.refs_1_ = f32[32,8,384]{2,1,0:T(8,128)S(1)} async-done(((f32[32,8,384]{2,1,0:T(8,128)}), f32[32,8,384]{2,1,0:T(8,128)S(1)}, u32[]{:S(2)}, u32[]{:S(2)}) %all-to-all-start) | async-done | bytes 393248 | tf_op jit(solution)/shard_map/all_to_all | solution.py:662
  33.8 2.8 %shard_map.140 = (f32[32,8,256]{2,1,0:T(8,128)S(1)}, f32[32,8,256]{2,1,0:T(8,128)S(1)}, f32[2,32,128]{2,1,0:T(8,128)S(1)}, f32[16,128]{1,0:T(8,128)S(1)}, f32[2,...) custom-call(s32[1]{0:T(128)} %bitcast.refs_0_, ...), custom_call_target="tpu_custom_call" | custom-call | tf_op jit(solution)/shard_map/pallas_call | solution.py:638
  36.7 2.4 %collective-permute-start.1 = (f32[32,8,256]{2,1,0:T(8,128)S(1)}, f32[32,8,256]{2,1,0:T(8,128)S(1)}, u32[]{:S(2)}, u32[]{:S(2)}) collective-permute-start(f32[32,8,256]{2,1,0:T(8,128)S(1)} %get-tuple-element.59), channel_id=1, source_target_pairs={{0,4},{4,0},{8,12},{12,8},{16,20},{20,16},{24,28},{28,24},{32,36},... | collective-permute-start | bytes 786440 | tf_op jit(solution)/shard_map/ppermute | solution.py:682
  39.1 1.2 collective-permute-done.1.refs_5_
  40.3 0.8 shard_map.141
  41.0 20.4 %all_to_all.30.refs_1_.refs_3_ = f32[32,8,512]{2,1,0:T(8,128)S(1)} all-to-all(f32[32,8,512]{2,1,0:T(8,128)S(1)} %get-tuple-element.60), channel_id=1, replica_groups={{0,8,16,24,32,40,48,56,64,72,80,88,96,104,112,120,128,136,144,152,160,1..., dimensions={0} | all-to-all | bytes 1048576 | tf_op jit(solution)/shard_map/all_to_all | solution.py:662
  61.4 1.1 shard_map.142
  62.5 2.3 %collective-permute-start.2 = (f32[32,8,256]{2,1,0:T(8,128)S(1)}, f32[32,8,256]{2,1,0:T(8,128)S(1)}, u32[]{:S(2)}, u32[]{:S(2)}) collective-permute-start(f32[32,8,256]{2,1,0:T(8,128)S(1)} %get-tuple-element.64), channel_id=1, source_target_pairs={{0,4},{4,0},{8,12},{12,8},{16,20},{20,16},{24,28},{28,24},{32,36},... | collective-permute-start | bytes 786440 | tf_op jit(solution)/shard_map/ppermute | solution.py:682
  64.8 1.2 collective-permute-done.2.refs_2_
  66.0 4.0 %shard_map.143 = (f32[32,8,384]{2,1,0:T(8,128)}, f32[64,8,256]{2,1,0:T(8,128)}, f32[8,128]{1,0:T(8,128)}, f32[256,128]{1,0:T(8,128)}) custom-call(s32[1]{0:T(128)} %bitcast.refs_0_, f32[32,8,256]{2,1,0:T(8,128)S(1)} %get-tuple-element.63.refs_1_, f32[32,8,256]{2,1,0:T(8,128)S(1)} %collective-permute-done.2.refs_2_, ...), custom_call_target="tpu_custom_call" | custom-call | tf_op jit(solution)/shard_map/pallas_call | solution.py:638
  70.0 4.3 %all-to-all-start.2 = ((f32[32,8,384]{2,1,0:T(8,128)}), f32[32,8,384]{2,1,0:T(8,128)S(1)}, u32[]{:S(2)}, u32[]{:S(2)}) async-start(f32[32,8,384]{2,1,0:T(8,128)} %get-tuple-element.73), calls=%async_computation.2 | async-start | bytes 786432 | tf_op jit(solution)/shard_map/all_to_all | solution.py:662
  74.3 6.2 %shard_map.144 = (bf16[256,512]{1,0:T(8,128)(2,1)}, f32[256,1024]{1,0:T(8,128)}, f32[256,512]{1,0:T(8,128)}, f32[256,128]{1,0:T(8,128)}, f32[8,256]{1,0:T(8,128)}) custom-call(f32[64,8,256]{2,1,0:T(8,128)} %get-tuple-element.67.refs_0_.refs_8_, f32[256,128]{1,0:T(8,128)} %get-tuple-element.66.refs_5_.refs_1_, ...), custom_call_target="tpu_custom_call" | custom-call | tf_op jit(solution)/shard_map/pallas_call | solution.py:638
  80.5 7.6 %all-to-all-done.2.refs_1_ = f32[32,8,384]{2,1,0:T(8,128)S(1)} async-done(((f32[32,8,384]{2,1,0:T(8,128)}), f32[32,8,384]{2,1,0:T(8,128)S(1)}, u32[]{:S(2)}, u32[]{:S(2)}) %all-to-all-start.2) | async-done | bytes 393248 | tf_op jit(solution)/shard_map/all_to_all | solution.py:662
  88.2 1.1 shard_map.145
  89.3 2.6 %collective-permute-start.3 = (f32[33,8,256]{2,1,0:T(8,128)S(1)}, f32[33,8,256]{2,1,0:T(8,128)S(1)}, u32[]{:S(2)}, u32[]{:S(2)}) collective-permute-start(f32[33,8,256]{2,1,0:T(8,128)S(1)} %get-tuple-element.79), channel_id=1, source_target_pairs={{0,4},{4,0},{8,12},{12,8},{16,20},{20,16},{24,28},{28,24},{32,36},... | collective-permute-start | bytes 811016 | tf_op jit(solution)/shard_map/ppermute | solution.py:682
  91.9 1.2 collective-permute-done.3.refs_2_
  93.1 3.9 %shard_map.146 = (f32[64,8,256]{2,1,0:T(8,128)}, f32[8,128]{1,0:T(8,128)}, f32[64,4,128]{2,1,0:T(4,128)S(1)}) custom-call(s32[1]{0:T(128)} %bitcast.refs_0_, f32[32,8,256]{2,1,0:T(8,128)S(1)} %get-tuple-element.78.refs_1_, f32[33,8,256]{2,1,0:T(8,128)S(1)} %collective-permute-done.3.refs_2_, f32[8,128]{1,0:T(8,128)S(1)} %get-tuple-element.80.refs_3_, ...), custom_call_target="tpu_custom_call" | custom-call | tf_op jit(solution)/shard_map/pallas_call | solution.py:638
  97.0 15.8 %all_to_all.31.refs_0_ = f32[64,4,128]{2,1,0:T(4,128)S(1)} all-to-all(f32[64,4,128]{2,1,0:T(4,128)S(1)} %get-tuple-element.88), channel_id=1, replica_groups=mesh['ctx'=64,'dp'=4] {'ctx'}, dimensions={0} | all-to-all | bytes 262144 | tf_op jit(solution)/shard_map/all_to_all | solution.py:662
  112.8 0.1 shard_map.148
  112.9 8.2 %all_to_all.32.refs_0_ = f32[4,4,128]{2,1,0:T(4,128)S(1)} all-to-all(f32[4,4,128]{2,1,0:T(4,128)S(1)} %shard_map.148), channel_id=1, replica_groups=mesh['ctx'=64,'dp'=4] {'dp'}, dimensions={0} | all-to-all | bytes 16384 | tf_op jit(solution)/shard_map/all_to_all | solution.py:662
  121.0 0.7 shard_map.149
  121.7 5.9 %all-to-all-start.5 = ((f32[64,4,128]{2,1,0:T(4,128)}), f32[64,4,128]{2,1,0:T(4,128)S(1)}, u32[]{:S(2)}, u32[]{:S(2)}) async-start(f32[64,4,128]{2,1,0:T(4,128)} %shard_map.149), calls=%async_computation.5 | async-start | bytes 262144 | tf_op jit(solution)/shard_map/all_to_all | solution.py:662
  127.6 4.0 %shard_map.147 = (bf16[256,512]{1,0:T(8,128)(2,1)}, bf16[256,1024]{1,0:T(8,128)(2,1)}) custom-call(f32[64,8,256]{2,1,0:T(8,128)} %get-tuple-element.83.refs_0_, f32[8,128]{1,0:T(8,128)} %get-tuple-element.84.refs_1_, f32[16,128]{1,0:T(8,128)} %get-tuple-element.62.refs_3_.refs_2_.refs_4_, f32[256,128]{1,0:T(8,128)} %get-tuple-element.53.refs_1_.refs_3_.refs_5_, ...), custom_call_target="tpu_custom_call" | custom-call | tf_op jit(solution)/shard_map/pallas_call | solution.py:638
  131.6 7.3 %all-to-all-done.5.refs_0_ = f32[64,4,128]{2,1,0:T(4,128)S(1)} async-done(((f32[64,4,128]{2,1,0:T(4,128)}), f32[64,4,128]{2,1,0:T(4,128)S(1)}, u32[]{:S(2)}, u32[]{:S(2)}) %all-to-all-start.5) | async-done | bytes 131104 | tf_op jit(solution)/shard_map/all_to_all | solution.py:662
  138.9 0.7 shard_map.150
Async XLA Ops:
  4.6 4.5 %collective-permute-start = (f32[33,8,256]{2,1,0:T(8,128)S(1)}, f32[33,8,256]{2,1,0:T(8,128)S(1)}, u32[]{:S(2)}, u32[]{:S(2)}) collective-permute-start(f32[33,8,256]{2,1,0:T(8,128)S(1)} %get-tuple-element.50), channel_id=1, source_target_pairs={{0,4},{4,0},{8,12},{12,8},{16,20},{20,16},{24,28},{28,24},{32,36},... | collective-permute-start | bytes 811016 | tf_op jit(solution)/shard_map/ppermute | solution.py:682
  10.6 23.2 %all-to-all-start = ((f32[32,8,384]{2,1,0:T(8,128)}), f32[32,8,384]{2,1,0:T(8,128)S(1)}, u32[]{:S(2)}, u32[]{:S(2)}) async-start(f32[32,8,384]{2,1,0:T(8,128)} %get-tuple-element.51), calls=%async_computation | async-start | bytes 786432 | tf_op jit(solution)/shard_map/all_to_all | solution.py:662
  36.7 3.6 %collective-permute-start.1 = (f32[32,8,256]{2,1,0:T(8,128)S(1)}, f32[32,8,256]{2,1,0:T(8,128)S(1)}, u32[]{:S(2)}, u32[]{:S(2)}) collective-permute-start(f32[32,8,256]{2,1,0:T(8,128)S(1)} %get-tuple-element.59), channel_id=1, source_target_pairs={{0,4},{4,0},{8,12},{12,8},{16,20},{20,16},{24,28},{28,24},{32,36},... | collective-permute-start | bytes 786440 | tf_op jit(solution)/shard_map/ppermute | solution.py:682
  62.5 3.4 %collective-permute-start.2 = (f32[32,8,256]{2,1,0:T(8,128)S(1)}, f32[32,8,256]{2,1,0:T(8,128)S(1)}, u32[]{:S(2)}, u32[]{:S(2)}) collective-permute-start(f32[32,8,256]{2,1,0:T(8,128)S(1)} %get-tuple-element.64), channel_id=1, source_target_pairs={{0,4},{4,0},{8,12},{12,8},{16,20},{20,16},{24,28},{28,24},{32,36},... | collective-permute-start | bytes 786440 | tf_op jit(solution)/shard_map/ppermute | solution.py:682
  70.0 18.2 %all-to-all-start.2 = ((f32[32,8,384]{2,1,0:T(8,128)}), f32[32,8,384]{2,1,0:T(8,128)S(1)}, u32[]{:S(2)}, u32[]{:S(2)}) async-start(f32[32,8,384]{2,1,0:T(8,128)} %get-tuple-element.73), calls=%async_computation.2 | async-start | bytes 786432 | tf_op jit(solution)/shard_map/all_to_all | solution.py:662
  89.3 3.8 %collective-permute-start.3 = (f32[33,8,256]{2,1,0:T(8,128)S(1)}, f32[33,8,256]{2,1,0:T(8,128)S(1)}, u32[]{:S(2)}, u32[]{:S(2)}) collective-permute-start(f32[33,8,256]{2,1,0:T(8,128)S(1)} %get-tuple-element.79), channel_id=1, source_target_pairs={{0,4},{4,0},{8,12},{12,8},{16,20},{20,16},{24,28},{28,24},{32,36},... | collective-permute-start | bytes 811016 | tf_op jit(solution)/shard_map/ppermute | solution.py:682
  121.7 17.2 %all-to-all-start.5 = ((f32[64,4,128]{2,1,0:T(4,128)}), f32[64,4,128]{2,1,0:T(4,128)S(1)}, u32[]{:S(2)}, u32[]{:S(2)}) async-start(f32[64,4,128]{2,1,0:T(4,128)} %shard_map.149), calls=%async_computation.5 | async-start | bytes 262144 | tf_op jit(solution)/shard_map/all_to_all | solution.py:662

commit v4 on v3

--- a/solution.py
+++ b/solution.py
@@ -32,10 +32,20 @@
     return dot(a, high, ca, cb) + dot(a, low, ca, cb)
 
 
-def dot_exact(a, b):
-    return lax.dot_general(
-        a, b, (((1,), (0,)), ((), ())), precision=lax.Precision.HIGHEST, preferred_element_type=F32
-    )
+def thirds(x):
+    high = x.astype(BF16).astype(F32)
+    middle = (x - high).astype(BF16).astype(F32)
+    return [high, middle, x - high - middle]
+
+
+def times_ones(x, ones):
+    parts = dot(jnp.concatenate(thirds(x), axis=0).astype(BF16), ones.astype(F32).astype(BF16), 1, 0)
+    return parts[:8] + parts[8:16] + parts[16:24]
+
+
+def ones_times(ones, x):
+    parts = dot(ones.astype(F32).astype(BF16), jnp.concatenate(thirds(x), axis=1).astype(BF16), 1, 0)
+    return parts[:, :128] + parts[:, 128:256] + parts[:, 256:]
 
 
 def iota(shape, dim):
@@ -52,20 +62,45 @@
     return jnp.where(iota(acc.shape, 1) == h, col, acc)
 
 
+def down(row, heads):
+    return jnp.concatenate([pick(row, h) for h in range(heads)], axis=0)
+
+
+def across(column):
+    row = jnp.zeros((1, 128), F32)
+    for h in range(column.shape[0]):
+        row = put(row, column[h : h + 1], h)
+    return row
+
+
+def padded(rows):
+    return jnp.concatenate([rows, jnp.zeros((8 - rows.shape[0], rows.shape[1]), F32)], axis=0)
+
+
+def rows_times(rows, b):
+    parts = dot(jnp.concatenate(thirds(padded(rows)), axis=0).astype(BF16), b, 1, 0)
+    return parts[:8] + parts[8:16] + parts[16:24]
+
+
 def pick(row, lane):
     return jnp.sum(jnp.where(iota(row.shape, 1) == lane, row, 0.0), axis=1, keepdims=True)
 
 
 def gates_kernel(
-    heads, me_ref, x_ref, wi_ref, wf_ref, bi_ref, bf_ref, pos_ref, k_ref, v_ref,
-    give_ref, mem_ref, tile_ref, rows_ref, cols_ref,
+    heads, me_ref, wi_ref, wf_ref, bi_ref, bf_ref, pos_ref, k_ref, x_ref, v_ref,
+    give_ref, mem_ref, tile_ref, rows_ref,
 ):
     core = me_ref[0] % 2
     n = x_ref.shape[0]
     dk = k_ref.shape[1] // heads
     dv = v_ref.shape[1] // heads
-    w8 = jnp.concatenate([wi_ref[...].astype(F32), wf_ref[...].astype(F32)], axis=0).astype(BF16)
-    gates = dot(w8, x_ref[...], 1, 1)
+    weights = [wi_ref[...].astype(F32), wf_ref[...].astype(F32)]
+    weights.append(jnp.zeros((16 - 2 * heads, weights[0].shape[1]), F32))
+    weights = jnp.concatenate(weights, axis=0).astype(BF16)
+    k = k_ref[...]
+    turned = k.T
+    gates = dot(x_ref[...], weights, 1, 1)
+    gates = jnp.concatenate([gates, jnp.zeros((n, 112), F32)], axis=1).T[: 2 * heads]
     row8 = iota(gates.shape, 0)
     for h in range(heads):
         gates = gates + jnp.where(row8 == h, bi_ref[h], 0.0)
@@ -74,32 +109,27 @@
     log_forget = jnp.minimum(forget_pre, 0.0) - jnp.log1p(jnp.exp(-jnp.abs(forget_pre)))
     start = (pos_ref[...] == 0).astype(F32)
     stacked = jnp.concatenate([log_forget, start, jnp.zeros((7 - heads, n), F32)], axis=0)
-    upto = (iota((n, n), 0) <= iota((n, n), 1)).astype(F32)
-    cum = dot_exact(stacked, upto)
-    lc_row, dc_row = cum[:heads], cum[heads : heads + 1]
+    cum = times_ones(stacked, iota((n, n), 0) <= iota((n, n), 1))
+    lc, dc = cum[:heads], cum[heads : heads + 1]
+    total, last = lc[:, n - 1 :], dc[:, n - 1 :]
+    key_log = jnp.where(dc == last, total - lc + in_gate, NEG)
     rows_ref[...] = jnp.concatenate(
-        [in_gate, forget_pre, lc_row, dc_row, jnp.zeros((3, n), F32)], axis=0
-    )
-    ig = column_of(in_gate)
-    lc = column_of(lc_row)
-    dc = jnp.broadcast_to(dc_row, (128, n)).T
-    total, last = lc[n - 1 :], dc[n - 1 :]
-    key_log = jnp.where(dc == last, total - lc + ig, NEG)
-    cols_ref[...] = pack([lc, key_log, dc], heads)
+        [in_gate, forget_pre, lc, key_log, dc, jnp.zeros((7, n), F32)], axis=0
+    )
     rows_ref.send()
-    cols_ref.send()
-    own_max = jnp.max(key_log, axis=0, keepdims=True)
+    own_max = jnp.max(key_log, axis=1, keepdims=True)
     weight = jnp.exp(key_log - own_max)
-    vectors = []
+    sums = rows_times(weight, k)
+    column = column_of(weight)
     for h in range(heads):
-        weighted = k_ref[:, dk * h : dk * (h + 1)].astype(F32) * weight[:, h : h + 1]
-        vectors.append(jnp.sum(weighted, axis=0, keepdims=True))
-        memory = dot_left(weighted, v_ref[:, dv * h : dv * (h + 1)], 0, 0)
+        weighted = v_ref[:, dv * h : dv * (h + 1)].astype(F32) * column[:, h : h + 1]
+        memory = dot_right(turned[dk * h : dk * (h + 1)], weighted, 1, 0)
         mem_ref[dk // 8 * h : dk // 8 * (h + 1)] = memory.reshape(dk // 8, 8, dv)
     cut = jnp.where(last > 0.5, BIG, 0.0)
     tile = jnp.concatenate(
-        vectors
-        + [own_max, total - cut, ig[:1] - lc[:1], jnp.where(dc[:1] < 0.5, 1.0, 0.0)],
+        [sums[h : h + 1, dk * h : dk * (h + 1)] for h in range(heads)]
+        + [across(own_max), across(total - cut), across(in_gate[:, :1] - lc[:, :1])]
+        + [jnp.broadcast_to(jnp.where(dc[:, :1] < 0.5, 1.0, 0.0), (1, 128))],
         axis=0,
     )
     tile_ref[...] = tile
@@ -108,7 +138,7 @@
     give_ref[half] = jnp.concatenate([tile, jnp.zeros((8, dv - 128), F32)], axis=1)
 
 
-def first_kernel(heads, me_ref, mem_ref, tile_ref, got_ref, out_ref, even_ref, even_tile_ref):
+def first_kernel(heads, me_ref, mem_ref, tile_ref, got_ref, out_ref):
     core = me_ref[0] % 2
     half, dv = out_ref.shape[0], mem_ref.shape[2]
     mine, other = tile_ref[...], got_ref[half, :, :128]
@@ -131,27 +161,30 @@
         at = core * (heads // 2) + i
         slab = slice(i * per_head, (i + 1) * per_head)
         own = mem_ref[pl.ds(core * half + i * per_head, per_head)]
-        other = got_ref[slab]
-        out_ref[slab, :, :dv] = pick(weight_mine, at) * own + pick(weight_other, at) * other
-        even_ref[slab] = jnp.where(core == 0, own, other)
-    even_tile_ref[...] = even
+        out_ref[slab, :, :dv] = pick(weight_mine, at) * own + pick(weight_other, at) * got_ref[slab]
 
 
 def pairs_kernel(
-    heads, rows_ref, cols_ref, q_ref, k_ref, v_ref, g_ref,
-    wl_ref, pc_ref, gv_ref, sums_ref,
-):
+    heads, me_ref, mem_ref, tile_ref, got_ref, rows_ref, q_ref, k_ref, v_ref, g_ref,
+    even_ref, even_tile_ref, turned_ref, wl_ref, pc_ref, gv_ref, sums_ref,
+):
+    core = me_ref[0] % 2
+    half = even_ref.shape[0]
+    even_ref[...] = jnp.where(core == 0, mem_ref[pl.ds(core * half, half)], got_ref[:half])
+    even_ref.send()
+    even_tile_ref[...] = jnp.where(core == 0, tile_ref[...], got_ref[half, :, :128])
     n = q_ref.shape[0]
     dk = k_ref.shape[1] // heads
     dv = v_ref.shape[1] // heads
-    lc = cols_ref[...]
-    dc = lc[:, 2 * heads : 2 * heads + 1]
-    mask = (iota((n, n), 0) >= iota((n, n), 1)) & (dc == rows_ref[3 * heads : 3 * heads + 1])
-    rm = jnp.zeros((n, 128), F32)
-    ls, lg = rm, rm
+    rows = rows_ref[...]
+    lc = column_of(rows)
+    place = 4 * heads
+    mask = (iota((n, n), 0) >= iota((n, n), 1)) & (lc[:, place : place + 1] == rows[place : place + 1])
+    turned_ref[...] = q_ref[...].T
+    sums = jnp.zeros((n, 128), F32)
     for h in range(heads):
-        offset = rows_ref[h : h + 1] - rows_ref[2 * heads + h : 2 * heads + h + 1]
-        pair_log = jnp.where(mask, lc[:, h : h + 1] + offset, NEG)
+        offset = rows[h : h + 1] - rows[2 * heads + h : 2 * heads + h + 1]
+        pair_log = jnp.where(mask, lc[:, 2 * heads + h : 2 * heads + h + 1] + offset, NEG)
         row_max = jnp.max(pair_log, axis=1, keepdims=True)
         weight = jnp.exp(pair_log - row_max)
         ks, vs = slice(dk * h, dk * (h + 1)), slice(dv * h, dv * (h + 1))
@@ -160,10 +193,10 @@
         wl_ref[h] = weight
         pc_ref[h] = coupled
         gv_ref[h] = grad_pair
-        rm = put(rm, row_max, h)
-        ls = put(ls, jnp.sum(coupled, axis=1, keepdims=True), h)
-        lg = put(lg, jnp.sum(coupled * grad_pair, axis=1, keepdims=True), h)
-    sums_ref[...] = pack([rm, ls, lg], heads)
+        sums = put(sums, row_max, h)
+        sums = put(sums, jnp.sum(coupled, axis=1, keepdims=True), heads + h)
+        sums = put(sums, jnp.sum(coupled * grad_pair, axis=1, keepdims=True), 2 * heads + h)
+    sums_ref[...] = sums.T[: sums_ref.shape[0]]
 
 
 def shift_down(x, d, fill):
@@ -176,12 +209,12 @@
 
 
 def dual_kernel(
-    heads, scale, me_ref, got_ref, tile_ref, cols_ref, sums_ref, q_ref, g_ref,
+    heads, scale, me_ref, got_ref, tile_ref, rows_ref, sums_ref, turned_ref, g_ref,
     give_ref, dual_ref, coef_ref, now_ref, coef_later_ref, later_ref, small_ref, tokens_ref,
 ):
     count = got_ref.shape[0]
-    n = q_ref.shape[0]
-    dk = q_ref.shape[1] // heads
+    n = g_ref.shape[0]
+    dk = turned_ref.shape[0] // heads
     dv = g_ref.shape[1] // heads
     me = me_ref[0]
     core, chip = me % 2, me // 2
@@ -220,7 +253,6 @@
     for i, c in enumerate(coefs):
         mine = jnp.sum(jnp.where(lane == my_head, c, 0.0), axis=1, keepdims=True)
         (coef_ref if i < 2 else coef_later_ref)[i % 2] = jnp.broadcast_to(mine, c.shape)
-    coef_later_ref.send()
 
     def here(x):
         return jnp.sum(jnp.where(row == chip, x, 0.0), axis=0, keepdims=True)
@@ -233,17 +265,16 @@
     keep = here(jnp.exp(in_even + total_even - in_odd))
     add = here(jnp.exp(max_even - in_odd))
     later_row = iota((count, count), 0) < iota((count, count), 1)
-    between = dot_exact(later_row.astype(F32), jnp.where(row < chip, total, 0.0))
+    between = ones_times(later_row, jnp.where(row < chip, total, 0.0))
     weight = jnp.where(
         row < chip, jnp.exp(jnp.minimum(chip_max + between - here(in_even), 0.0)), 0.0
     )
     earlier_row = iota((count, count), 0) > iota((count, count), 1)
-    between = dot_exact(earlier_row.astype(F32), jnp.where(row > chip, total, 0.0))
+    between = ones_times(earlier_row, jnp.where(row > chip, total, 0.0))
     source = jnp.where(core == 0, dual_even, total_even + dual_odd)
     later_ref[...] = jnp.where(
         row > chip, jnp.exp(jnp.minimum(source + between - here(later_odd), 0.0)), 0.0
     )
-    later_ref.send()
     even_tile = tile_ref[...]
     vectors = []
     for h in range(heads):
@@ -270,31 +301,32 @@
     small_ref[...] = small
     small_ref.send()
     now_ref[...] = small
-    lc = cols_ref[...]
-    open_query = lc[:, 2 * heads : 2 * heads + 1] < 0.5
-    sums = sums_ref[...]
-    cross_log = jnp.where(open_query, lc + in_me, NEG)
-    row_max = jnp.maximum(sums, cross_log)
-    inside = jnp.exp(sums - row_max)
+    lc = rows_ref[2 * heads : 3 * heads]
+    open_query = rows_ref[4 * heads : 4 * heads + 1] < 0.5
+    inner_max = sums_ref[:heads]
+    cross_log = jnp.where(open_query, lc + down(in_me, heads), NEG)
+    row_max = jnp.maximum(inner_max, cross_log)
+    inside = jnp.exp(inner_max - row_max)
     cross = jnp.exp(cross_log - row_max)
-    qn = jnp.zeros((n, 128), F32)
-    for h in range(heads):
-        along = q_ref[:, dk * h : dk * (h + 1)].astype(F32) * vectors[h]
-        qn = put(qn, jnp.sum(along, axis=1, keepdims=True), h)
-    sums = scale * (unpack(sums, 1, heads) * inside + cross * qn)
+    qn = [
+        rows_times(small[:heads], turned_ref[dk * h : dk * (h + 1)])[h : h + 1] for h in range(heads)
+    ]
+    qn = jnp.concatenate(qn, axis=0)
+    sums = scale * (sums_ref[heads : 2 * heads] * inside + cross * qn)
     floor = jnp.exp(-row_max)
     size = jnp.abs(sums)
     inverse = 1.0 / jnp.maximum(size, floor)
     active = jnp.where(size > floor, jnp.where(sums > 0.0, 1.0, -1.0), 0.0)
-    query_weight = jnp.where(open_query, jnp.exp(jnp.minimum(lc - row_max - dual_me, 0.0)), 0.0)
-    tokens_ref[...] = pack([inside, cross, inverse, active, query_weight, qn], heads)
+    query_weight = jnp.exp(jnp.minimum(lc - row_max - down(dual_me, heads), 0.0))
+    query_weight = jnp.where(open_query, query_weight, 0.0)
+    tokens_ref[...] = jnp.concatenate([inside, cross, inverse, active, query_weight, qn], axis=0)
     tokens_ref.send()
-    grad_weight = query_weight * inverse * scale
+    grad_weight = column_of(query_weight * inverse * scale)
     half = give_ref.shape[0]
     per_head = dk // 8
     for h in range(heads):
         weighted = g_ref[:, dv * h : dv * (h + 1)].astype(F32) * grad_weight[:, h : h + 1]
-        memory = dot_right(q_ref[:, dk * h : dk * (h + 1)], weighted, 0, 0).reshape(per_head, 8, dv)
+        memory = dot_right(turned_ref[dk * h : dk * (h + 1)], weighted, 1, 0).reshape(per_head, 8, dv)
         slab = slice(per_head * h % half, per_head * h % half + per_head)
 
         @pl.when(core == h // (heads // 2))
@@ -311,7 +343,7 @@
 
 
 def second_kernel(
-    heads, me_ref, got_ref, coef_ref, small_ref, dual_ref, pair_ref, out_ref, odd_ref
+    heads, me_ref, got_ref, coef_ref, small_ref, dual_ref, pair_ref, out_ref
 ):
     core = me_ref[0] % 2
     count, dv = got_ref.shape[0], dual_ref.shape[2]
@@ -329,18 +361,20 @@
     for i in range(heads // 2):
         at = core * (heads // 2) + i
         slab = slice(i * per_head, (i + 1) * per_head)
-        own, other = dual_ref[slab], pair_ref[slab]
-        out_ref[slab, :, dv:] = pick(weight_mine, at) * own + pick(weight_other, at) * other
-        odd_ref[slab] = jnp.where(core == 0, other, own)
-    odd_ref.send()
+        step = pick(weight_other, at) * pair_ref[slab]
+        out_ref[slab, :, dv:] = pick(weight_mine, at) * dual_ref[slab] + step
     lax.fori_loop(0, count, forward, jnp.zeros((8, dv), F32), unroll=8)
 
 
-def halves_kernel(heads, me_ref, got_ref, even_ref, small_ref, give_ref, mine_ref):
+def odd_kernel(me_ref, dual_ref, pair_ref, odd_ref):
+    odd_ref[...] = jnp.where(me_ref[0] % 2 == 0, pair_ref[...], dual_ref[...])
+
+
+def halves_kernel(heads, me_ref, got_ref, even_ref, small_ref, unused_ref, give_ref, mine_ref):
     core = me_ref[0] % 2
     count, dv = give_ref.shape[0], give_ref.shape[2]
     per_head = count // (heads // 2)
-    even, small = even_ref.ready(), small_ref[...]
+    even, small = even_ref, small_ref[...]
 
     def fill(to_even_ref, to_odd_ref):
         for i in range(heads // 2):
@@ -360,7 +394,7 @@
 
 
 def vector_kernel(
-    heads, scale, me_ref, mine_ref, pair_ref, got_ref, coef_ref, cols_ref, sums_ref, q_ref, g_ref,
+    heads, scale, me_ref, mine_ref, pair_ref, got_ref, coef_ref, tokens_ref, sums_ref, q_ref, g_ref,
     out_ref, mem_ref, tile_ref, gt_ref,
 ):
     core = me_ref[0] % 2
@@ -372,51 +406,48 @@
     mem_ref[pl.ds(core * count, count)] = mine_ref[...]
     mem_ref[pl.ds((1 - core) * count, count)] = pair_ref[...]
     mem_ref.send()
+    coef = coef_ref
+
+    def backward(i, state):
+        j = count - 1 - i
+        for i in range(2):
+            for c in range(reps):
+                out_ref[j, i * reps + c] = state[4 * i : 4 * (i + 1), 128 * c : 128 * (c + 1)]
+        step = wide(coef, 1, j, reps) * got_ref[j, :, dv:]
+        return wide(coef, 0, j, reps) * state + step
+
+    lax.fori_loop(0, count, backward, jnp.zeros((8, dv), F32), unroll=8)
     gc = jnp.zeros((n, 128), F32)
     for h in range(heads):
         memory = mem_ref[dk // 8 * h : dk // 8 * (h + 1)].reshape(dk, dv)
         crossing = dot_right(q_ref[:, dk * h : dk * (h + 1)], memory, 1, 0)
         along = g_ref[:, dv * h : dv * (h + 1)].astype(F32) * crossing
         gc = put(gc, jnp.sum(along, axis=1, keepdims=True), h)
-    tokens = cols_ref[...]
-    inside, cross, inverse, active, query_weight = (unpack(tokens, i, heads) for i in range(5))
-    gt = -scale * (unpack(sums_ref[...], 2, heads) * inside + cross * gc) * inverse * inverse * active
-    gt_ref[...] = pack([gt, gc], heads)
+    inside, cross, inverse, active, query_weight = (
+        tokens_ref[heads * i : heads * (i + 1)] for i in range(5)
+    )
+    gc = gc.T[:heads]
+    gt = sums_ref[2 * heads : 3 * heads] * inside + cross * gc
+    gt = -scale * gt * inverse * inverse * active
+    gt_ref[...] = jnp.concatenate([gt, gc], axis=0)
     gt_ref.send()
-    weight = query_weight * gt * scale
-    vectors = [
-        jnp.sum(
-            q_ref[:, dk * h : dk * (h + 1)].astype(F32) * weight[:, h : h + 1], axis=0, keepdims=True
-        )
-        for h in range(heads)
-    ]
+    vectors = rows_times(query_weight * gt * scale, q_ref[...])
+    vectors = [vectors[h : h + 1, dk * h : dk * (h + 1)] for h in range(heads)]
     tile = jnp.concatenate(vectors + [jnp.zeros((8 - heads, 128), F32)], axis=0)
     tile_ref[...] = tile
-    tile_ref.send()
-    out_ref[:, :, dv:] = jnp.broadcast_to(tile[None], (count, 8, 128))
-
-    coef = coef_ref.ready()
-
-    def backward(i, state):
-        j = count - 1 - i
-        out_ref[j, :, :dv] = state
-        step = wide(coef, 1, j, reps) * got_ref[j, :, dv:]
-        return wide(coef, 0, j, reps) * state + step
-
-    lax.fori_loop(0, count, backward, jnp.zeros((8, dv), F32), unroll=8)
+    out_ref[:, 2 * reps] = jnp.broadcast_to(tile[None, :4], (count, 4, 128))
 
 
 def inner_kernel(
-    heads, scale, mem_ref, cols_ref, small_ref, gt_ref, wl_ref, pc_ref, gv_ref,
+    heads, scale, mem_ref, tokens_ref, small_ref, gt_ref, wl_ref, pc_ref, gv_ref,
     q_ref, k_ref, g_ref,
     gq_ref, gvalue_ref, gk_ref, row_ref, cold_ref,
 ):
     n = q_ref.shape[0]
     dk = q_ref.shape[1] // heads
     dv = g_ref.shape[1] // heads
-    gt, tokens = gt_ref[...], cols_ref[...]
-    gc = unpack(gt, 1, heads)
-    inside, cross, inverse, qn = (unpack(tokens, i, heads) for i in (0, 1, 2, 5))
+    tokens = column_of(jnp.concatenate([tokens_ref[...], gt_ref[...]], axis=0))
+    inside, cross, inverse, qn, gt, gc = (unpack(tokens, i, heads) for i in (0, 1, 2, 5, 6, 7))
     row_part = scale * cross * (inverse * gc + gt * qn)
     for h in range(heads):
         ks, vs = slice(dk * h, dk * (h + 1)), slice(dv * h, dv * (h + 1))
@@ -438,7 +469,7 @@
         gk_ref[:, ks] = scale * (dot(score_high, q, 0, 0) + dot(score_low, q, 0, 0))
         coupled = pc_ref[h] * (scale * inside[:, one] * inverse[:, one])
         gvalue_ref[:, vs] = dot_left(coupled, g, 0, 0)
-    row_ref[...] = row_part
+    row_ref[...] = row_part.T[:8]
     cold_ref[heads:, :] = jnp.zeros((8 - heads, n), F32)
 
 
@@ -448,9 +479,10 @@
 ):
     core = me_ref[0] % 2
     count, dv = mine_ref.shape[0], mine_ref.shape[2]
+    reps = dv // 128
     per_head = count // (heads // 2)
     vectors = [
-        jnp.sum(later_ref[:, h : h + 1] * got_ref[:, h, dv:], axis=0, keepdims=True)
+        jnp.sum(later_ref[:, h : h + 1] * got_ref[:, 2 * reps, h, :], axis=0, keepdims=True)
         for h in range(heads)
     ]
     tile = jnp.concatenate(vectors + [tile_ref[:heads]], axis=0)
@@ -462,7 +494,11 @@
         for i in range(heads // 2):
             at = core * (heads // 2) + i
             slab = slice(i * per_head, (i + 1) * per_head)
-            after = got_ref[slab, :, :dv]
+            after = [
+                jnp.concatenate([got_ref[slab, i * reps + c] for c in range(reps)], axis=2)
+                for i in range(2)
+            ]
+            after = jnp.concatenate(after, axis=1)
             to_odd_ref[slab] = after
             to_even_ref[slab] = pick(small[8:9], at) * after + pick(small[9:10], at) * odd[slab]
 
@@ -476,8 +512,8 @@
 
 
 def weights_kernel(
-    heads, me_ref, mine_ref, pair_ref, sum_ref, small_ref, cols_ref, k_ref, v_ref, mem_ref, row_ref,
-    cold_ref, rows_ref, x_ref,
+    heads, me_ref, mine_ref, pair_ref, sum_ref, small_ref, k_ref, v_ref, mem_ref, rows_ref, row_ref,
+    cold_ref, x_ref,
     after_ref, vector_ref, pay_ref,
 ):
     core = me_ref[0] % 2
@@ -489,9 +525,8 @@
     after_ref[pl.ds((1 - core) * count, count)] = pair_ref[:count]
     after_ref.send()
     mine, other = sum_ref[...], pair_ref[count, :, :128]
-    key_scale = jnp.exp(unpack(cols_ref[...], 1, heads) + small_ref[heads : heads + 1])
     column_cross = jnp.zeros((n, 128), F32)
-    through = jnp.zeros((1, 128), F32)
+    through = []
     vectors = []
     for h in range(heads):
         ks, vs, one = slice(dk * h, dk * (h + 1)), slice(dv * h, dv * (h + 1)), slice(h, h + 1)
@@ -504,21 +539,20 @@
         carried = dot_right(k_ref[:, ks], following, 1, 0)
         along = jnp.sum(v_ref[:, vs].astype(F32) * carried, axis=1, keepdims=True)
         along = along + jnp.sum(k_ref[:, ks].astype(F32) * vector, axis=1, keepdims=True)
-        column_cross = put(column_cross, key_scale[:, one] * along, h)
+        column_cross = put(column_cross, along, h)
         product = jnp.sum(mem_ref[slab].reshape(dk, dv) * following, axis=0, keepdims=True)
         product = jnp.sum(product, axis=1, keepdims=True)
         product = product + jnp.sum(small_ref[one] * vector, axis=1, keepdims=True)
-        through = put(through, product, h)
+        through.append(product)
     vector_ref[...] = jnp.concatenate(vectors + [jnp.zeros((8 - heads, 128), F32)], axis=0)
     vector_ref.send()
-    through = through * small_ref[heads + 1 : heads + 2]
-    row = row_ref[...].T[:8]
-    crossing = column_cross.T[:8]
-    passing = jnp.broadcast_to(through, (128, 128)).T[:8, :1]
-    inner = cold_ref[...]
+    passing = padded(jnp.concatenate(through, axis=0) * down(small_ref[heads + 1 : heads + 2], heads))
+    key_scale = jnp.exp(rows_ref[3 * heads : 4 * heads] + down(small_ref[heads : heads + 1], heads))
+    crossing = padded(column_cross.T[:heads] * key_scale)
+    row, inner = row_ref[...], cold_ref[...]
     after = iota((n, n), 0) >= iota((n, n), 1)
-    suffix = dot_exact(row - inner, after.astype(F32))
-    prefix = dot_exact(crossing, 1.0 - after.astype(F32))
+    suffix = times_ones(row - inner, after)
+    prefix = times_ones(crossing, jnp.logical_not(after))
     grad_log = suffix + prefix + passing
     grad_forget = grad_log[:heads] / (1.0 + jnp.exp(rows_ref[heads : 2 * heads, :]))
     coefs = jnp.concatenate([(inner + crossing)[:heads], grad_forget], axis=0)
@@ -526,19 +560,18 @@
     both = jnp.concatenate([high, coefs - high], axis=0).astype(BF16)
     product = dot(both, x_ref[...], 1, 0)
     result = product[: 2 * heads] + product[2 * heads :]
-    tiles = result.shape[1] // 128
+    tiles, _, width = pay_ref.shape
     for c in range(tiles):
-        pay_ref[c] = result[:heads, 128 * c : 128 * (c + 1)]
-        pay_ref[tiles + c] = result[heads:, 128 * c : 128 * (c + 1)]
+        pay_ref[c] = result[:, width * c : width * (c + 1)]
 
 
 def finish_kernel(
-    heads, after_ref, vector_ref, small_ref, cols_ref, gk_ref, gvalue_ref, k_ref, v_ref,
+    heads, after_ref, vector_ref, small_ref, rows_ref, gk_ref, gvalue_ref, k_ref, v_ref,
     gkey_ref, out_ref,
 ):
     dk = gk_ref.shape[1] // heads
     dv = v_ref.shape[1] // heads
-    key_scale = jnp.exp(unpack(cols_ref[...], 1, heads) + small_ref[heads : heads + 1])
+    key_scale = jnp.exp(unpack(column_of(rows_ref[...]), 3, heads) + small_ref[heads : heads + 1])
     for h in range(heads):
         ks, vs, one = slice(dk * h, dk * (h + 1)), slice(dv * h, dv * (h + 1)), slice(h, h + 1)
         following = after_ref[dk // 8 * h : dk // 8 * (h + 1)].reshape(dk, dv)
@@ -549,16 +582,18 @@
         out_ref[:, vs] = (gvalue_ref[:, vs] + key_scale[:, one] * carried).astype(BF16)
 
 
-def sum_kernel(got_ref, out_ref):
+def sum_kernel(got_ref, *refs):
+    out_ref = refs[-1]
     total = jnp.sum(got_ref[...], axis=0, keepdims=True)
     out_ref[...] = jnp.broadcast_to(total, out_ref.shape)
 
 
 def place_kernel(got_ref, first_ref, second_ref):
-    tiles = got_ref.shape[0] // 2
+    heads = first_ref.shape[0]
+    tiles, _, width = got_ref.shape
     for c in range(tiles):
-        first_ref[:, 128 * c : 128 * (c + 1)] = got_ref[c]
-        second_ref[:, 128 * c : 128 * (c + 1)] = got_ref[tiles + c]
+        first_ref[:, width * c : width * (c + 1)] = got_ref[c, :heads]
+        second_ref[:, width * c : width * (c + 1)] = got_ref[c, heads:]
 
 
 class Fetched:
@@ -645,15 +680,6 @@
     )(*[pltpu.with_memory_space_constraint(a, pltpu.HBM) if k in "hma" else a for k, a in ins])
 
 
-def pack(items, heads):
-    total = None
-    for i, x in enumerate(items):
-        x = jnp.where(iota(x.shape, 1) < heads, x, 0.0)
-        x = pltpu.roll(x, heads * i, 1) if i else x
-        total = x if total is None else total + x
-    return total
-
-
 def unpack(x, i, heads):
     return pltpu.roll(x, 128 - heads * i, 1) if i else x
 
@@ -674,7 +700,6 @@
     count = devices // 2
     me = lax.axis_index("ctx").astype(jnp.int32).reshape(1)
     part = functools.partial
-    cols = (n, 128)
     slabs = heads * dk // 8
     cores = [[2 * i + c for i in range(count)] for c in range(2)]
 
@@ -686,79 +711,87 @@
     def given(kinds, *arrays):
         return list(zip(kinds, arrays, strict=True))
 
-    give, memory, tile, rows, token_cols = call(
+    give, memory, tile, rows = call(
         part(gates_kernel, heads),
-        given("vvvhh", (slabs // 2 + 1, 8, dv), (slabs, 8, dv), (8, 128), (16, n), cols),
-        given("shhhmmhhh", me, x, w_input.T, w_forget.T, b_input, b_forget, doc_pos, k, v),
+        given("vvvh", (slabs // 2 + 1, 8, dv), (slabs, 8, dv), (8, 128), (24, n)),
+        given("shhmmhhhh", me, w_input.T, w_forget.T, b_input, b_forget, doc_pos, k, x, v),
     )
     pair = to_pair(give)
-    pay, even_memory, even_tile = call(
+    (pay,) = call(
         part(first_kernel, heads),
-        given("vhh", (count, 8, dv + 128), (count, 8, dv), (8, 128)),
+        given("v", (count, 8, dv + 128)),
         given("svvv", me, memory, tile, pair),
     )
     first = exchange(pay, "ctx", cores)
-    wl, pc, gv, sums = call(
+    even_memory, even_tile, turned, wl, pc, gv, sums = call(
         part(pairs_kernel, heads),
-        given("hhhh", *[(heads, n, n)] * 3, cols),
-        given("hhhhhh", rows, token_cols, q, k, v, g),
+        given(
+            "hvvhhhv", (count, 8, dv), (8, 128), low((heads * dk, n), BF16), *[(heads, n, n)] * 3, (16, n)
+        ),
+        given("svvvhhhhh", me, memory, tile, pair, rows, q, k, v, g),
     )
     give, dual, coef, now, coef_later, later, small, tokens = call(
         part(dual_kernel, heads, scale),
         given(
-            "vvvvhhhh", (count, 8, dv), (count, 8, dv), (2, count, 128), (16, 128),
-            (2, count, 128), (count, 128), (16, 128), cols,
+            "vvvvvvhh", (count, 8, dv), (count, 8, dv), (2, count, 128), (16, 128),
+            (2, count, 128), (count, 128), (16, 128), (24, n),
         ),
-        given("svhhhhh", me, first, even_tile, token_cols, sums, q, g),
+        given("svvhvvh", me, first, even_tile, rows, sums, turned, g),
     )
     pair = to_pair(give)
-    pay, odd_dual = call(
+    (pay,) = call(
         part(second_kernel, heads),
-        given("vh", (count, 8, 2 * dv), (count, 8, dv)),
+        given("v", (count, 8, 2 * dv)),
         given("svvvvv", me, first, coef, now, dual, pair),
     )
     second = exchange(pay, "ctx", cores)
+    (odd_dual,) = call(odd_kernel, given("h", (count, 8, dv)), given("svv", me, dual, pair))
     give, mine = call(
         part(halves_kernel, heads),
         given("vv", (count, 8, dv), (count, 8, dv)),
-        given("svhh", me, second, even_memory, small),
+        given("svvva", me, second, even_memory, now, odd_dual),
     )
     pair = to_pair(give)
     pay, states, tile, gt = call(
         part(vector_kernel, heads, scale),
-        given("vhhh", (count, 8, dv + 128), (slabs, 8, dv), (8, 128), cols),
-        given("svvvhhhhh", me, mine, pair, second, coef_later, tokens, sums, q, g),
+        given("vhvh", (count, 2 * dv // 128 + 1, 4, 128), (slabs, 8, dv), (8, 128), (8, n)),
+        given("svvvvvvvv", me, mine, pair, second, coef_later, tokens, sums, q, g),
     )
     third = exchange(pay, "ctx", cores)
     grad_q, gvalue, gk, row, cold = call(
         part(inner_kernel, heads, scale),
-        given("hhhhh", low(q.shape, BF16), v.shape, k.shape, cols, (8, n)),
+        given("hhhhh", low(q.shape, BF16), v.shape, k.shape, (8, n), (8, n)),
         given("hhhhhhhhhh", states, tokens, small, gt, wl, pc, gv, q, k, g),
     )
     give, mine, sums = call(
         part(after_kernel, heads),
         given("vvv", (count + 1, 8, dv), (count, 8, dv), (8, 128)),
-        given("svhhhha", me, third, later, small, odd_dual, tile, gk),
+        given("svvvhva", me, third, later, now, odd_dual, tile, gk),
     )
     pair = to_pair(give)
-    chunks = 2 * x.shape[1] // 128
+    batch, across_x = lax.axis_size("dp"), 4
+    tiles = batch * across_x
+    at = [[[(z * across_x + i) * 2 + c for i in range(across_x)] for c in range(2)] for z in range(count // across_x)]
+    planes = [[i * batch + d for i in row for d in range(batch)] for z in at for row in z]
+    lines = [[row[i] for z in at for row in z] for i in range(across_x)]
+    chunk = (8, x.shape[1] // tiles)
     following, vector, pay = call(
         part(weights_kernel, heads),
-        given("hhv", (slabs, 8, dv), (8, 128), (chunks, heads, 128)),
+        given("hhv", (slabs, 8, dv), (8, 128), (tiles, *chunk)),
         given(
-            "svvvhhhhhhhhh", me, mine, pair, sums, small, token_cols, k, v, states, row, cold, rows, x
+            "svvvvvvhhhhv", me, mine, pair, sums, now, k, v, states, rows, row, cold, x
         ),
     )
-    got = exchange(pay, "ctx")
+    got = exchange(pay, ("ctx", "dp"), planes)
     grad_k, grad_v = call(
         part(finish_kernel, heads),
         given("hh", low(k.shape, BF16), low(v.shape, BF16)),
-        given("hhhhhhhh", following, vector, small, token_cols, gk, gvalue, k, v),
-    )
-    (pay,) = call(sum_kernel, given("v", (lax.axis_size("dp"), heads, 128)), given("v", got))
-    got = exchange(pay, "dp")
-    (pay,) = call(sum_kernel, given("v", (devices, heads, 128)), given("v", got))
-    got = exchange(pay, "ctx")
+        given("hhhhhhhh", following, vector, small, rows, gk, gvalue, k, v),
+    )
+    (pay,) = call(sum_kernel, given("v", (len(lines[0]), *chunk)), given("va", got, grad_k))
+    got = exchange(pay, "ctx", lines)
+    (pay,) = call(sum_kernel, given("v", (tiles, *chunk)), given("v", got))
+    got = exchange(pay, ("ctx", "dp"), planes)
     first, second = call(
         place_kernel, given("vv", (heads, x.shape[1]), (heads, x.shape[1])), given("v", got)
     )

time: 140 us -> 129 us (0.921)
  blocking collectives: 44.3 us -> 23.7 us
  waiting for transfers between devices: 29.2 us -> 39 us
  Pallas kernels: 35.2 us -> 30.8 us
  starting transfers between devices: 30.2 us -> 33.7 us
    all_to_all x3 -> x2, blocking collectives: 44.3 us -> 23.7 us  [exchange(): return lax.all_to_all(x, axis, 0, 0, axis_index_groups=groups)]
    all_to_all x3 -> x4, waiting for transfers between devices: 24.5 us -> 34.3 us  [exchange(): return lax.all_to_all(x, axis, 0, 0, axis_index_groups=groups)]
    pallas_call x14 -> x15, Pallas kernels: 35.2 us -> 30.8 us  [call(): pl.pallas_call(kernel, out_shape=[pltpu.HBM(o.shape, o.dtype) if k == 'h'...]
    all_to_all x3 -> x4, starting transfers between devices: 19.5 us -> 23.1 us  [exchange(): return lax.all_to_all(x, axis, 0, 0, axis_index_groups=groups)]
  transfers between devices with their start and end apart: 7 -> 8, of which waited for: 7 -> 8; matrix products, arithmetic and copies ran while one was open for 0% -> 0% of each run, Pallas kernels for 10% -> 12%
where the time goes in v4:
time: 129 us; the launch traced here: 128 us
  waiting for transfers between devices  39 us (30%)
  starting transfers between devices  33.7 us (26%)
  Pallas kernels  30.8 us (24%)
  blocking collectives  23.7 us (18%)
    all_to_all x4, waiting for transfers between devices, exchange(): return lax.all_to_all(x, axis, 0, 0, axis_index_groups=groups)  34.3 us
    pallas_call x15, Pallas kernels, call(): pl.pallas_call(kernel, out_shape=[pltpu.HBM(o.shape, o.dtype) if k == 'h'...  30.8 us
    all_to_all x2, blocking collectives, exchange(): return lax.all_to_all(x, axis, 0, 0, axis_index_groups=groups)  23.7 us
    all_to_all x4, starting transfers between devices, exchange(): return lax.all_to_all(x, axis, 0, 0, axis_index_groups=groups)  23.1 us
    ppermute x4, starting transfers between devices, to_pair(): return lax.ppermute(a, 'ctx', [(i, i ^ 1) for i in range(devices)])  10.6 us
    ppermute x4, waiting for transfers between devices, to_pair(): return lax.ppermute(a, 'ctx', [(i, i ^ 1) for i in range(devices)])  4.67 us
  transfers between devices with their start and end apart: 8, of which 8 were waited for; matrix products, arithmetic and copies ran while one was open for 0% of the time, Pallas kernels for 12%

profile of v4, /device:TPU:1, one launch (start us, length us, event | category | flops | bytes accessed | tf_op | source)
XLA Modules:
  0.0 128.0 jit_solution(7974875687226421770)
XLA Ops:
  0.6 3.8 %shard_map.137 = (f32[33,8,256]{2,1,0:T(8,128)S(1)}, f32[64,8,256]{2,1,0:T(8,128)S(1)}, f32[8,128]{1,0:T(8,128)S(1)}, f32[24,256]{1,0:T(8,128)}) custom-call(s32[1]{0:T(128)} %bitcast.refs_0_, bf16[4,4096]{1,0:T(4,128)(2,1)} %bitcast.32, bf16[4,4096]{1,0:T(4,128)(2,1)} %bitcast.33, f32[4]{0:T(128)} %refs_3_.1, f32[4]{0:T(128)} %refs_4_.1, s32[1,256]{1,0:T(1,128)} %refs_5_.1, ...), custom_call_target="tpu_custom_call" | custom-call | tf_op jit(solution)/shard_map/pallas_call | solution.py:673
  4.4 3.4 %collective-permute-start = (f32[33,8,256]{2,1,0:T(8,128)S(1)}, f32[33,8,256]{2,1,0:T(8,128)S(1)}, u32[]{:S(2)}, u32[]{:S(2)}) collective-permute-start(f32[33,8,256]{2,1,0:T(8,128)S(1)} %get-tuple-element.47), channel_id=1, source_target_pairs={{0,4},{4,0},{8,12},{12,8},{16,20},{20,16},{24,28},{28,24},{32,36},... | collective-permute-start | bytes 811016 | tf_op jit(solution)/shard_map/ppermute | solution.py:707
  7.8 1.2 collective-permute-done.refs_3_
  8.9 0.9 shard_map.138
  9.8 9.3 %all-to-all-start = ((f32[32,8,384]{2,1,0:T(8,128)}), f32[32,8,384]{2,1,0:T(8,128)S(1)}, u32[]{:S(2)}, u32[]{:S(2)}) async-start(f32[32,8,384]{2,1,0:T(8,128)} %shard_map.138), calls=%async_computation | async-start | bytes 786432 | tf_op jit(solution)/shard_map/all_to_all | solution.py:688
  19.2 4.4 %shard_map.139 = (f32[32,8,256]{2,1,0:T(8,128)}, f32[8,128]{1,0:T(8,128)S(1)}, bf16[512,256]{1,0:T(8,128)(2,1)S(1)}, f32[4,256,256]{2,1,0:T(8,128)}, f32[4,256,2...) custom-call(s32[1]{0:T(128)} %bitcast.refs_0_, f32[64,8,256]{2,1,0:T(8,128)S(1)} %get-tuple-element.45.refs_1_, ...), custom_call_target="tpu_custom_call" | custom-call | tf_op jit(solution)/shard_map/pallas_call | solution.py:673
  23.5 9.5 %all-to-all-done.refs_1_ = f32[32,8,384]{2,1,0:T(8,128)S(1)} async-done(((f32[32,8,384]{2,1,0:T(8,128)}), f32[32,8,384]{2,1,0:T(8,128)S(1)}, u32[]{:S(2)}, u32[]{:S(2)}) %all-to-all-start) | async-done | bytes 393248 | tf_op jit(solution)/shard_map/all_to_all | solution.py:688
  33.0 2.5 %shard_map.140 = (f32[32,8,256]{2,1,0:T(8,128)S(1)}, f32[32,8,256]{2,1,0:T(8,128)S(1)}, f32[2,32,128]{2,1,0:T(8,128)S(1)}, f32[16,128]{1,0:T(8,128)S(1)}, f32[2,...) custom-call(s32[1]{0:T(128)} %bitcast.refs_0_, ...), custom_call_target="tpu_custom_call" | custom-call | tf_op jit(solution)/shard_map/pallas_call | solution.py:673
  35.6 2.4 %collective-permute-start.1 = (f32[32,8,256]{2,1,0:T(8,128)S(1)}, f32[32,8,256]{2,1,0:T(8,128)S(1)}, u32[]{:S(2)}, u32[]{:S(2)}) collective-permute-start(f32[32,8,256]{2,1,0:T(8,128)S(1)} %get-tuple-element.55), channel_id=1, source_target_pairs={{0,4},{4,0},{8,12},{12,8},{16,20},{20,16},{24,28},{28,24},{32,36},... | collective-permute-start | bytes 786440 | tf_op jit(solution)/shard_map/ppermute | solution.py:707
  38.0 1.2 collective-permute-done.1.refs_5_.refs_2_
  39.2 1.0 shard_map.141
  40.2 4.0 %all-to-all-start.1 = ((f32[32,8,512]{2,1,0:T(8,128)}), f32[32,8,512]{2,1,0:T(8,128)S(1)}, u32[]{:S(2)}, u32[]{:S(2)}) async-start(f32[32,8,512]{2,1,0:T(8,128)} %shard_map.141), calls=%async_computation.1 | async-start | bytes 1048576 | tf_op jit(solution)/shard_map/all_to_all | solution.py:688
  44.3 0.8 shard_map.142.refs_4_
  45.0 15.8 %all-to-all-done.1.refs_1_.refs_3_ = f32[32,8,512]{2,1,0:T(8,128)S(1)} async-done(((f32[32,8,512]{2,1,0:T(8,128)}), f32[32,8,512]{2,1,0:T(8,128)S(1)}, u32[]{:S(2)}, u32[]{:S(2)}) %all-to-all-start.1) | async-done | bytes 524320 | tf_op jit(solution)/shard_map/all_to_all | solution.py:688
  60.9 0.1 shard_map.143
  61.0 2.3 %collective-permute-start.2 = (f32[32,8,256]{2,1,0:T(8,128)S(1)}, f32[32,8,256]{2,1,0:T(8,128)S(1)}, u32[]{:S(2)}, u32[]{:S(2)}) collective-permute-start(f32[32,8,256]{2,1,0:T(8,128)S(1)} %get-tuple-element.58), channel_id=1, source_target_pairs={{0,4},{4,0},{8,12},{12,8},{16,20},{20,16},{24,28},{28,24},{32,36},... | collective-permute-start | bytes 786440 | tf_op jit(solution)/shard_map/ppermute | solution.py:707
  63.3 1.2 collective-permute-done.2.refs_2_
  64.4 2.0 %shard_map.144 = (f32[32,5,4,128]{3,2,1,0:T(4,128)}, f32[64,8,256]{2,1,0:T(8,128)}, f32[8,128]{1,0:T(8,128)S(1)}, f32[8,256]{1,0:T(8,128)}) custom-call(s32[1]{0:T(128)} %bitcast.refs_0_, f32[32,8,256]{2,1,0:T(8,128)S(1)} %get-tuple-element.57.refs_1_, f32[32,8,256]{2,1,0:T(8,128)S(1)} %collective-permute-done.2.refs_2_, ...), custom_call_target="tpu_custom_call" | custom-call | tf_op jit(solution)/shard_map/pallas_call | solution.py:673
  66.5 4.3 %all-to-all-start.2 = ((f32[32,5,4,128]{3,2,1,0:T(4,128)}), f32[32,5,4,128]{3,2,1,0:T(4,128)S(1)}, u32[]{:S(2)}, u32[]{:S(2)}) async-start(f32[32,5,4,128]{3,2,1,0:T(4,128)} %get-tuple-element.68), calls=%async_computation.2 | async-start | bytes 655360 | tf_op jit(solution)/shard_map/all_to_all | solution.py:688
  70.8 0.0 copy-start.3
  70.8 6.4 %shard_map.145 = (bf16[256,512]{1,0:T(8,128)(2,1)}, f32[256,1024]{1,0:T(8,128)}, f32[256,512]{1,0:T(8,128)}, f32[8,256]{1,0:T(8,128)}, f32[8,256]{1,0:T(8,128)}) custom-call(f32[64,8,256]{2,1,0:T(8,128)} %get-tuple-element.61.refs_0_.refs_7_, f32[24,256]{1,0:T(8,128)} %get-tuple-element.60.refs_5_.refs_1_, f32[16,128]{1,0:T(8,128)} %get-tuple-element.62.refs_2_, ...), custom_call_target="tpu_custom_call" | custom-call | tf_op jit(solution)/shard_map/pallas_call | solution.py:673
  77.2 6.3 %all-to-all-done.2.refs_1_ = f32[32,5,4,128]{3,2,1,0:T(4,128)S(1)} async-done(((f32[32,5,4,128]{3,2,1,0:T(4,128)}), f32[32,5,4,128]{3,2,1,0:T(4,128)S(1)}, u32[]{:S(2)}, u32[]{:S(2)}) %all-to-all-start.2) | async-done | bytes 327712 | tf_op jit(solution)/shard_map/all_to_all | solution.py:688
  83.6 1.1 shard_map.146
  84.7 2.5 %collective-permute-start.3 = (f32[33,8,256]{2,1,0:T(8,128)S(1)}, f32[33,8,256]{2,1,0:T(8,128)S(1)}, u32[]{:S(2)}, u32[]{:S(2)}) collective-permute-start(f32[33,8,256]{2,1,0:T(8,128)S(1)} %get-tuple-element.73), channel_id=1, source_target_pairs={{0,4},{4,0},{8,12},{12,8},{16,20},{20,16},{24,28},{28,24},{32,36},... | collective-permute-start | bytes 811016 | tf_op jit(solution)/shard_map/ppermute | solution.py:707
  87.2 1.2 collective-permute-done.3.refs_2_
  88.3 3.1 %shard_map.147 = (f32[64,8,256]{2,1,0:T(8,128)}, f32[8,128]{1,0:T(8,128)}, f32[16,8,256]{2,1,0:T(8,128)}) custom-call(s32[1]{0:T(128)} %bitcast.refs_0_, f32[32,8,256]{2,1,0:T(8,128)S(1)} %get-tuple-element.72.refs_1_, f32[33,8,256]{2,1,0:T(8,128)S(1)} %collective-permute-done.3.refs_2_, f32[8,128]{1,0:T(8,128)S(1)} %get-tuple-element.74.refs_3_, ...), custom_call_target="tpu_custom_call" | custom-call | tf_op jit(solution)/shard_map/pallas_call | solution.py:673
  91.4 5.4 %all-to-all-start.3 = ((f32[16,8,256]{2,1,0:T(8,128)}), f32[16,8,256]{2,1,0:T(8,128)S(1)}, u32[]{:S(2)}, u32[]{:S(2)}) async-start(f32[16,8,256]{2,1,0:T(8,128)} %get-tuple-element.82), calls=%async_computation.3 | async-start | bytes 262144 | tf_op jit(solution)/shard_map/all_to_all | solution.py:688
  96.9 4.0 %shard_map.148 = (bf16[256,512]{1,0:T(8,128)(2,1)}, bf16[256,1024]{1,0:T(8,128)(2,1)}) custom-call(f32[64,8,256]{2,1,0:T(8,128)} %get-tuple-element.77.refs_0_, f32[8,128]{1,0:T(8,128)} %get-tuple-element.78.refs_1_, f32[16,128]{1,0:T(8,128)} %get-tuple-element.62.refs_2_, f32[24,256]{1,0:T(8,128)} %get-tuple-element.48.refs_4_.refs_3_.refs_8_, ...), custom_call_target="tpu_custom_call" | custom-call | tf_op jit(solution)/shard_map/pallas_call | solution.py:673
  100.9 2.7 %all-to-all-done.3.refs_0_ = f32[16,8,256]{2,1,0:T(8,128)S(1)} async-done(((f32[16,8,256]{2,1,0:T(8,128)}), f32[16,8,256]{2,1,0:T(8,128)S(1)}, u32[]{:S(2)}, u32[]{:S(2)}) %all-to-all-start.3) | async-done | bytes 131104 | tf_op jit(solution)/shard_map/all_to_all | solution.py:688
  103.6 13.4 %all_to_all.30.refs_0_ = f32[16,8,256]{2,1,0:T(8,128)S(1)} all-to-all(f32[16,8,256]{2,1,0:T(8,128)S(1)} %shard_map.149), channel_id=1, replica_groups={{0,4,32,36,64,68,96,100,128,132,160,164,192,196,224,228},{8,12,40,44,72..., dimensions={0} | all-to-all | bytes 262144 | tf_op jit(solution)/shard_map/all_to_all | solution.py:688
  117.1 10.2 %all_to_all.31.refs_0_ = f32[16,8,256]{2,1,0:T(8,128)S(1)} all-to-all(f32[16,8,256]{2,1,0:T(8,128)S(1)} %shard_map.150), channel_id=1, replica_groups={{0,1,2,3,8,9,10,11,16,17,18,19,24,25,26,27},{4,5,6,7,12,13,14,15,20,21,..., dimensions={0} | all-to-all | bytes 262144 | tf_op jit(solution)/shard_map/all_to_all | solution.py:688
  127.3 0.7 shard_map.151
  (15 shorter events, 0.1 us)
Async XLA Ops:
  4.4 4.5 %collective-permute-start = (f32[33,8,256]{2,1,0:T(8,128)S(1)}, f32[33,8,256]{2,1,0:T(8,128)S(1)}, u32[]{:S(2)}, u32[]{:S(2)}) collective-permute-start(f32[33,8,256]{2,1,0:T(8,128)S(1)} %get-tuple-element.47), channel_id=1, source_target_pairs={{0,4},{4,0},{8,12},{12,8},{16,20},{20,16},{24,28},{28,24},{32,36},... | collective-permute-start | bytes 811016 | tf_op jit(solution)/shard_map/ppermute | solution.py:707
  9.8 23.2 %all-to-all-start = ((f32[32,8,384]{2,1,0:T(8,128)}), f32[32,8,384]{2,1,0:T(8,128)S(1)}, u32[]{:S(2)}, u32[]{:S(2)}) async-start(f32[32,8,384]{2,1,0:T(8,128)} %shard_map.138), calls=%async_computation | async-start | bytes 786432 | tf_op jit(solution)/shard_map/all_to_all | solution.py:688
  33.0 27.8 %copy-start.5 = (f32[32,8,256]{2,1,0:T(8,128)S(1)}, f32[32,8,256]{2,1,0:T(8,128)}, u32[]{:S(2)}) copy-start(f32[32,8,256]{2,1,0:T(8,128)} %get-tuple-element.56.refs_2_) | copy-start | bytes 786436
  35.6 3.6 %collective-permute-start.1 = (f32[32,8,256]{2,1,0:T(8,128)S(1)}, f32[32,8,256]{2,1,0:T(8,128)S(1)}, u32[]{:S(2)}, u32[]{:S(2)}) collective-permute-start(f32[32,8,256]{2,1,0:T(8,128)S(1)} %get-tuple-element.55), channel_id=1, source_target_pairs={{0,4},{4,0},{8,12},{12,8},{16,20},{20,16},{24,28},{28,24},{32,36},... | collective-permute-start | bytes 786440 | tf_op jit(solution)/shard_map/ppermute | solution.py:707
  39.2 25.2 %copy-start.1 = (bf16[1,256,1024]{2,1,0:T(8,128)(2,1)S(1)}, bf16[1,256,1024]{2,1,0:T(8,128)(2,1)}, u32[]{:S(2)}) copy-start(bf16[1,256,1024]{2,1,0:T(8,128)(2,1)} %param.14) | copy-start | bytes 1572868
  39.2 25.2 %copy-start.4 = (bf16[1,256,512]{2,1,0:T(8,128)(2,1)S(1)}, bf16[1,256,512]{2,1,0:T(8,128)(2,1)}, u32[]{:S(2)}) copy-start(bf16[1,256,512]{2,1,0:T(8,128)(2,1)} %param.11) | copy-start | bytes 786436
  39.2 25.2 %copy-start.6 = (f32[24,256]{1,0:T(8,128)S(1)}, f32[24,256]{1,0:T(8,128)}, u32[]{:S(2)}) copy-start(f32[24,256]{1,0:T(8,128)} %get-tuple-element.60.refs_5_.refs_1_) | copy-start | bytes 73732
  40.2 20.6 %all-to-all-start.1 = ((f32[32,8,512]{2,1,0:T(8,128)}), f32[32,8,512]{2,1,0:T(8,128)S(1)}, u32[]{:S(2)}, u32[]{:S(2)}) async-start(f32[32,8,512]{2,1,0:T(8,128)} %shard_map.141), calls=%async_computation.1 | async-start | bytes 1048576 | tf_op jit(solution)/shard_map/all_to_all | solution.py:688
  61.0 3.4 %collective-permute-start.2 = (f32[32,8,256]{2,1,0:T(8,128)S(1)}, f32[32,8,256]{2,1,0:T(8,128)S(1)}, u32[]{:S(2)}, u32[]{:S(2)}) collective-permute-start(f32[32,8,256]{2,1,0:T(8,128)S(1)} %get-tuple-element.58), channel_id=1, source_target_pairs={{0,4},{4,0},{8,12},{12,8},{16,20},{20,16},{24,28},{28,24},{32,36},... | collective-permute-start | bytes 786440 | tf_op jit(solution)/shard_map/ppermute | solution.py:707
  66.5 17.1 %all-to-all-start.2 = ((f32[32,5,4,128]{3,2,1,0:T(4,128)}), f32[32,5,4,128]{3,2,1,0:T(4,128)S(1)}, u32[]{:S(2)}, u32[]{:S(2)}) async-start(f32[32,5,4,128]{3,2,1,0:T(4,128)} %get-tuple-element.68), calls=%async_computation.2 | async-start | bytes 655360 | tf_op jit(solution)/shard_map/all_to_all | solution.py:688
  70.8 17.5 %copy-start = (bf16[1,256,4096]{2,1,0:T(8,128)(2,1)S(1)}, bf16[1,256,4096]{2,1,0:T(8,128)(2,1)}, u32[]{:S(2)}) copy-start(bf16[1,256,4096]{2,1,0:T(8,128)(2,1)} %param.10) | copy-start | bytes 6291460
  70.8 17.5 %copy-start.2 = (bf16[1,256,1024]{2,1,0:T(8,128)(2,1)S(1)}, bf16[1,256,1024]{2,1,0:T(8,128)(2,1)}, u32[]{:S(2)}) copy-start(bf16[1,256,1024]{2,1,0:T(8,128)(2,1)} %param.13) | copy-start | bytes 1572868
  70.8 17.5 %copy-start.3 = (bf16[1,256,512]{2,1,0:T(8,128)(2,1)S(1)}, bf16[1,256,512]{2,1,0:T(8,128)(2,1)}, u32[]{:S(2)}) copy-start(bf16[1,256,512]{2,1,0:T(8,128)(2,1)} %param.12) | copy-start | bytes 786436
  84.7 3.7 %collective-permute-start.3 = (f32[33,8,256]{2,1,0:T(8,128)S(1)}, f32[33,8,256]{2,1,0:T(8,128)S(1)}, u32[]{:S(2)}, u32[]{:S(2)}) collective-permute-start(f32[33,8,256]{2,1,0:T(8,128)S(1)} %get-tuple-element.73), channel_id=1, source_target_pairs={{0,4},{4,0},{8,12},{12,8},{16,20},{20,16},{24,28},{28,24},{32,36},... | collective-permute-start | bytes 811016 | tf_op jit(solution)/shard_map/ppermute | solution.py:707
  91.4 12.1 %all-to-all-start.3 = ((f32[16,8,256]{2,1,0:T(8,128)}), f32[16,8,256]{2,1,0:T(8,128)S(1)}, u32[]{:S(2)}, u32[]{:S(2)}) async-start(f32[16,8,256]{2,1,0:T(8,128)} %get-tuple-element.82), calls=%async_computation.3 | async-start | bytes 262144 | tf_op jit(solution)/shard_map/all_to_all | solution.py:688

commit v5 on v4

--- a/solution.py
+++ b/solution.py
@@ -86,9 +86,25 @@
     return jnp.sum(jnp.where(iota(row.shape, 1) == lane, row, 0.0), axis=1, keepdims=True)
 
 
+def outer_products(side, heads, turned_ref, rows_ref, columns, out_ref):
+    half = heads // 2
+    dk, dv = turned_ref.shape[0] // heads, rows_ref.shape[1] // heads
+    columns = jnp.where(side == 0, columns, pltpu.roll(columns, 128 - half, 1))
+    for i in range(half):
+        at = pl.multiple_of((side * half + i) * dv, dv)
+        weighted = rows_ref[:, pl.ds(at, dv)].astype(F32) * columns[:, i : i + 1]
+        at = pl.multiple_of((side * half + i) * dk, dk)
+        product = dot_right(turned_ref[pl.ds(at, dk), :], weighted, 1, 0)
+        out_ref[dk // 8 * i : dk // 8 * (i + 1)] = product.reshape(dk // 8, 8, dv)
+
+
+def products_kernel(heads, me_ref, turned_ref, rows_ref, column_ref, out_ref):
+    outer_products(me_ref[0] % 2, heads, turned_ref, rows_ref, column_ref[...], out_ref)
+
+
 def gates_kernel(
     heads, me_ref, wi_ref, wf_ref, bi_ref, bf_ref, pos_ref, k_ref, x_ref, v_ref,
-    give_ref, mem_ref, tile_ref, rows_ref,
+    give_ref, turned_ref, column_ref, tile_ref, rows_ref,
 ):
     core = me_ref[0] % 2
     n = x_ref.shape[0]
@@ -121,10 +137,10 @@
     weight = jnp.exp(key_log - own_max)
     sums = rows_times(weight, k)
     column = column_of(weight)
-    for h in range(heads):
-        weighted = v_ref[:, dv * h : dv * (h + 1)].astype(F32) * column[:, h : h + 1]
-        memory = dot_right(turned[dk * h : dk * (h + 1)], weighted, 1, 0)
-        mem_ref[dk // 8 * h : dk // 8 * (h + 1)] = memory.reshape(dk // 8, 8, dv)
+    column_ref[...] = column
+    turned_ref[...] = turned
+    half = give_ref.shape[0] - 1
+    outer_products(1 - core, heads, turned_ref, v_ref, column, give_ref)
     cut = jnp.where(last > 0.5, BIG, 0.0)
     tile = jnp.concatenate(
         [sums[h : h + 1, dk * h : dk * (h + 1)] for h in range(heads)]
@@ -133,8 +149,6 @@
         axis=0,
     )
     tile_ref[...] = tile
-    half = mem_ref.shape[0] // 2
-    give_ref[:half] = mem_ref[pl.ds((1 - core) * half, half)]
     give_ref[half] = jnp.concatenate([tile, jnp.zeros((8, dv - 128), F32)], axis=1)
 
 
@@ -160,7 +174,7 @@
     for i in range(heads // 2):
         at = core * (heads // 2) + i
         slab = slice(i * per_head, (i + 1) * per_head)
-        own = mem_ref[pl.ds(core * half + i * per_head, per_head)]
+        own = mem_ref[slab]
         out_ref[slab, :, :dv] = pick(weight_mine, at) * own + pick(weight_other, at) * got_ref[slab]
 
 
@@ -170,7 +184,7 @@
 ):
     core = me_ref[0] % 2
     half = even_ref.shape[0]
-    even_ref[...] = jnp.where(core == 0, mem_ref[pl.ds(core * half, half)], got_ref[:half])
+    even_ref[...] = jnp.where(core == 0, mem_ref[...], got_ref[:half])
     even_ref.send()
     even_tile_ref[...] = jnp.where(core == 0, tile_ref[...], got_ref[half, :, :128])
     n = q_ref.shape[0]
@@ -210,7 +224,7 @@
 
 def dual_kernel(
     heads, scale, me_ref, got_ref, tile_ref, rows_ref, sums_ref, turned_ref, g_ref,
-    give_ref, dual_ref, coef_ref, now_ref, coef_later_ref, later_ref, small_ref, tokens_ref,
+    give_ref, column_ref, coef_ref, now_ref, coef_later_ref, later_ref, small_ref, tokens_ref,
 ):
     count = got_ref.shape[0]
     n = g_ref.shape[0]
@@ -322,38 +336,32 @@
     tokens_ref[...] = jnp.concatenate([inside, cross, inverse, active, query_weight, qn], axis=0)
     tokens_ref.send()
     grad_weight = column_of(query_weight * inverse * scale)
-    half = give_ref.shape[0]
-    per_head = dk // 8
-    for h in range(heads):
-        weighted = g_ref[:, dv * h : dv * (h + 1)].astype(F32) * grad_weight[:, h : h + 1]
-        memory = dot_right(turned_ref[dk * h : dk * (h + 1)], weighted, 1, 0).reshape(per_head, 8, dv)
-        slab = slice(per_head * h % half, per_head * h % half + per_head)
-
-        @pl.when(core == h // (heads // 2))
-        def _():
-            dual_ref[slab] = memory
-
-        @pl.when(core != h // (heads // 2))
-        def _():
-            give_ref[slab] = memory
+    column_ref[...] = grad_weight
+    outer_products(1 - core, heads, turned_ref, g_ref, grad_weight, give_ref)
 
 
 def wide(coef_ref, i, j, reps):
     return jnp.concatenate([coef_ref[i, pl.ds(j, 1), :]] * reps, axis=1)
 
 
-def second_kernel(
-    heads, me_ref, got_ref, coef_ref, small_ref, dual_ref, pair_ref, out_ref
-):
-    core = me_ref[0] % 2
-    count, dv = got_ref.shape[0], dual_ref.shape[2]
+def before_kernel(got_ref, coef_ref, out_ref):
+    count, _, dv = out_ref.shape
     reps = dv // 128
 
     def forward(j, state):
-        out_ref[j, :, :dv] = state
+        out_ref[j] = state
         step = wide(coef_ref, 1, j, reps) * got_ref[j, :, :dv]
         return wide(coef_ref, 0, j, reps) * state + step
 
+    lax.fori_loop(0, count, forward, jnp.zeros((8, dv), F32), unroll=8)
+
+
+def second_kernel(heads, me_ref, before_ref, small_ref, dual_ref, pair_ref, out_ref, odd_ref):
+    core = me_ref[0] % 2
+    count, _, dv = dual_ref.shape
+    odd_ref[...] = jnp.where(core == 0, pair_ref[...], dual_ref[...])
+    odd_ref.send()
+    out_ref[:, :, :dv] = before_ref[...]
     even, odd = small_ref[10:11], small_ref[11:12]
     weight_mine = jnp.where(core == 0, even, odd)
     weight_other = jnp.where(core == 0, odd, even)
@@ -363,14 +371,9 @@
         slab = slice(i * per_head, (i + 1) * per_head)
         step = pick(weight_other, at) * pair_ref[slab]
         out_ref[slab, :, dv:] = pick(weight_mine, at) * dual_ref[slab] + step
-    lax.fori_loop(0, count, forward, jnp.zeros((8, dv), F32), unroll=8)
-
-
-def odd_kernel(me_ref, dual_ref, pair_ref, odd_ref):
-    odd_ref[...] = jnp.where(me_ref[0] % 2 == 0, pair_ref[...], dual_ref[...])
-
-
-def halves_kernel(heads, me_ref, got_ref, even_ref, small_ref, unused_ref, give_ref, mine_ref):
+
+
+def halves_kernel(heads, me_ref, got_ref, even_ref, small_ref, give_ref, mine_ref):
     core = me_ref[0] % 2
     count, dv = give_ref.shape[0], give_ref.shape[2]
     per_head = count // (heads // 2)
@@ -393,36 +396,51 @@
         fill(give_ref, mine_ref)
 
 
-def vector_kernel(
-    heads, scale, me_ref, mine_ref, pair_ref, got_ref, coef_ref, tokens_ref, sums_ref, q_ref, g_ref,
-    out_ref, mem_ref, tile_ref, gt_ref,
-):
-    core = me_ref[0] % 2
-    n = q_ref.shape[0]
-    dk = q_ref.shape[1] // heads
-    dv = g_ref.shape[1] // heads
-    count = got_ref.shape[0]
+def crossings(side, heads, memory_ref, q_ref, g_ref):
+    half = heads // 2
+    n, dk, dv = q_ref.shape[0], q_ref.shape[1] // heads, g_ref.shape[1] // heads
+    result = jnp.zeros((n, 128), F32)
+    for i in range(half):
+        memory = memory_ref[dk // 8 * i : dk // 8 * (i + 1)].reshape(dk, dv)
+        at = pl.multiple_of((side * half + i) * dk, dk)
+        crossing = dot_right(q_ref[:, pl.ds(at, dk)], memory, 1, 0)
+        at = pl.multiple_of((side * half + i) * dv, dv)
+        along = g_ref[:, pl.ds(at, dv)].astype(F32) * crossing
+        result = put(result, jnp.sum(along, axis=1, keepdims=True), i)
+    return result
+
+
+def merged(core, heads, mine, other):
+    half = heads // 2
+    first = jnp.where(core == 0, mine, other)
+    return first + pltpu.roll(jnp.where(core == 0, other, mine), half, 1)
+
+
+def mine_kernel(heads, me_ref, mine_ref, got_ref, coef_ref, q_ref, g_ref, out_ref, gc_ref):
+    count, dv = mine_ref.shape[0], mine_ref.shape[2]
     reps = dv // 128
-    mem_ref[pl.ds(core * count, count)] = mine_ref[...]
-    mem_ref[pl.ds((1 - core) * count, count)] = pair_ref[...]
-    mem_ref.send()
-    coef = coef_ref
 
     def backward(i, state):
         j = count - 1 - i
         for i in range(2):
             for c in range(reps):
                 out_ref[j, i * reps + c] = state[4 * i : 4 * (i + 1), 128 * c : 128 * (c + 1)]
-        step = wide(coef, 1, j, reps) * got_ref[j, :, dv:]
-        return wide(coef, 0, j, reps) * state + step
+        step = wide(coef_ref, 1, j, reps) * got_ref[j, :, dv:]
+        return wide(coef_ref, 0, j, reps) * state + step
 
     lax.fori_loop(0, count, backward, jnp.zeros((8, dv), F32), unroll=8)
-    gc = jnp.zeros((n, 128), F32)
-    for h in range(heads):
-        memory = mem_ref[dk // 8 * h : dk // 8 * (h + 1)].reshape(dk, dv)
-        crossing = dot_right(q_ref[:, dk * h : dk * (h + 1)], memory, 1, 0)
-        along = g_ref[:, dv * h : dv * (h + 1)].astype(F32) * crossing
-        gc = put(gc, jnp.sum(along, axis=1, keepdims=True), h)
+    gc_ref[...] = crossings(me_ref[0] % 2, heads, mine_ref, q_ref, g_ref)
+
+
+def vector_kernel(
+    heads, scale, me_ref, mine_ref, pair_ref, after_ref, crossing_ref, tokens_ref, sums_ref, q_ref, g_ref,
+    out_ref, tile_ref, gt_ref,
+):
+    core = me_ref[0] % 2
+    dk = q_ref.shape[1] // heads
+    count, pieces = mine_ref.shape[0], after_ref.shape[1]
+    out_ref[:, :pieces] = after_ref[...]
+    gc = merged(core, heads, crossing_ref[...], crossings(1 - core, heads, pair_ref, q_ref, g_ref))
     inside, cross, inverse, active, query_weight = (
         tokens_ref[heads * i : heads * (i + 1)] for i in range(5)
     )
@@ -430,19 +448,22 @@
     gt = sums_ref[2 * heads : 3 * heads] * inside + cross * gc
     gt = -scale * gt * inverse * inverse * active
     gt_ref[...] = jnp.concatenate([gt, gc], axis=0)
-    gt_ref.send()
     vectors = rows_times(query_weight * gt * scale, q_ref[...])
     vectors = [vectors[h : h + 1, dk * h : dk * (h + 1)] for h in range(heads)]
     tile = jnp.concatenate(vectors + [jnp.zeros((8 - heads, 128), F32)], axis=0)
     tile_ref[...] = tile
-    out_ref[:, 2 * reps] = jnp.broadcast_to(tile[None, :4], (count, 4, 128))
+    out_ref[:, pieces] = jnp.broadcast_to(tile[None, :4], (count, 4, 128))
 
 
 def inner_kernel(
-    heads, scale, mem_ref, tokens_ref, small_ref, gt_ref, wl_ref, pc_ref, gv_ref,
+    heads, scale, me_ref, mine_ref, pair_ref, gt_ref, tokens_ref, small_ref, wl_ref, pc_ref, gv_ref,
     q_ref, k_ref, g_ref,
-    gq_ref, gvalue_ref, gk_ref, row_ref, cold_ref,
+    mem_ref, gq_ref, gvalue_ref, gk_ref, row_ref, cold_ref,
 ):
+    core, count = me_ref[0] % 2, mine_ref.shape[0]
+    mem_ref[pl.ds(core * count, count)] = mine_ref[...]
+    mem_ref[pl.ds((1 - core) * count, count)] = pair_ref[...]
+    mem_ref.send()
     n = q_ref.shape[0]
     dk = q_ref.shape[1] // heads
     dv = g_ref.shape[1] // heads
@@ -511,9 +532,27 @@
         fill(give_ref, mine_ref)
 
 
+def alongs(side, heads, after_ref, k_ref, v_ref):
+    half = heads // 2
+    n, dk, dv = k_ref.shape[0], k_ref.shape[1] // heads, v_ref.shape[1] // heads
+    result = jnp.zeros((n, 128), F32)
+    for i in range(half):
+        following = after_ref[dk // 8 * i : dk // 8 * (i + 1)].reshape(dk, dv)
+        at = pl.multiple_of((side * half + i) * dk, dk)
+        carried = dot_right(k_ref[:, pl.ds(at, dk)], following, 1, 0)
+        at = pl.multiple_of((side * half + i) * dv, dv)
+        along = v_ref[:, pl.ds(at, dv)].astype(F32) * carried
+        result = put(result, jnp.sum(along, axis=1, keepdims=True), i)
+    return result
+
+
+def along_kernel(heads, me_ref, mine_ref, k_ref, v_ref, out_ref):
+    out_ref[...] = alongs(me_ref[0] % 2, heads, mine_ref, k_ref, v_ref)
+
+
 def weights_kernel(
-    heads, me_ref, mine_ref, pair_ref, sum_ref, small_ref, k_ref, v_ref, mem_ref, rows_ref, row_ref,
-    cold_ref, x_ref,
+    heads, me_ref, mine_ref, pair_ref, sum_ref, along_ref, small_ref, k_ref, v_ref, mem_ref, rows_ref,
+    row_ref, cold_ref, x_ref,
     after_ref, vector_ref, pay_ref,
 ):
     core = me_ref[0] % 2
@@ -525,21 +564,21 @@
     after_ref[pl.ds((1 - core) * count, count)] = pair_ref[:count]
     after_ref.send()
     mine, other = sum_ref[...], pair_ref[count, :, :128]
-    column_cross = jnp.zeros((n, 128), F32)
+    column_cross = merged(
+        core, heads, along_ref[...], alongs(1 - core, heads, pair_ref, k_ref, v_ref)
+    )
     through = []
     vectors = []
     for h in range(heads):
-        ks, vs, one = slice(dk * h, dk * (h + 1)), slice(dv * h, dv * (h + 1)), slice(h, h + 1)
+        ks, one = slice(dk * h, dk * (h + 1)), slice(h, h + 1)
         slab = slice(dk // 8 * h, dk // 8 * (h + 1))
         odd = mine[one] + other[one]
         even = small_ref[8:9, one] * odd + small_ref[9:10, one] * other[heads + h : heads + h + 1]
         vector = jnp.where(core == 0, even, odd)
         vectors.append(vector)
+        along = jnp.sum(k_ref[:, ks].astype(F32) * vector, axis=1, keepdims=True)
+        column_cross = column_cross + put(jnp.zeros((n, 128), F32), along, h)
         following = after_ref[slab].reshape(dk, dv)
-        carried = dot_right(k_ref[:, ks], following, 1, 0)
-        along = jnp.sum(v_ref[:, vs].astype(F32) * carried, axis=1, keepdims=True)
-        along = along + jnp.sum(k_ref[:, ks].astype(F32) * vector, axis=1, keepdims=True)
-        column_cross = put(column_cross, along, h)
         product = jnp.sum(mem_ref[slab].reshape(dk, dv) * following, axis=0, keepdims=True)
         product = jnp.sum(product, axis=1, keepdims=True)
         product = product + jnp.sum(small_ref[one] * vector, axis=1, keepdims=True)
@@ -711,12 +750,17 @@
     def given(kinds, *arrays):
         return list(zip(kinds, arrays, strict=True))
 
-    give, memory, tile, rows = call(
+    give, turned, column, tile, rows = call(
         part(gates_kernel, heads),
-        given("vvvh", (slabs // 2 + 1, 8, dv), (slabs, 8, dv), (8, 128), (24, n)),
+        given(
+            "vvvvh", (slabs // 2 + 1, 8, dv), low((heads * dk, n), BF16), (n, 128), (8, 128), (24, n)
+        ),
         given("shhmmhhhh", me, w_input.T, w_forget.T, b_input, b_forget, doc_pos, k, x, v),
     )
     pair = to_pair(give)
+    (memory,) = call(
+        part(products_kernel, heads), given("v", (count, 8, dv)), given("svhv", me, turned, v, column)
+    )
     (pay,) = call(
         part(first_kernel, heads),
         given("v", (count, 8, dv + 128)),
@@ -730,38 +774,46 @@
         ),
         given("svvvhhhhh", me, memory, tile, pair, rows, q, k, v, g),
     )
-    give, dual, coef, now, coef_later, later, small, tokens = call(
+    give, column, coef, now, coef_later, later, small, tokens = call(
         part(dual_kernel, heads, scale),
         given(
-            "vvvvvvhh", (count, 8, dv), (count, 8, dv), (2, count, 128), (16, 128),
+            "vvvvvvhh", (count, 8, dv), (n, 128), (2, count, 128), (16, 128),
             (2, count, 128), (count, 128), (16, 128), (24, n),
         ),
         given("svvhvvh", me, first, even_tile, rows, sums, turned, g),
     )
     pair = to_pair(give)
-    (pay,) = call(
+    (dual,) = call(
+        part(products_kernel, heads), given("v", (count, 8, dv)), given("svhv", me, turned, g, column)
+    )
+    (before,) = call(before_kernel, given("v", (count, 8, dv)), given("vv", first, coef))
+    pay, odd_dual = call(
         part(second_kernel, heads),
-        given("v", (count, 8, 2 * dv)),
-        given("svvvvv", me, first, coef, now, dual, pair),
+        given("vh", (count, 8, 2 * dv), (count, 8, dv)),
+        given("svvvv", me, before, now, dual, pair),
     )
     second = exchange(pay, "ctx", cores)
-    (odd_dual,) = call(odd_kernel, given("h", (count, 8, dv)), given("svv", me, dual, pair))
     give, mine = call(
         part(halves_kernel, heads),
         given("vv", (count, 8, dv), (count, 8, dv)),
-        given("svvva", me, second, even_memory, now, odd_dual),
+        given("svvv", me, second, even_memory, now),
     )
     pair = to_pair(give)
-    pay, states, tile, gt = call(
+    after, crossing = call(
+        part(mine_kernel, heads),
+        given("vv", (count, 2 * dv // 128, 4, 128), (n, 128)),
+        given("svvvvv", me, mine, second, coef_later, q, g),
+    )
+    pay, tile, gt = call(
         part(vector_kernel, heads, scale),
-        given("vhvh", (count, 2 * dv // 128 + 1, 4, 128), (slabs, 8, dv), (8, 128), (8, n)),
-        given("svvvvvvvv", me, mine, pair, second, coef_later, tokens, sums, q, g),
+        given("vvv", (count, 2 * dv // 128 + 1, 4, 128), (8, 128), (8, n)),
+        given("svvvvvvvv", me, mine, pair, after, crossing, tokens, sums, q, g),
     )
     third = exchange(pay, "ctx", cores)
-    grad_q, gvalue, gk, row, cold = call(
+    states, grad_q, gvalue, gk, row, cold = call(
         part(inner_kernel, heads, scale),
-        given("hhhhh", low(q.shape, BF16), v.shape, k.shape, (8, n), (8, n)),
-        given("hhhhhhhhhh", states, tokens, small, gt, wl, pc, gv, q, k, g),
+        given("hhhhhh", (slabs, 8, dv), low(q.shape, BF16), v.shape, k.shape, (8, n), (8, n)),
+        given("svvvhhhhhhhh", me, mine, pair, gt, tokens, small, wl, pc, gv, q, k, g),
     )
     give, mine, sums = call(
         part(after_kernel, heads),
@@ -769,6 +821,7 @@
         given("svvvhva", me, third, later, now, odd_dual, tile, gk),
     )
     pair = to_pair(give)
+    (along,) = call(part(along_kernel, heads), given("v", (n, 128)), given("svvv", me, mine, k, v))
     batch, across_x = lax.axis_size("dp"), 4
     tiles = batch * across_x
     at = [[[(z * across_x + i) * 2 + c for i in range(across_x)] for c in range(2)] for z in range(count // across_x)]
@@ -779,7 +832,7 @@
         part(weights_kernel, heads),
         given("hhv", (slabs, 8, dv), (8, 128), (tiles, *chunk)),
         given(
-            "svvvvvvhhhhv", me, mine, pair, sums, now, k, v, states, rows, row, cold, x
+            "svvvvvvvhhhhv", me, mine, pair, sums, along, now, k, v, states, rows, row, cold, x
         ),
     )
     got = exchange(pay, ("ctx", "dp"), planes)

time: 129 us -> 128 us (level)
  blocking collectives: 23.7 us -> 44.2 us
  waiting for transfers between devices: 39 us -> 20.6 us
  starting transfers between devices: 33.7 us -> 29.1 us
    all_to_all x2 -> x3, blocking collectives: 23.7 us -> 44.2 us  [exchange(): return lax.all_to_all(x, axis, 0, 0, axis_index_groups=groups)]
    all_to_all x4 -> x3, waiting for transfers between devices: 34.3 us -> 19.2 us  [exchange(): return lax.all_to_all(x, axis, 0, 0, axis_index_groups=groups)]
    all_to_all x4 -> x3, starting transfers between devices: 23.1 us -> 19.2 us  [exchange(): return lax.all_to_all(x, axis, 0, 0, axis_index_groups=groups)]
    ppermute x4, waiting for transfers between devices: 4.67 us -> 1.47 us  [to_pair(): return lax.ppermute(a, 'ctx', [(i, i ^ 1) for i in range(devices)])]
    pallas_call x15 -> x19, Pallas kernels: 30.8 us -> 32 us  [call(): pl.pallas_call(kernel, out_shape=[pltpu.HBM(o.shape, o.dtype) if k == 'h'...]
  transfers between devices with their start and end apart: 8 -> 7, of which waited for: 8 -> 5; matrix products, arithmetic and copies ran while one was open for 0% -> 0% of each run, Pallas kernels for 12% -> 15%
where the time goes in v5:
time: 128 us; the launch traced here: 127 us
  blocking collectives  44.2 us (35%)
  Pallas kernels  32 us (25%)
  starting transfers between devices  29.1 us (23%)
  waiting for transfers between devices  20.6 us (16%)
    all_to_all x3, blocking collectives, exchange(): return lax.all_to_all(x, axis, 0, 0, axis_index_groups=groups)  44.2 us
    pallas_call x19, Pallas kernels, call(): pl.pallas_call(kernel, out_shape=[pltpu.HBM(o.shape, o.dtype) if k == 'h'...  32 us
    all_to_all x3, starting transfers between devices, exchange(): return lax.all_to_all(x, axis, 0, 0, axis_index_groups=groups)  19.2 us
    all_to_all x3, waiting for transfers between devices, exchange(): return lax.all_to_all(x, axis, 0, 0, axis_index_groups=groups)  19.2 us
    ppermute x4, starting transfers between devices, to_pair(): return lax.ppermute(a, 'ctx', [(i, i ^ 1) for i in range(devices)])  9.88 us
  transfers between devices with their start and end apart: 7, of which 5 were waited for; matrix products, arithmetic and copies ran while one was open for 0% of the time, Pallas kernels for 15%

profile of v5, /device:TPU:1, one launch (start us, length us, event | category | flops | bytes accessed | tf_op | source)
XLA Modules:
  0.0 127.0 jit_solution(9856387312060722754)
XLA Ops:
  0.6 3.8 %shard_map.137 = (f32[33,8,256]{2,1,0:T(8,128)S(1)}, bf16[512,256]{1,0:T(8,128)(2,1)S(1)}, f32[256,128]{1,0:T(8,128)S(1)}, f32[8,128]{1,0:T(8,128)S(1)}, f32[24,256]{1,0:T(8,128)}) custom-call(s32[1]{0:T(128)} %bitcast.refs_0_, bf16[4,4096]{1,0:T(4,128)(2,1)} %bitcast.38, bf16[4,4096]{1,0:T(4,128)(2,1)} %bitcast.39, f32[4]{0:T(128)} %refs_3_.1, f32[4]{0:T(128)} %refs_4_.1, ...), custom_call_target="tpu_custom_call" | custom-call | tf_op jit(solution)/shard_map/pallas_call | solution.py:712
  4.4 3.3 %collective-permute-start = (f32[33,8,256]{2,1,0:T(8,128)S(1)}, f32[33,8,256]{2,1,0:T(8,128)S(1)}, u32[]{:S(2)}, u32[]{:S(2)}) collective-permute-start(f32[33,8,256]{2,1,0:T(8,128)S(1)} %get-tuple-element.53), channel_id=1, source_target_pairs={{0,4},{4,0},{8,12},{12,8},{16,20},{20,16},{24,28},{28,24},{32,36},... | collective-permute-start | bytes 811016 | tf_op jit(solution)/shard_map/ppermute | solution.py:746
  7.7 1.4 %shard_map.138.refs_1_ = f32[32,8,256]{2,1,0:T(8,128)S(1)} custom-call(s32[1]{0:T(128)} %bitcast.refs_0_, bf16[512,256]{1,0:T(8,128)(2,1)S(1)} %get-tuple-element.50.refs_1_, bf16[256,1024]{1,0:T(8,128)(2,1)} %bitcast.20, f32[256,128]{1,0:T(8,128)S(1)} %get-tuple-element.51.refs_3_), custom_call_target="tpu_custom_call" | custom-call | tf_op jit(solution)/shard_map/pallas_call | solution.py:712
  9.2 0.9 shard_map.139
  10.1 9.3 %all-to-all-start = ((f32[32,8,384]{2,1,0:T(8,128)}), f32[32,8,384]{2,1,0:T(8,128)S(1)}, u32[]{:S(2)}, u32[]{:S(2)}) async-start(f32[32,8,384]{2,1,0:T(8,128)} %shard_map.139), calls=%async_computation | async-start | bytes 786432 | tf_op jit(solution)/shard_map/all_to_all | solution.py:727
  19.5 4.3 %shard_map.140 = (f32[32,8,256]{2,1,0:T(8,128)}, f32[8,128]{1,0:T(8,128)S(1)}, bf16[512,256]{1,0:T(8,128)(2,1)S(1)}, f32[4,256,256]{2,1,0:T(8,128)}, f32[4,256,2...) custom-call(s32[1]{0:T(128)} %bitcast.refs_0_, f32[32,8,256]{2,1,0:T(8,128)S(1)} %shard_map.138.refs_1_, ...), custom_call_target="tpu_custom_call" | custom-call | tf_op jit(solution)/shard_map/pallas_call | solution.py:712
  23.8 10.1 %all-to-all-done.refs_1_.refs_0_ = f32[32,8,384]{2,1,0:T(8,128)S(1)} async-done(((f32[32,8,384]{2,1,0:T(8,128)}), f32[32,8,384]{2,1,0:T(8,128)S(1)}, u32[]{:S(2)}, u32[]{:S(2)}) %all-to-all-start) | async-done | bytes 393248 | tf_op jit(solution)/shard_map/all_to_all | solution.py:727
  33.9 1.8 %shard_map.141 = (f32[32,8,256]{2,1,0:T(8,128)S(1)}, f32[256,128]{1,0:T(8,128)S(1)}, f32[2,32,128]{2,1,0:T(8,128)S(1)}, f32[16,128]{1,0:T(8,128)S(1)}, f32[2,32,...) custom-call(s32[1]{0:T(128)} %bitcast.refs_0_, ...), custom_call_target="tpu_custom_call" | custom-call | tf_op jit(solution)/shard_map/pallas_call | solution.py:712
  35.8 1.9 %collective-permute-start.1 = (f32[32,8,256]{2,1,0:T(8,128)S(1)}, f32[32,8,256]{2,1,0:T(8,128)S(1)}, u32[]{:S(2)}, u32[]{:S(2)}) collective-permute-start(f32[32,8,256]{2,1,0:T(8,128)S(1)} %get-tuple-element.61), channel_id=1, source_target_pairs={{0,4},{4,0},{8,12},{12,8},{16,20},{20,16},{24,28},{28,24},{32,36},... | collective-permute-start | bytes 786440 | tf_op jit(solution)/shard_map/ppermute | solution.py:746
  37.7 1.5 %shard_map.143.refs_3_ = f32[32,8,256]{2,1,0:T(8,128)S(1)} custom-call(s32[1]{0:T(128)} %bitcast.refs_0_, bf16[512,256]{1,0:T(8,128)(2,1)S(1)} %get-tuple-element.57.refs_5_.refs_1_, bf16[256,1024]{1,0:T(8,128)(2,1)} %bitcast.15, f32[256,128]{1,0:T(8,128)S(1)} %get-tuple-element.60.refs_3_), custom_call_target="tpu_custom_call" | custom-call | tf_op jit(solution)/shard_map/pallas_call | solution.py:712
  39.2 0.1 shard_map.142.refs_1_
  39.3 0.8 shard_map.144
  40.1 20.6 %all_to_all.30.refs_1_.refs_2_ = f32[32,8,512]{2,1,0:T(8,128)S(1)} all-to-all(f32[32,8,512]{2,1,0:T(8,128)S(1)} %get-tuple-element.62), channel_id=1, replica_groups={{0,8,16,24,32,40,48,56,64,72,80,88,96,104,112,120,128,136,144,152,160,1..., dimensions={0} | all-to-all | bytes 1048576 | tf_op jit(solution)/shard_map/all_to_all | solution.py:727
  60.7 0.1 shard_map.145
  60.8 2.0 %collective-permute-start.2 = (f32[32,8,256]{2,1,0:T(8,128)S(1)}, f32[32,8,256]{2,1,0:T(8,128)S(1)}, u32[]{:S(2)}, u32[]{:S(2)}) collective-permute-start(f32[32,8,256]{2,1,0:T(8,128)S(1)} %get-tuple-element.65), channel_id=1, source_target_pairs={{0,4},{4,0},{8,12},{12,8},{16,20},{20,16},{24,28},{28,24},{32,36},... | collective-permute-start | bytes 786440 | tf_op jit(solution)/shard_map/ppermute | solution.py:746
  62.8 0.5 shard_map.146
  63.2 0.7 collective-permute-done.2.refs_2_
  63.9 1.4 %shard_map.147 = (f32[32,5,4,128]{3,2,1,0:T(4,128)}, f32[8,128]{1,0:T(8,128)S(1)}, f32[8,256]{1,0:T(8,128)S(1)}) custom-call(s32[1]{0:T(128)} %bitcast.refs_0_, f32[32,8,256]{2,1,0:T(8,128)S(1)} %get-tuple-element.64.refs_1_, f32[32,8,256]{2,1,0:T(8,128)S(1)} %collective-permute-done.2.refs_2_, f32[32,4,4,128]{3,2,1,0:T(4,128)S(1)} %get-tuple-element.67.refs_3_, ...), custom_call_target="tpu_custom_call" | custom-call | tf_op jit(solution)/shard_map/pallas_call | solution.py:712
  65.3 4.4 %all-to-all-start.2 = ((f32[32,5,4,128]{3,2,1,0:T(4,128)}), f32[32,5,4,128]{3,2,1,0:T(4,128)S(1)}, u32[]{:S(2)}, u32[]{:S(2)}) async-start(f32[32,5,4,128]{3,2,1,0:T(4,128)} %get-tuple-element.76), calls=%async_computation.2 | async-start | bytes 655360 | tf_op jit(solution)/shard_map/all_to_all | solution.py:727
  69.8 6.3 %shard_map.148 = (f32[64,8,256]{2,1,0:T(8,128)}, bf16[256,512]{1,0:T(8,128)(2,1)}, f32[256,1024]{1,0:T(8,128)}, f32[256,512]{1,0:T(8,128)}, f32[8,256]{1,0:T(8,128)}, /*index=5*/f32[8,256]{1,0:T(8,128)}) custom-call(s32[1]{0:T(128)} %bitcast.refs_0_, f32[32,8,256]{2,1,0:T(8,128)S(1)} %get-tuple-element.64.refs_1_, ...), custom_call_target="tpu_custom_call" | custom-call | tf_op jit(solution)/shard_map/pallas_call | solution.py:712
  76.1 6.4 %all-to-all-done.2.refs_1_ = f32[32,5,4,128]{3,2,1,0:T(4,128)S(1)} async-done(((f32[32,5,4,128]{3,2,1,0:T(4,128)}), f32[32,5,4,128]{3,2,1,0:T(4,128)S(1)}, u32[]{:S(2)}, u32[]{:S(2)}) %all-to-all-start.2) | async-done | bytes 327712 | tf_op jit(solution)/shard_map/all_to_all | solution.py:727
  82.5 1.1 shard_map.149
  83.6 2.7 %collective-permute-start.3 = (f32[33,8,256]{2,1,0:T(8,128)S(1)}, f32[33,8,256]{2,1,0:T(8,128)S(1)}, u32[]{:S(2)}, u32[]{:S(2)}) collective-permute-start(f32[33,8,256]{2,1,0:T(8,128)S(1)} %get-tuple-element.82), channel_id=1, source_target_pairs={{0,4},{4,0},{8,12},{12,8},{16,20},{20,16},{24,28},{28,24},{32,36},... | collective-permute-start | bytes 811016 | tf_op jit(solution)/shard_map/ppermute | solution.py:746
  86.3 0.4 shard_map.150.refs_4_
  86.7 0.8 collective-permute-done.3.refs_2_
  87.4 2.9 %shard_map.151 = (f32[64,8,256]{2,1,0:T(8,128)}, f32[8,128]{1,0:T(8,128)}, f32[16,8,256]{2,1,0:T(8,128)}) custom-call(s32[1]{0:T(128)} %bitcast.refs_0_, f32[32,8,256]{2,1,0:T(8,128)S(1)} %get-tuple-element.81.refs_1_, f32[33,8,256]{2,1,0:T(8,128)S(1)} %collective-permute-done.3.refs_2_, f32[8,128]{1,0:T(8,128)S(1)} %get-tuple-element.83.refs_3_, ...), custom_call_target="tpu_custom_call" | custom-call | tf_op jit(solution)/shard_map/pallas_call | solution.py:712
  90.3 5.5 %all-to-all-start.3 = ((f32[16,8,256]{2,1,0:T(8,128)}), f32[16,8,256]{2,1,0:T(8,128)S(1)}, u32[]{:S(2)}, u32[]{:S(2)}) async-start(f32[16,8,256]{2,1,0:T(8,128)} %get-tuple-element.92), calls=%async_computation.3 | async-start | bytes 262144 | tf_op jit(solution)/shard_map/all_to_all | solution.py:727
  95.8 4.0 %shard_map.152 = (bf16[256,512]{1,0:T(8,128)(2,1)}, bf16[256,1024]{1,0:T(8,128)(2,1)}) custom-call(f32[64,8,256]{2,1,0:T(8,128)} %get-tuple-element.87.refs_0_, f32[8,128]{1,0:T(8,128)} %get-tuple-element.88.refs_1_, f32[16,128]{1,0:T(8,128)} %get-tuple-element.71.refs_5_.refs_2_, f32[24,256]{1,0:T(8,128)} %get-tuple-element.54.refs_4_.refs_3_.refs_9_, ...), custom_call_target="tpu_custom_call" | custom-call | tf_op jit(solution)/shard_map/pallas_call | solution.py:712
  99.8 2.7 %all-to-all-done.3.refs_0_ = f32[16,8,256]{2,1,0:T(8,128)S(1)} async-done(((f32[16,8,256]{2,1,0:T(8,128)}), f32[16,8,256]{2,1,0:T(8,128)S(1)}, u32[]{:S(2)}, u32[]{:S(2)}) %all-to-all-start.3) | async-done | bytes 131104 | tf_op jit(solution)/shard_map/all_to_all | solution.py:727
  102.5 13.4 %all_to_all.31.refs_0_ = f32[16,8,256]{2,1,0:T(8,128)S(1)} all-to-all(f32[16,8,256]{2,1,0:T(8,128)S(1)} %shard_map.153), channel_id=1, replica_groups={{0,4,32,36,64,68,96,100,128,132,160,164,192,196,224,228},{8,12,40,44,72..., dimensions={0} | all-to-all | bytes 262144 | tf_op jit(solution)/shard_map/all_to_all | solution.py:727
  116.0 10.2 %all_to_all.32.refs_0_ = f32[16,8,256]{2,1,0:T(8,128)S(1)} all-to-all(f32[16,8,256]{2,1,0:T(8,128)S(1)} %shard_map.154), channel_id=1, replica_groups={{0,1,2,3,8,9,10,11,16,17,18,19,24,25,26,27},{4,5,6,7,12,13,14,15,20,21,..., dimensions={0} | all-to-all | bytes 262144 | tf_op jit(solution)/shard_map/all_to_all | solution.py:727
  126.2 0.7 shard_map.155
  (18 shorter events, 0.1 us)
Async XLA Ops:
  4.4 4.8 %collective-permute-start = (f32[33,8,256]{2,1,0:T(8,128)S(1)}, f32[33,8,256]{2,1,0:T(8,128)S(1)}, u32[]{:S(2)}, u32[]{:S(2)}) collective-permute-start(f32[33,8,256]{2,1,0:T(8,128)S(1)} %get-tuple-element.53), channel_id=1, source_target_pairs={{0,4},{4,0},{8,12},{12,8},{16,20},{20,16},{24,28},{28,24},{32,36},... | collective-permute-start | bytes 811016 | tf_op jit(solution)/shard_map/ppermute | solution.py:746
  10.1 23.8 %all-to-all-start = ((f32[32,8,384]{2,1,0:T(8,128)}), f32[32,8,384]{2,1,0:T(8,128)S(1)}, u32[]{:S(2)}, u32[]{:S(2)}) async-start(f32[32,8,384]{2,1,0:T(8,128)} %shard_map.139), calls=%async_computation | async-start | bytes 786432 | tf_op jit(solution)/shard_map/all_to_all | solution.py:727
  35.7 24.9 %copy-start.5 = (f32[32,8,256]{2,1,0:T(8,128)S(1)}, f32[32,8,256]{2,1,0:T(8,128)}, u32[]{:S(2)}) copy-start(f32[32,8,256]{2,1,0:T(8,128)} %get-tuple-element.63.refs_2_) | copy-start | bytes 786436
  35.8 3.5 %collective-permute-start.1 = (f32[32,8,256]{2,1,0:T(8,128)S(1)}, f32[32,8,256]{2,1,0:T(8,128)S(1)}, u32[]{:S(2)}, u32[]{:S(2)}) collective-permute-start(f32[32,8,256]{2,1,0:T(8,128)S(1)} %get-tuple-element.61), channel_id=1, source_target_pairs={{0,4},{4,0},{8,12},{12,8},{16,20},{20,16},{24,28},{28,24},{32,36},... | collective-permute-start | bytes 786440 | tf_op jit(solution)/shard_map/ppermute | solution.py:746
  37.7 25.1 %copy-start = (bf16[1,256,1024]{2,1,0:T(8,128)(2,1)S(1)}, bf16[1,256,1024]{2,1,0:T(8,128)(2,1)}, u32[]{:S(2)}) copy-start(bf16[1,256,1024]{2,1,0:T(8,128)(2,1)} %param.14) | copy-start | bytes 1572868
  37.7 25.1 %copy-start.4 = (bf16[1,256,512]{2,1,0:T(8,128)(2,1)S(1)}, bf16[1,256,512]{2,1,0:T(8,128)(2,1)}, u32[]{:S(2)}) copy-start(bf16[1,256,512]{2,1,0:T(8,128)(2,1)} %param.11) | copy-start | bytes 786436
  39.3 24.6 %copy-start.6 = (f32[24,256]{1,0:T(8,128)S(1)}, f32[24,256]{1,0:T(8,128)}, u32[]{:S(2)}) copy-start(f32[24,256]{1,0:T(8,128)} %get-tuple-element.69.refs_5_.refs_4_) | copy-start | bytes 73732
  60.8 3.1 %collective-permute-start.2 = (f32[32,8,256]{2,1,0:T(8,128)S(1)}, f32[32,8,256]{2,1,0:T(8,128)S(1)}, u32[]{:S(2)}, u32[]{:S(2)}) collective-permute-start(f32[32,8,256]{2,1,0:T(8,128)S(1)} %get-tuple-element.65), channel_id=1, source_target_pairs={{0,4},{4,0},{8,12},{12,8},{16,20},{20,16},{24,28},{28,24},{32,36},... | collective-permute-start | bytes 786440 | tf_op jit(solution)/shard_map/ppermute | solution.py:746
  65.3 17.2 %all-to-all-start.2 = ((f32[32,5,4,128]{3,2,1,0:T(4,128)}), f32[32,5,4,128]{3,2,1,0:T(4,128)S(1)}, u32[]{:S(2)}, u32[]{:S(2)}) async-start(f32[32,5,4,128]{3,2,1,0:T(4,128)} %get-tuple-element.76), calls=%async_computation.2 | async-start | bytes 655360 | tf_op jit(solution)/shard_map/all_to_all | solution.py:727
  69.7 16.5 %copy-start.1 = (bf16[1,256,1024]{2,1,0:T(8,128)(2,1)S(1)}, bf16[1,256,1024]{2,1,0:T(8,128)(2,1)}, u32[]{:S(2)}) copy-start(bf16[1,256,1024]{2,1,0:T(8,128)(2,1)} %param.13) | copy-start | bytes 1572868
  69.7 16.5 %copy-start.2 = (bf16[1,256,512]{2,1,0:T(8,128)(2,1)S(1)}, bf16[1,256,512]{2,1,0:T(8,128)(2,1)}, u32[]{:S(2)}) copy-start(bf16[1,256,512]{2,1,0:T(8,128)(2,1)} %param.12) | copy-start | bytes 786436
  76.1 11.4 %copy-start.3 = (bf16[1,256,4096]{2,1,0:T(8,128)(2,1)S(1)}, bf16[1,256,4096]{2,1,0:T(8,128)(2,1)}, u32[]{:S(2)}) copy-start(bf16[1,256,4096]{2,1,0:T(8,128)(2,1)} %param.10) | copy-start | bytes 6291460
  83.6 3.8 %collective-permute-start.3 = (f32[33,8,256]{2,1,0:T(8,128)S(1)}, f32[33,8,256]{2,1,0:T(8,128)S(1)}, u32[]{:S(2)}, u32[]{:S(2)}) collective-permute-start(f32[33,8,256]{2,1,0:T(8,128)S(1)} %get-tuple-element.82), channel_id=1, source_target_pairs={{0,4},{4,0},{8,12},{12,8},{16,20},{20,16},{24,28},{28,24},{32,36},... | collective-permute-start | bytes 811016 | tf_op jit(solution)/shard_map/ppermute | solution.py:746
  90.3 12.2 %all-to-all-start.3 = ((f32[16,8,256]{2,1,0:T(8,128)}), f32[16,8,256]{2,1,0:T(8,128)S(1)}, u32[]{:S(2)}, u32[]{:S(2)}) async-start(f32[16,8,256]{2,1,0:T(8,128)} %get-tuple-element.92), calls=%async_computation.3 | async-start | bytes 262144 | tf_op jit(solution)/shard_map/all_to_all | solution.py:727

commit v6 on v5

--- a/solution.py
+++ b/solution.py
@@ -546,6 +546,13 @@
     return result
 
 
+def of_head(h, heads, core, mine_ref, pair_ref):
+    half = heads // 2
+    per_head = mine_ref.shape[0] // half
+    slab = slice(per_head * (h % half), per_head * (h % half + 1))
+    return jnp.where(core == h // half, mine_ref[slab], pair_ref[slab])
+
+
 def along_kernel(heads, me_ref, mine_ref, k_ref, v_ref, out_ref):
     out_ref[...] = alongs(me_ref[0] % 2, heads, mine_ref, k_ref, v_ref)
 
@@ -553,16 +560,13 @@
 def weights_kernel(
     heads, me_ref, mine_ref, pair_ref, sum_ref, along_ref, small_ref, k_ref, v_ref, mem_ref, rows_ref,
     row_ref, cold_ref, x_ref,
-    after_ref, vector_ref, pay_ref,
+    vector_ref, pay_ref,
 ):
     core = me_ref[0] % 2
     n = k_ref.shape[0]
     dk = k_ref.shape[1] // heads
     dv = v_ref.shape[1] // heads
     count = mine_ref.shape[0]
-    after_ref[pl.ds(core * count, count)] = mine_ref[...]
-    after_ref[pl.ds((1 - core) * count, count)] = pair_ref[:count]
-    after_ref.send()
     mine, other = sum_ref[...], pair_ref[count, :, :128]
     column_cross = merged(
         core, heads, along_ref[...], alongs(1 - core, heads, pair_ref, k_ref, v_ref)
@@ -578,7 +582,7 @@
         vectors.append(vector)
         along = jnp.sum(k_ref[:, ks].astype(F32) * vector, axis=1, keepdims=True)
         column_cross = column_cross + put(jnp.zeros((n, 128), F32), along, h)
-        following = after_ref[slab].reshape(dk, dv)
+        following = of_head(h, heads, core, mine_ref, pair_ref).reshape(dk, dv)
         product = jnp.sum(mem_ref[slab].reshape(dk, dv) * following, axis=0, keepdims=True)
         product = jnp.sum(product, axis=1, keepdims=True)
         product = product + jnp.sum(small_ref[one] * vector, axis=1, keepdims=True)
@@ -605,7 +609,7 @@
 
 
 def finish_kernel(
-    heads, after_ref, vector_ref, small_ref, rows_ref, gk_ref, gvalue_ref, k_ref, v_ref,
+    heads, me_ref, mine_ref, pair_ref, vector_ref, small_ref, rows_ref, gk_ref, gvalue_ref, k_ref, v_ref,
     gkey_ref, out_ref,
 ):
     dk = gk_ref.shape[1] // heads
@@ -613,7 +617,7 @@
     key_scale = jnp.exp(unpack(column_of(rows_ref[...]), 3, heads) + small_ref[heads : heads + 1])
     for h in range(heads):
         ks, vs, one = slice(dk * h, dk * (h + 1)), slice(dv * h, dv * (h + 1)), slice(h, h + 1)
-        following = after_ref[dk // 8 * h : dk // 8 * (h + 1)].reshape(dk, dv)
+        following = of_head(h, heads, me_ref[0] % 2, mine_ref, pair_ref).reshape(dk, dv)
         high, low = split(following)
         carried = dot(v_ref[:, vs], high, 1, 1) + dot(v_ref[:, vs], low, 1, 1) + vector_ref[one]
         gkey_ref[:, ks] = (gk_ref[:, ks] + key_scale[:, one] * carried).astype(BF16)
@@ -828,9 +832,9 @@
     planes = [[i * batch + d for i in row for d in range(batch)] for z in at for row in z]
     lines = [[row[i] for z in at for row in z] for i in range(across_x)]
     chunk = (8, x.shape[1] // tiles)
-    following, vector, pay = call(
+    vector, pay = call(
         part(weights_kernel, heads),
-        given("hhv", (slabs, 8, dv), (8, 128), (tiles, *chunk)),
+        given("hh", (8, 128), (tiles, *chunk)),
         given(
             "svvvvvvvhhhhv", me, mine, pair, sums, along, now, k, v, states, rows, row, cold, x
         ),
@@ -839,7 +843,7 @@
     grad_k, grad_v = call(
         part(finish_kernel, heads),
         given("hh", low(k.shape, BF16), low(v.shape, BF16)),
-        given("hhhhhhhh", following, vector, small, rows, gk, gvalue, k, v),
+        given("svvhhhhhhh", me, mine, pair, vector, small, rows, gk, gvalue, k, v),
     )
     (pay,) = call(sum_kernel, given("v", (len(lines[0]), *chunk)), given("va", got, grad_k))
     got = exchange(pay, "ctx", lines)

time: 128 us -> 128 us (level)
  transfers between devices with their start and end apart: 7 -> 7, of which waited for: 5 -> 5; matrix products, arithmetic and copies ran while one was open for 0% -> 0% of each run, Pallas kernels for 15% -> 14%
where the time goes in v6:
time: 128 us; the launch traced here: 127 us
  blocking collectives  44.2 us (35%)
  Pallas kernels  32 us (25%)
  starting transfers between devices  29.1 us (23%)
  waiting for transfers between devices  20.8 us (16%)
    all_to_all x3, blocking collectives, exchange(): return lax.all_to_all(x, axis, 0, 0, axis_index_groups=groups)  44.2 us
    pallas_call x19, Pallas kernels, call(): pl.pallas_call(kernel, out_shape=[pltpu.HBM(o.shape, o.dtype) if k == 'h'...  32 us
    all_to_all x3, waiting for transfers between devices, exchange(): return lax.all_to_all(x, axis, 0, 0, axis_index_groups=groups)  19.3 us
    all_to_all x3, starting transfers between devices, exchange(): return lax.all_to_all(x, axis, 0, 0, axis_index_groups=groups)  19.2 us
    ppermute x4, starting transfers between devices, to_pair(): return lax.ppermute(a, 'ctx', [(i, i ^ 1) for i in range(devices)])  9.88 us
  transfers between devices with their start and end apart: 7, of which 5 were waited for; matrix products, arithmetic and copies ran while one was open for 0% of the time, Pallas kernels for 14%

profile of v6, /device:TPU:1, one launch (start us, length us, event | category | flops | bytes accessed | tf_op | source)
XLA Modules:
  0.0 127.2 jit_solution(16923496293595250105)
XLA Ops:
  0.6 3.8 %shard_map.137 = (f32[33,8,256]{2,1,0:T(8,128)S(1)}, bf16[512,256]{1,0:T(8,128)(2,1)S(1)}, f32[256,128]{1,0:T(8,128)S(1)}, f32[8,128]{1,0:T(8,128)S(1)}, f32[24,256]{1,0:T(8,128)}) custom-call(s32[1]{0:T(128)} %bitcast.refs_0_, bf16[4,4096]{1,0:T(4,128)(2,1)} %bitcast.38, bf16[4,4096]{1,0:T(4,128)(2,1)} %bitcast.39, f32[4]{0:T(128)} %refs_3_.1, f32[4]{0:T(128)} %refs_4_.1, ...), custom_call_target="tpu_custom_call" | custom-call | tf_op jit(solution)/shard_map/pallas_call | solution.py:716
  4.4 3.3 %collective-permute-start = (f32[33,8,256]{2,1,0:T(8,128)S(1)}, f32[33,8,256]{2,1,0:T(8,128)S(1)}, u32[]{:S(2)}, u32[]{:S(2)}) collective-permute-start(f32[33,8,256]{2,1,0:T(8,128)S(1)} %get-tuple-element.52), channel_id=1, source_target_pairs={{0,4},{4,0},{8,12},{12,8},{16,20},{20,16},{24,28},{28,24},{32,36},... | collective-permute-start | bytes 811016 | tf_op jit(solution)/shard_map/ppermute | solution.py:750
  7.7 1.4 %shard_map.138.refs_1_ = f32[32,8,256]{2,1,0:T(8,128)S(1)} custom-call(s32[1]{0:T(128)} %bitcast.refs_0_, bf16[512,256]{1,0:T(8,128)(2,1)S(1)} %get-tuple-element.49.refs_1_, bf16[256,1024]{1,0:T(8,128)(2,1)} %bitcast.20, f32[256,128]{1,0:T(8,128)S(1)} %get-tuple-element.50.refs_3_), custom_call_target="tpu_custom_call" | custom-call | tf_op jit(solution)/shard_map/pallas_call | solution.py:716
  9.2 0.9 shard_map.139
  10.1 9.3 %all-to-all-start = ((f32[32,8,384]{2,1,0:T(8,128)}), f32[32,8,384]{2,1,0:T(8,128)S(1)}, u32[]{:S(2)}, u32[]{:S(2)}) async-start(f32[32,8,384]{2,1,0:T(8,128)} %shard_map.139), calls=%async_computation | async-start | bytes 786432 | tf_op jit(solution)/shard_map/all_to_all | solution.py:731
  19.5 4.3 %shard_map.140 = (f32[32,8,256]{2,1,0:T(8,128)}, f32[8,128]{1,0:T(8,128)S(1)}, bf16[512,256]{1,0:T(8,128)(2,1)S(1)}, f32[4,256,256]{2,1,0:T(8,128)}, f32[4,256,2...) custom-call(s32[1]{0:T(128)} %bitcast.refs_0_, f32[32,8,256]{2,1,0:T(8,128)S(1)} %shard_map.138.refs_1_, ...), custom_call_target="tpu_custom_call" | custom-call | tf_op jit(solution)/shard_map/pallas_call | solution.py:716
  23.8 10.1 %all-to-all-done.refs_1_.refs_0_ = f32[32,8,384]{2,1,0:T(8,128)S(1)} async-done(((f32[32,8,384]{2,1,0:T(8,128)}), f32[32,8,384]{2,1,0:T(8,128)S(1)}, u32[]{:S(2)}, u32[]{:S(2)}) %all-to-all-start) | async-done | bytes 393248 | tf_op jit(solution)/shard_map/all_to_all | solution.py:731
  33.9 1.8 %shard_map.141 = (f32[32,8,256]{2,1,0:T(8,128)S(1)}, f32[256,128]{1,0:T(8,128)S(1)}, f32[2,32,128]{2,1,0:T(8,128)S(1)}, f32[16,128]{1,0:T(8,128)S(1)}, f32[2,32,...) custom-call(s32[1]{0:T(128)} %bitcast.refs_0_, ...), custom_call_target="tpu_custom_call" | custom-call | tf_op jit(solution)/shard_map/pallas_call | solution.py:716
  35.8 1.9 %collective-permute-start.1 = (f32[32,8,256]{2,1,0:T(8,128)S(1)}, f32[32,8,256]{2,1,0:T(8,128)S(1)}, u32[]{:S(2)}, u32[]{:S(2)}) collective-permute-start(f32[32,8,256]{2,1,0:T(8,128)S(1)} %get-tuple-element.60), channel_id=1, source_target_pairs={{0,4},{4,0},{8,12},{12,8},{16,20},{20,16},{24,28},{28,24},{32,36},... | collective-permute-start | bytes 786440 | tf_op jit(solution)/shard_map/ppermute | solution.py:750
  37.7 1.5 %shard_map.143.refs_3_ = f32[32,8,256]{2,1,0:T(8,128)S(1)} custom-call(s32[1]{0:T(128)} %bitcast.refs_0_, bf16[512,256]{1,0:T(8,128)(2,1)S(1)} %get-tuple-element.56.refs_5_.refs_1_, bf16[256,1024]{1,0:T(8,128)(2,1)} %bitcast.15, f32[256,128]{1,0:T(8,128)S(1)} %get-tuple-element.59.refs_3_), custom_call_target="tpu_custom_call" | custom-call | tf_op jit(solution)/shard_map/pallas_call | solution.py:716
  39.2 0.1 shard_map.142.refs_1_
  39.3 0.8 shard_map.144
  40.1 20.6 %all_to_all.30.refs_1_.refs_2_ = f32[32,8,512]{2,1,0:T(8,128)S(1)} all-to-all(f32[32,8,512]{2,1,0:T(8,128)S(1)} %get-tuple-element.61), channel_id=1, replica_groups={{0,8,16,24,32,40,48,56,64,72,80,88,96,104,112,120,128,136,144,152,160,1..., dimensions={0} | all-to-all | bytes 1048576 | tf_op jit(solution)/shard_map/all_to_all | solution.py:731
  60.7 0.1 shard_map.145
  60.8 2.0 %collective-permute-start.2 = (f32[32,8,256]{2,1,0:T(8,128)S(1)}, f32[32,8,256]{2,1,0:T(8,128)S(1)}, u32[]{:S(2)}, u32[]{:S(2)}) collective-permute-start(f32[32,8,256]{2,1,0:T(8,128)S(1)} %get-tuple-element.64), channel_id=1, source_target_pairs={{0,4},{4,0},{8,12},{12,8},{16,20},{20,16},{24,28},{28,24},{32,36},... | collective-permute-start | bytes 786440 | tf_op jit(solution)/shard_map/ppermute | solution.py:750
  62.8 0.5 shard_map.146
  63.2 0.7 collective-permute-done.2.refs_2_
  63.9 1.4 %shard_map.147 = (f32[32,5,4,128]{3,2,1,0:T(4,128)}, f32[8,128]{1,0:T(8,128)S(1)}, f32[8,256]{1,0:T(8,128)S(1)}) custom-call(s32[1]{0:T(128)} %bitcast.refs_0_, f32[32,8,256]{2,1,0:T(8,128)S(1)} %get-tuple-element.63.refs_1_, f32[32,8,256]{2,1,0:T(8,128)S(1)} %collective-permute-done.2.refs_2_, f32[32,4,4,128]{3,2,1,0:T(4,128)S(1)} %get-tuple-element.66.refs_3_, ...), custom_call_target="tpu_custom_call" | custom-call | tf_op jit(solution)/shard_map/pallas_call | solution.py:716
  65.3 4.4 %all-to-all-start.2 = ((f32[32,5,4,128]{3,2,1,0:T(4,128)}), f32[32,5,4,128]{3,2,1,0:T(4,128)S(1)}, u32[]{:S(2)}, u32[]{:S(2)}) async-start(f32[32,5,4,128]{3,2,1,0:T(4,128)} %get-tuple-element.75), calls=%async_computation.2 | async-start | bytes 655360 | tf_op jit(solution)/shard_map/all_to_all | solution.py:731
  69.8 6.3 %shard_map.148 = (f32[64,8,256]{2,1,0:T(8,128)}, bf16[256,512]{1,0:T(8,128)(2,1)}, f32[256,1024]{1,0:T(8,128)}, f32[256,512]{1,0:T(8,128)}, f32[8,256]{1,0:T(8,128)}, /*index=5*/f32[8,256]{1,0:T(8,128)}) custom-call(s32[1]{0:T(128)} %bitcast.refs_0_, f32[32,8,256]{2,1,0:T(8,128)S(1)} %get-tuple-element.63.refs_1_, ...), custom_call_target="tpu_custom_call" | custom-call | tf_op jit(solution)/shard_map/pallas_call | solution.py:716
  76.1 6.4 %all-to-all-done.2.refs_1_ = f32[32,5,4,128]{3,2,1,0:T(4,128)S(1)} async-done(((f32[32,5,4,128]{3,2,1,0:T(4,128)}), f32[32,5,4,128]{3,2,1,0:T(4,128)S(1)}, u32[]{:S(2)}, u32[]{:S(2)}) %all-to-all-start.2) | async-done | bytes 327712 | tf_op jit(solution)/shard_map/all_to_all | solution.py:731
  82.5 1.1 shard_map.149
  83.6 2.7 %collective-permute-start.3 = (f32[33,8,256]{2,1,0:T(8,128)S(1)}, f32[33,8,256]{2,1,0:T(8,128)S(1)}, u32[]{:S(2)}, u32[]{:S(2)}) collective-permute-start(f32[33,8,256]{2,1,0:T(8,128)S(1)} %get-tuple-element.81), channel_id=1, source_target_pairs={{0,4},{4,0},{8,12},{12,8},{16,20},{20,16},{24,28},{28,24},{32,36},... | collective-permute-start | bytes 811016 | tf_op jit(solution)/shard_map/ppermute | solution.py:750
  86.3 0.4 shard_map.150.refs_4_
  86.7 0.8 collective-permute-done.3.refs_2_
  87.4 3.1 %shard_map.151 = (f32[8,128]{1,0:T(8,128)}, f32[16,8,256]{2,1,0:T(8,128)}) custom-call(s32[1]{0:T(128)} %bitcast.refs_0_, f32[32,8,256]{2,1,0:T(8,128)S(1)} %get-tuple-element.80.refs_1_, f32[33,8,256]{2,1,0:T(8,128)S(1)} %collective-permute-done.3.refs_2_, f32[8,128]{1,0:T(8,128)S(1)} %get-tuple-element.82.refs_3_, f32[256,128]{1,0:T(8,128)S(1)} %shard_map.150.refs_4_, ...), custom_call_target="tpu_custom_call" | custom-call | tf_op jit(solution)/shard_map/pallas_call | solution.py:716
  90.5 5.5 %all-to-all-start.3 = ((f32[16,8,256]{2,1,0:T(8,128)}), f32[16,8,256]{2,1,0:T(8,128)S(1)}, u32[]{:S(2)}, u32[]{:S(2)}) async-start(f32[16,8,256]{2,1,0:T(8,128)} %get-tuple-element.90), calls=%async_computation.3 | async-start | bytes 262144 | tf_op jit(solution)/shard_map/all_to_all | solution.py:731
  96.0 3.9 %shard_map.152 = (bf16[256,512]{1,0:T(8,128)(2,1)}, bf16[256,1024]{1,0:T(8,128)(2,1)}) custom-call(s32[1]{0:T(128)} %bitcast.refs_0_, f32[32,8,256]{2,1,0:T(8,128)S(1)} %get-tuple-element.80.refs_1_, f32[33,8,256]{2,1,0:T(8,128)S(1)} %collective-permute-done.3.refs_2_, f32[8,128]{1,0:T(8,128)} %get-tuple-element.86.refs_3_, ...), custom_call_target="tpu_custom_call" | custom-call | tf_op jit(solution)/shard_map/pallas_call | solution.py:716
  99.8 2.8 %all-to-all-done.3.refs_0_ = f32[16,8,256]{2,1,0:T(8,128)S(1)} async-done(((f32[16,8,256]{2,1,0:T(8,128)}), f32[16,8,256]{2,1,0:T(8,128)S(1)}, u32[]{:S(2)}, u32[]{:S(2)}) %all-to-all-start.3) | async-done | bytes 131104 | tf_op jit(solution)/shard_map/all_to_all | solution.py:731
  102.7 13.4 %all_to_all.31.refs_0_ = f32[16,8,256]{2,1,0:T(8,128)S(1)} all-to-all(f32[16,8,256]{2,1,0:T(8,128)S(1)} %shard_map.153), channel_id=1, replica_groups={{0,4,32,36,64,68,96,100,128,132,160,164,192,196,224,228},{8,12,40,44,72..., dimensions={0} | all-to-all | bytes 262144 | tf_op jit(solution)/shard_map/all_to_all | solution.py:731
  116.2 10.2 %all_to_all.32.refs_0_ = f32[16,8,256]{2,1,0:T(8,128)S(1)} all-to-all(f32[16,8,256]{2,1,0:T(8,128)S(1)} %shard_map.154), channel_id=1, replica_groups={{0,1,2,3,8,9,10,11,16,17,18,19,24,25,26,27},{4,5,6,7,12,13,14,15,20,21,..., dimensions={0} | all-to-all | bytes 262144 | tf_op jit(solution)/shard_map/all_to_all | solution.py:731
  126.4 0.7 shard_map.155
  (18 shorter events, 0.1 us)
Async XLA Ops:
  4.4 4.8 %collective-permute-start = (f32[33,8,256]{2,1,0:T(8,128)S(1)}, f32[33,8,256]{2,1,0:T(8,128)S(1)}, u32[]{:S(2)}, u32[]{:S(2)}) collective-permute-start(f32[33,8,256]{2,1,0:T(8,128)S(1)} %get-tuple-element.52), channel_id=1, source_target_pairs={{0,4},{4,0},{8,12},{12,8},{16,20},{20,16},{24,28},{28,24},{32,36},... | collective-permute-start | bytes 811016 | tf_op jit(solution)/shard_map/ppermute | solution.py:750
  10.1 23.8 %all-to-all-start = ((f32[32,8,384]{2,1,0:T(8,128)}), f32[32,8,384]{2,1,0:T(8,128)S(1)}, u32[]{:S(2)}, u32[]{:S(2)}) async-start(f32[32,8,384]{2,1,0:T(8,128)} %shard_map.139), calls=%async_computation | async-start | bytes 786432 | tf_op jit(solution)/shard_map/all_to_all | solution.py:731
  35.7 24.9 %copy-start.5 = (f32[32,8,256]{2,1,0:T(8,128)S(1)}, f32[32,8,256]{2,1,0:T(8,128)}, u32[]{:S(2)}) copy-start(f32[32,8,256]{2,1,0:T(8,128)} %get-tuple-element.62.refs_2_) | copy-start | bytes 786436
  35.8 3.5 %collective-permute-start.1 = (f32[32,8,256]{2,1,0:T(8,128)S(1)}, f32[32,8,256]{2,1,0:T(8,128)S(1)}, u32[]{:S(2)}, u32[]{:S(2)}) collective-permute-start(f32[32,8,256]{2,1,0:T(8,128)S(1)} %get-tuple-element.60), channel_id=1, source_target_pairs={{0,4},{4,0},{8,12},{12,8},{16,20},{20,16},{24,28},{28,24},{32,36},... | collective-permute-start | bytes 786440 | tf_op jit(solution)/shard_map/ppermute | solution.py:750
  37.7 25.1 %copy-start = (bf16[1,256,1024]{2,1,0:T(8,128)(2,1)S(1)}, bf16[1,256,1024]{2,1,0:T(8,128)(2,1)}, u32[]{:S(2)}) copy-start(bf16[1,256,1024]{2,1,0:T(8,128)(2,1)} %param.14) | copy-start | bytes 1572868
  37.7 25.1 %copy-start.4 = (bf16[1,256,512]{2,1,0:T(8,128)(2,1)S(1)}, bf16[1,256,512]{2,1,0:T(8,128)(2,1)}, u32[]{:S(2)}) copy-start(bf16[1,256,512]{2,1,0:T(8,128)(2,1)} %param.11) | copy-start | bytes 786436
  39.3 24.6 %copy-start.6 = (f32[24,256]{1,0:T(8,128)S(1)}, f32[24,256]{1,0:T(8,128)}, u32[]{:S(2)}) copy-start(f32[24,256]{1,0:T(8,128)} %get-tuple-element.68.refs_5_.refs_4_) | copy-start | bytes 73732
  60.8 3.1 %collective-permute-start.2 = (f32[32,8,256]{2,1,0:T(8,128)S(1)}, f32[32,8,256]{2,1,0:T(8,128)S(1)}, u32[]{:S(2)}, u32[]{:S(2)}) collective-permute-start(f32[32,8,256]{2,1,0:T(8,128)S(1)} %get-tuple-element.64), channel_id=1, source_target_pairs={{0,4},{4,0},{8,12},{12,8},{16,20},{20,16},{24,28},{28,24},{32,36},... | collective-permute-start | bytes 786440 | tf_op jit(solution)/shard_map/ppermute | solution.py:750
  65.3 17.2 %all-to-all-start.2 = ((f32[32,5,4,128]{3,2,1,0:T(4,128)}), f32[32,5,4,128]{3,2,1,0:T(4,128)S(1)}, u32[]{:S(2)}, u32[]{:S(2)}) async-start(f32[32,5,4,128]{3,2,1,0:T(4,128)} %get-tuple-element.75), calls=%async_computation.2 | async-start | bytes 655360 | tf_op jit(solution)/shard_map/all_to_all | solution.py:731
  69.7 16.5 %copy-start.1 = (bf16[1,256,1024]{2,1,0:T(8,128)(2,1)S(1)}, bf16[1,256,1024]{2,1,0:T(8,128)(2,1)}, u32[]{:S(2)}) copy-start(bf16[1,256,1024]{2,1,0:T(8,128)(2,1)} %param.13) | copy-start | bytes 1572868
  69.7 16.5 %copy-start.2 = (bf16[1,256,512]{2,1,0:T(8,128)(2,1)S(1)}, bf16[1,256,512]{2,1,0:T(8,128)(2,1)}, u32[]{:S(2)}) copy-start(bf16[1,256,512]{2,1,0:T(8,128)(2,1)} %param.12) | copy-start | bytes 786436
  76.1 11.4 %copy-start.3 = (bf16[1,256,4096]{2,1,0:T(8,128)(2,1)S(1)}, bf16[1,256,4096]{2,1,0:T(8,128)(2,1)}, u32[]{:S(2)}) copy-start(bf16[1,256,4096]{2,1,0:T(8,128)(2,1)} %param.10) | copy-start | bytes 6291460
  83.6 3.8 %collective-permute-start.3 = (f32[33,8,256]{2,1,0:T(8,128)S(1)}, f32[33,8,256]{2,1,0:T(8,128)S(1)}, u32[]{:S(2)}, u32[]{:S(2)}) collective-permute-start(f32[33,8,256]{2,1,0:T(8,128)S(1)} %get-tuple-element.81), channel_id=1, source_target_pairs={{0,4},{4,0},{8,12},{12,8},{16,20},{20,16},{24,28},{28,24},{32,36},... | collective-permute-start | bytes 811016 | tf_op jit(solution)/shard_map/ppermute | solution.py:750
  90.5 12.2 %all-to-all-start.3 = ((f32[16,8,256]{2,1,0:T(8,128)}), f32[16,8,256]{2,1,0:T(8,128)S(1)}, u32[]{:S(2)}, u32[]{:S(2)}) async-start(f32[16,8,256]{2,1,0:T(8,128)} %get-tuple-element.90), calls=%async_computation.3 | async-start | bytes 262144 | tf_op jit(solution)/shard_map/all_to_all | solution.py:731

commit v7 on v6

--- a/solution.py
+++ b/solution.py
@@ -677,7 +677,7 @@
         self.ref[at] = value
 
 
-def call(body, outs, ins, limit=24):
+def call(body, outs, ins, limit=14):
     outs = [(k, o if isinstance(o, jax.ShapeDtypeStruct) else jax.ShapeDtypeStruct(o, F32)) for k, o in outs]
     spaces = {"s": pltpu.SMEM, "v": pltpu.VMEM, "h": pltpu.HBM, "m": pltpu.HBM, "a": pltpu.HBM}
     scratch = [

time: 128 us -> 128 us (level)
  no operation moved by 1% of the time
where the time goes in v7:
time: 128 us; the launch traced here: 127 us
  blocking collectives  44.2 us (35%)
  Pallas kernels  32 us (25%)
  starting transfers between devices  29.1 us (23%)
  waiting for transfers between devices  20.8 us (16%)
    all_to_all x3, blocking collectives, exchange(): return lax.all_to_all(x, axis, 0, 0, axis_index_groups=groups)  44.2 us
    pallas_call x19, Pallas kernels, call(): pl.pallas_call(kernel, out_shape=[pltpu.HBM(o.shape, o.dtype) if k == 'h'...  32 us
    all_to_all x3, waiting for transfers between devices, exchange(): return lax.all_to_all(x, axis, 0, 0, axis_index_groups=groups)  19.3 us
    all_to_all x3, starting transfers between devices, exchange(): return lax.all_to_all(x, axis, 0, 0, axis_index_groups=groups)  19.2 us
    ppermute x4, starting transfers between devices, to_pair(): return lax.ppermute(a, 'ctx', [(i, i ^ 1) for i in range(devices)])  9.88 us
  transfers between devices with their start and end apart: 7, of which 5 were waited for; matrix products, arithmetic and copies ran while one was open for 0% of the time, Pallas kernels for 14%

profile of v7, /device:TPU:1, one launch (start us, length us, event | category | flops | bytes accessed | tf_op | source)
XLA Modules:
  0.0 127.2 jit_solution(12674414429974556493)
XLA Ops:
  0.6 3.8 %shard_map.137 = (f32[33,8,256]{2,1,0:T(8,128)S(1)}, bf16[512,256]{1,0:T(8,128)(2,1)S(1)}, f32[256,128]{1,0:T(8,128)S(1)}, f32[8,128]{1,0:T(8,128)S(1)}, f32[24,256]{1,0:T(8,128)}) custom-call(s32[1]{0:T(128)} %bitcast.refs_0_, bf16[4,4096]{1,0:T(4,128)(2,1)} %bitcast.38, bf16[4,4096]{1,0:T(4,128)(2,1)} %bitcast.39, f32[4]{0:T(128)} %refs_3_.1, f32[4]{0:T(128)} %refs_4_.1, ...), custom_call_target="tpu_custom_call" | custom-call | tf_op jit(solution)/shard_map/pallas_call | solution.py:716
  4.4 3.3 %collective-permute-start = (f32[33,8,256]{2,1,0:T(8,128)S(1)}, f32[33,8,256]{2,1,0:T(8,128)S(1)}, u32[]{:S(2)}, u32[]{:S(2)}) collective-permute-start(f32[33,8,256]{2,1,0:T(8,128)S(1)} %get-tuple-element.52), channel_id=1, source_target_pairs={{0,4},{4,0},{8,12},{12,8},{16,20},{20,16},{24,28},{28,24},{32,36},... | collective-permute-start | bytes 811016 | tf_op jit(solution)/shard_map/ppermute | solution.py:750
  7.7 1.4 %shard_map.138.refs_1_ = f32[32,8,256]{2,1,0:T(8,128)S(1)} custom-call(s32[1]{0:T(128)} %bitcast.refs_0_, bf16[512,256]{1,0:T(8,128)(2,1)S(1)} %get-tuple-element.49.refs_1_, bf16[256,1024]{1,0:T(8,128)(2,1)} %bitcast.20, f32[256,128]{1,0:T(8,128)S(1)} %get-tuple-element.50.refs_3_), custom_call_target="tpu_custom_call" | custom-call | tf_op jit(solution)/shard_map/pallas_call | solution.py:716
  9.2 0.9 shard_map.139
  10.1 9.3 %all-to-all-start = ((f32[32,8,384]{2,1,0:T(8,128)}), f32[32,8,384]{2,1,0:T(8,128)S(1)}, u32[]{:S(2)}, u32[]{:S(2)}) async-start(f32[32,8,384]{2,1,0:T(8,128)} %shard_map.139), calls=%async_computation | async-start | bytes 786432 | tf_op jit(solution)/shard_map/all_to_all | solution.py:731
  19.5 4.3 %shard_map.140 = (f32[32,8,256]{2,1,0:T(8,128)}, f32[8,128]{1,0:T(8,128)S(1)}, bf16[512,256]{1,0:T(8,128)(2,1)S(1)}, f32[4,256,256]{2,1,0:T(8,128)}, f32[4,256,2...) custom-call(s32[1]{0:T(128)} %bitcast.refs_0_, f32[32,8,256]{2,1,0:T(8,128)S(1)} %shard_map.138.refs_1_, ...), custom_call_target="tpu_custom_call" | custom-call | tf_op jit(solution)/shard_map/pallas_call | solution.py:716
  23.8 10.1 %all-to-all-done.refs_1_.refs_0_ = f32[32,8,384]{2,1,0:T(8,128)S(1)} async-done(((f32[32,8,384]{2,1,0:T(8,128)}), f32[32,8,384]{2,1,0:T(8,128)S(1)}, u32[]{:S(2)}, u32[]{:S(2)}) %all-to-all-start) | async-done | bytes 393248 | tf_op jit(solution)/shard_map/all_to_all | solution.py:731
  33.9 1.8 %shard_map.141 = (f32[32,8,256]{2,1,0:T(8,128)S(1)}, f32[256,128]{1,0:T(8,128)S(1)}, f32[2,32,128]{2,1,0:T(8,128)S(1)}, f32[16,128]{1,0:T(8,128)S(1)}, f32[2,32,...) custom-call(s32[1]{0:T(128)} %bitcast.refs_0_, ...), custom_call_target="tpu_custom_call" | custom-call | tf_op jit(solution)/shard_map/pallas_call | solution.py:716
  35.8 1.9 %collective-permute-start.1 = (f32[32,8,256]{2,1,0:T(8,128)S(1)}, f32[32,8,256]{2,1,0:T(8,128)S(1)}, u32[]{:S(2)}, u32[]{:S(2)}) collective-permute-start(f32[32,8,256]{2,1,0:T(8,128)S(1)} %get-tuple-element.60), channel_id=1, source_target_pairs={{0,4},{4,0},{8,12},{12,8},{16,20},{20,16},{24,28},{28,24},{32,36},... | collective-permute-start | bytes 786440 | tf_op jit(solution)/shard_map/ppermute | solution.py:750
  37.7 1.5 %shard_map.143.refs_3_ = f32[32,8,256]{2,1,0:T(8,128)S(1)} custom-call(s32[1]{0:T(128)} %bitcast.refs_0_, bf16[512,256]{1,0:T(8,128)(2,1)S(1)} %get-tuple-element.56.refs_5_.refs_1_, bf16[256,1024]{1,0:T(8,128)(2,1)} %bitcast.15, f32[256,128]{1,0:T(8,128)S(1)} %get-tuple-element.59.refs_3_), custom_call_target="tpu_custom_call" | custom-call | tf_op jit(solution)/shard_map/pallas_call | solution.py:716
  39.2 0.1 shard_map.142.refs_1_
  39.3 0.8 shard_map.144
  40.1 20.6 %all_to_all.30.refs_1_.refs_2_ = f32[32,8,512]{2,1,0:T(8,128)S(1)} all-to-all(f32[32,8,512]{2,1,0:T(8,128)S(1)} %get-tuple-element.61), channel_id=1, replica_groups={{0,8,16,24,32,40,48,56,64,72,80,88,96,104,112,120,128,136,144,152,160,1..., dimensions={0} | all-to-all | bytes 1048576 | tf_op jit(solution)/shard_map/all_to_all | solution.py:731
  60.7 0.1 shard_map.145
  60.8 2.0 %collective-permute-start.2 = (f32[32,8,256]{2,1,0:T(8,128)S(1)}, f32[32,8,256]{2,1,0:T(8,128)S(1)}, u32[]{:S(2)}, u32[]{:S(2)}) collective-permute-start(f32[32,8,256]{2,1,0:T(8,128)S(1)} %get-tuple-element.64), channel_id=1, source_target_pairs={{0,4},{4,0},{8,12},{12,8},{16,20},{20,16},{24,28},{28,24},{32,36},... | collective-permute-start | bytes 786440 | tf_op jit(solution)/shard_map/ppermute | solution.py:750
  62.8 0.5 shard_map.146
  63.2 0.7 collective-permute-done.2.refs_2_
  63.9 1.4 %shard_map.147 = (f32[32,5,4,128]{3,2,1,0:T(4,128)}, f32[8,128]{1,0:T(8,128)S(1)}, f32[8,256]{1,0:T(8,128)S(1)}) custom-call(s32[1]{0:T(128)} %bitcast.refs_0_, f32[32,8,256]{2,1,0:T(8,128)S(1)} %get-tuple-element.63.refs_1_, f32[32,8,256]{2,1,0:T(8,128)S(1)} %collective-permute-done.2.refs_2_, f32[32,4,4,128]{3,2,1,0:T(4,128)S(1)} %get-tuple-element.66.refs_3_, ...), custom_call_target="tpu_custom_call" | custom-call | tf_op jit(solution)/shard_map/pallas_call | solution.py:716
  65.3 4.4 %all-to-all-start.2 = ((f32[32,5,4,128]{3,2,1,0:T(4,128)}), f32[32,5,4,128]{3,2,1,0:T(4,128)S(1)}, u32[]{:S(2)}, u32[]{:S(2)}) async-start(f32[32,5,4,128]{3,2,1,0:T(4,128)} %get-tuple-element.75), calls=%async_computation.2 | async-start | bytes 655360 | tf_op jit(solution)/shard_map/all_to_all | solution.py:731
  69.8 6.3 %shard_map.148 = (f32[64,8,256]{2,1,0:T(8,128)}, bf16[256,512]{1,0:T(8,128)(2,1)}, f32[256,1024]{1,0:T(8,128)}, f32[256,512]{1,0:T(8,128)}, f32[8,256]{1,0:T(8,128)}, /*index=5*/f32[8,256]{1,0:T(8,128)}) custom-call(s32[1]{0:T(128)} %bitcast.refs_0_, f32[32,8,256]{2,1,0:T(8,128)S(1)} %get-tuple-element.63.refs_1_, ...), custom_call_target="tpu_custom_call" | custom-call | tf_op jit(solution)/shard_map/pallas_call | solution.py:716
  76.1 6.4 %all-to-all-done.2.refs_1_ = f32[32,5,4,128]{3,2,1,0:T(4,128)S(1)} async-done(((f32[32,5,4,128]{3,2,1,0:T(4,128)}), f32[32,5,4,128]{3,2,1,0:T(4,128)S(1)}, u32[]{:S(2)}, u32[]{:S(2)}) %all-to-all-start.2) | async-done | bytes 327712 | tf_op jit(solution)/shard_map/all_to_all | solution.py:731
  82.5 1.1 shard_map.149
  83.6 2.7 %collective-permute-start.3 = (f32[33,8,256]{2,1,0:T(8,128)S(1)}, f32[33,8,256]{2,1,0:T(8,128)S(1)}, u32[]{:S(2)}, u32[]{:S(2)}) collective-permute-start(f32[33,8,256]{2,1,0:T(8,128)S(1)} %get-tuple-element.81), channel_id=1, source_target_pairs={{0,4},{4,0},{8,12},{12,8},{16,20},{20,16},{24,28},{28,24},{32,36},... | collective-permute-start | bytes 811016 | tf_op jit(solution)/shard_map/ppermute | solution.py:750
  86.3 0.4 shard_map.150.refs_4_
  86.7 0.8 collective-permute-done.3.refs_2_
  87.4 3.1 %shard_map.151 = (f32[8,128]{1,0:T(8,128)}, f32[16,8,256]{2,1,0:T(8,128)}) custom-call(s32[1]{0:T(128)} %bitcast.refs_0_, f32[32,8,256]{2,1,0:T(8,128)S(1)} %get-tuple-element.80.refs_1_, f32[33,8,256]{2,1,0:T(8,128)S(1)} %collective-permute-done.3.refs_2_, f32[8,128]{1,0:T(8,128)S(1)} %get-tuple-element.82.refs_3_, f32[256,128]{1,0:T(8,128)S(1)} %shard_map.150.refs_4_, ...), custom_call_target="tpu_custom_call" | custom-call | tf_op jit(solution)/shard_map/pallas_call | solution.py:716
  90.5 5.5 %all-to-all-start.3 = ((f32[16,8,256]{2,1,0:T(8,128)}), f32[16,8,256]{2,1,0:T(8,128)S(1)}, u32[]{:S(2)}, u32[]{:S(2)}) async-start(f32[16,8,256]{2,1,0:T(8,128)} %get-tuple-element.90), calls=%async_computation.3 | async-start | bytes 262144 | tf_op jit(solution)/shard_map/all_to_all | solution.py:731
  96.0 3.9 %shard_map.152 = (bf16[256,512]{1,0:T(8,128)(2,1)}, bf16[256,1024]{1,0:T(8,128)(2,1)}) custom-call(s32[1]{0:T(128)} %bitcast.refs_0_, f32[32,8,256]{2,1,0:T(8,128)S(1)} %get-tuple-element.80.refs_1_, f32[33,8,256]{2,1,0:T(8,128)S(1)} %collective-permute-done.3.refs_2_, f32[8,128]{1,0:T(8,128)} %get-tuple-element.86.refs_3_, ...), custom_call_target="tpu_custom_call" | custom-call | tf_op jit(solution)/shard_map/pallas_call | solution.py:716
  99.8 2.8 %all-to-all-done.3.refs_0_ = f32[16,8,256]{2,1,0:T(8,128)S(1)} async-done(((f32[16,8,256]{2,1,0:T(8,128)}), f32[16,8,256]{2,1,0:T(8,128)S(1)}, u32[]{:S(2)}, u32[]{:S(2)}) %all-to-all-start.3) | async-done | bytes 131104 | tf_op jit(solution)/shard_map/all_to_all | solution.py:731
  102.7 13.4 %all_to_all.31.refs_0_ = f32[16,8,256]{2,1,0:T(8,128)S(1)} all-to-all(f32[16,8,256]{2,1,0:T(8,128)S(1)} %shard_map.153), channel_id=1, replica_groups={{0,4,32,36,64,68,96,100,128,132,160,164,192,196,224,228},{8,12,40,44,72..., dimensions={0} | all-to-all | bytes 262144 | tf_op jit(solution)/shard_map/all_to_all | solution.py:731
  116.2 10.2 %all_to_all.32.refs_0_ = f32[16,8,256]{2,1,0:T(8,128)S(1)} all-to-all(f32[16,8,256]{2,1,0:T(8,128)S(1)} %shard_map.154), channel_id=1, replica_groups={{0,1,2,3,8,9,10,11,16,17,18,19,24,25,26,27},{4,5,6,7,12,13,14,15,20,21,..., dimensions={0} | all-to-all | bytes 262144 | tf_op jit(solution)/shard_map/all_to_all | solution.py:731
  126.4 0.7 shard_map.155
  (18 shorter events, 0.1 us)
Async XLA Ops:
  4.4 4.8 %collective-permute-start = (f32[33,8,256]{2,1,0:T(8,128)S(1)}, f32[33,8,256]{2,1,0:T(8,128)S(1)}, u32[]{:S(2)}, u32[]{:S(2)}) collective-permute-start(f32[33,8,256]{2,1,0:T(8,128)S(1)} %get-tuple-element.52), channel_id=1, source_target_pairs={{0,4},{4,0},{8,12},{12,8},{16,20},{20,16},{24,28},{28,24},{32,36},... | collective-permute-start | bytes 811016 | tf_op jit(solution)/shard_map/ppermute | solution.py:750
  10.1 23.8 %all-to-all-start = ((f32[32,8,384]{2,1,0:T(8,128)}), f32[32,8,384]{2,1,0:T(8,128)S(1)}, u32[]{:S(2)}, u32[]{:S(2)}) async-start(f32[32,8,384]{2,1,0:T(8,128)} %shard_map.139), calls=%async_computation | async-start | bytes 786432 | tf_op jit(solution)/shard_map/all_to_all | solution.py:731
  35.7 24.9 %copy-start.5 = (f32[32,8,256]{2,1,0:T(8,128)S(1)}, f32[32,8,256]{2,1,0:T(8,128)}, u32[]{:S(2)}) copy-start(f32[32,8,256]{2,1,0:T(8,128)} %get-tuple-element.62.refs_2_) | copy-start | bytes 786436
  35.8 3.5 %collective-permute-start.1 = (f32[32,8,256]{2,1,0:T(8,128)S(1)}, f32[32,8,256]{2,1,0:T(8,128)S(1)}, u32[]{:S(2)}, u32[]{:S(2)}) collective-permute-start(f32[32,8,256]{2,1,0:T(8,128)S(1)} %get-tuple-element.60), channel_id=1, source_target_pairs={{0,4},{4,0},{8,12},{12,8},{16,20},{20,16},{24,28},{28,24},{32,36},... | collective-permute-start | bytes 786440 | tf_op jit(solution)/shard_map/ppermute | solution.py:750
  37.7 25.1 %copy-start = (bf16[1,256,1024]{2,1,0:T(8,128)(2,1)S(1)}, bf16[1,256,1024]{2,1,0:T(8,128)(2,1)}, u32[]{:S(2)}) copy-start(bf16[1,256,1024]{2,1,0:T(8,128)(2,1)} %param.14) | copy-start | bytes 1572868
  37.7 25.1 %copy-start.4 = (bf16[1,256,512]{2,1,0:T(8,128)(2,1)S(1)}, bf16[1,256,512]{2,1,0:T(8,128)(2,1)}, u32[]{:S(2)}) copy-start(bf16[1,256,512]{2,1,0:T(8,128)(2,1)} %param.11) | copy-start | bytes 786436
  39.3 24.6 %copy-start.6 = (f32[24,256]{1,0:T(8,128)S(1)}, f32[24,256]{1,0:T(8,128)}, u32[]{:S(2)}) copy-start(f32[24,256]{1,0:T(8,128)} %get-tuple-element.68.refs_5_.refs_4_) | copy-start | bytes 73732
  60.8 3.1 %collective-permute-start.2 = (f32[32,8,256]{2,1,0:T(8,128)S(1)}, f32[32,8,256]{2,1,0:T(8,128)S(1)}, u32[]{:S(2)}, u32[]{:S(2)}) collective-permute-start(f32[32,8,256]{2,1,0:T(8,128)S(1)} %get-tuple-element.64), channel_id=1, source_target_pairs={{0,4},{4,0},{8,12},{12,8},{16,20},{20,16},{24,28},{28,24},{32,36},... | collective-permute-start | bytes 786440 | tf_op jit(solution)/shard_map/ppermute | solution.py:750
  65.3 17.2 %all-to-all-start.2 = ((f32[32,5,4,128]{3,2,1,0:T(4,128)}), f32[32,5,4,128]{3,2,1,0:T(4,128)S(1)}, u32[]{:S(2)}, u32[]{:S(2)}) async-start(f32[32,5,4,128]{3,2,1,0:T(4,128)} %get-tuple-element.75), calls=%async_computation.2 | async-start | bytes 655360 | tf_op jit(solution)/shard_map/all_to_all | solution.py:731
  69.7 16.5 %copy-start.1 = (bf16[1,256,1024]{2,1,0:T(8,128)(2,1)S(1)}, bf16[1,256,1024]{2,1,0:T(8,128)(2,1)}, u32[]{:S(2)}) copy-start(bf16[1,256,1024]{2,1,0:T(8,128)(2,1)} %param.13) | copy-start | bytes 1572868
  69.7 16.5 %copy-start.2 = (bf16[1,256,512]{2,1,0:T(8,128)(2,1)S(1)}, bf16[1,256,512]{2,1,0:T(8,128)(2,1)}, u32[]{:S(2)}) copy-start(bf16[1,256,512]{2,1,0:T(8,128)(2,1)} %param.12) | copy-start | bytes 786436
  76.1 11.4 %copy-start.3 = (bf16[1,256,4096]{2,1,0:T(8,128)(2,1)S(1)}, bf16[1,256,4096]{2,1,0:T(8,128)(2,1)}, u32[]{:S(2)}) copy-start(bf16[1,256,4096]{2,1,0:T(8,128)(2,1)} %param.10) | copy-start | bytes 6291460
  83.6 3.8 %collective-permute-start.3 = (f32[33,8,256]{2,1,0:T(8,128)S(1)}, f32[33,8,256]{2,1,0:T(8,128)S(1)}, u32[]{:S(2)}, u32[]{:S(2)}) collective-permute-start(f32[33,8,256]{2,1,0:T(8,128)S(1)} %get-tuple-element.81), channel_id=1, source_target_pairs={{0,4},{4,0},{8,12},{12,8},{16,20},{20,16},{24,28},{28,24},{32,36},... | collective-permute-start | bytes 811016 | tf_op jit(solution)/shard_map/ppermute | solution.py:750
  90.5 12.2 %all-to-all-start.3 = ((f32[16,8,256]{2,1,0:T(8,128)}), f32[16,8,256]{2,1,0:T(8,128)S(1)}, u32[]{:S(2)}, u32[]{:S(2)}) async-start(f32[16,8,256]{2,1,0:T(8,128)} %get-tuple-element.90), calls=%async_computation.3 | async-start | bytes 262144 | tf_op jit(solution)/shard_map/all_to_all | solution.py:731
